TPU v7x, 32 devices: a whole 2x2x4 slice. The times are simulated.
32 devices in a mesh: grp: 4 (over y, x), blk: 8 (over z, core).
Axes of the slice: x: 2, y: 2, z: 4, core: 2. Of those that a mesh axis runs over, the one named last changes fastest.
Arguments:
- residual_in: bfloat16 [256, 16384], P('grp', 'blk'), may hold values from -6 to 6
- queries: bfloat16 [256, 16384], P('grp')
- key_cache: bfloat16 [256, 8, 64, 128], P('grp', 'blk')
- value_cache: bfloat16 [256, 8, 64, 128], P('grp', 'blk'), may hold values from -6 to 6
- key_new: bfloat16 [256, 1024], P('grp'), may hold values from -6 to 6
- value_new: bfloat16 [256, 1024], P('grp'), may hold values from -6 to 6
- lengths: int32 [256], P('grp'), may hold values from 2 to 64, as said below
- ffn_gain: bfloat16 [16384], P('blk'), may hold values from 0.099609375 to 1.8984375
- gate_weight: bfloat16 [16384, 26624], P('blk', 'grp'), may hold values from -0.046875 to 0.046875
- up_weight: bfloat16 [16384, 26624], P('blk', 'grp'), may hold values from -0.046875 to 0.046875
- down_weight: bfloat16 [26624, 16384], P('grp', 'blk'), may hold values from -0.0390625 to 0.0390625
Outputs:
- layer_out: float32 [256, 16384], P('grp', 'blk')
Inputs may be any that keep to these rules, and one draw needn't show every extreme that they name: `lengths`: every sequence has at least two valid cache positions, and some sequence fills all 64.
All inputs are finite; a program needn't handle non-finite values.
Results may differ from a plain program's by a relative error of at most 0.0075.
Values may be sent and summed in bfloat16 or wider, within the bound.
No kernel may reach another device: no remote copies, remote signals or barrier semaphores. Data moves between devices by JAX's collectives and lax.ppermute only.
A program may use at most 192 MiB of HBM per device.

v0:
```python
import functools
import math

import jax
import jax.numpy as jnp
from jax import lax
from jax.experimental import pallas as pl
from jax.experimental.pallas import tpu as pltpu
from jax.sharding import PartitionSpec as P

D = 16384
HEADS = 128
KV_HEADS = 8
CHUNK_UNITS = (8, 10, 8)
SLOTS = 3
VMEM = 38 * 1024 * 1024
SMALL_VMEM = 8 * 1024 * 1024


def partner(x, axis, distance):
    return lax.ppermute(x, axis, [(i, i ^ distance) for i in range(lax.axis_size(axis))])


def along_ring(x):
    chips = lax.axis_size("blk") // 2
    ring = [0, *range(1, chips, 2), *range(chips - 2, 0, -2)]
    hops = zip(ring, ring[1:] + ring[:1])
    return lax.ppermute(x, "blk", [(2 * a + c, 2 * b + c) for a, b in hops for c in range(2)])


def stream(units, copies, prepare, compute):
    def start(i, slot):
        for copy in copies(i, slot):
            copy.start()

    for i in range(min(SLOTS - 1, units)):
        start(i, i)
    prepare()

    def step(i, _):
        later = i + SLOTS - 1

        @pl.when(later < units)
        def _():
            start(later, lax.rem(later, SLOTS))

        slot = lax.rem(i, SLOTS)
        for copy in copies(i, slot):
            copy.wait()
        compute(i, slot)
        return 0

    lax.fori_loop(0, units, step, 0)


def gate_up_kernel(n_blocks, has_ride, first_unit, units, place_ref, *refs):
    blocks, gate_ref, up_ref = refs[:n_blocks], refs[n_blocks], refs[n_blocks + 1]
    keep_ref, send_ref, *rest = refs[-5 - has_ride :]
    x_ref, held, sems = rest[-3:]
    half = keep_ref.shape[1]
    unit = held.shape[3]
    parts = place_ref.shape[0] // n_blocks
    rows = blocks[0].shape[0] // parts

    def copies(i, slot):
        columns = pl.ds(pl.multiple_of((first_unit + i) * unit, unit), unit)
        return [
            pltpu.make_async_copy(weight.at[:, columns], held.at[slot, j], sems.at[slot, j])
            for j, weight in enumerate((gate_ref, up_ref))
        ]

    def prepare():
        if has_ride:
            rest[0][...] = refs[n_blocks + 2][...]
        for i in range(n_blocks * parts):
            to = pl.ds(pl.multiple_of(place_ref[i] * rows, rows), rows)
            x_ref[to, :] = blocks[i // parts][i % parts * rows : (i % parts + 1) * rows, :]

    def compute(i, slot):
        columns = pl.ds(pl.multiple_of(i * unit, unit), unit)
        for j in range(2):
            y = jnp.dot(x_ref[...], held[slot, j], preferred_element_type=jnp.float32)
            keep_ref[j, :, columns] = y[:half].astype(jnp.bfloat16)
            send_ref[j, :, columns] = y[half:].astype(jnp.bfloat16)

    stream(units, copies, prepare, compute)


def gate_up(place, blocks, gate_weight, up_weight, unit, start, units, after, ride=None):
    rows, depth = blocks[0].shape
    total = rows * len(blocks)
    cols = units * unit
    rides = [] if ride is None else [ride]
    vmem = pl.BlockSpec(memory_space=pltpu.VMEM)
    anywhere = pl.BlockSpec(memory_space=pl.ANY)
    return pl.pallas_call(
        functools.partial(gate_up_kernel, len(blocks), len(rides), start, units),
        in_specs=[pl.BlockSpec(memory_space=pltpu.SMEM)]
        + [vmem] * len(blocks)
        + [pl.BlockSpec(memory_space=pltpu.HBM)] * 2
        + [vmem] * len(rides)
        + [anywhere] * len(after),
        out_specs=[vmem] * (2 + len(rides)),
        out_shape=[jax.ShapeDtypeStruct((2, total // 2, cols), jnp.bfloat16)] * 2
        + [jax.ShapeDtypeStruct(r.shape, r.dtype) for r in rides],
        scratch_shapes=[
            pltpu.VMEM((total, depth), jnp.bfloat16),
            pltpu.VMEM((SLOTS, 2, depth, unit), jnp.bfloat16),
            pltpu.SemaphoreType.DMA((SLOTS, 2)),
        ],
        compiler_params=pltpu.CompilerParams(vmem_limit_bytes=VMEM),
        cost_estimate=pl.CostEstimate(
            flops=4 * total * depth * cols,
            bytes_accessed=4 * depth * cols + 2 * total * depth + 4 * total * cols,
            transcendentals=0,
        ),
    )(place, *blocks, gate_weight, up_weight, *rides, *after)


def nothing(*refs):
    pass


def hold(x, after):
    anywhere = pl.BlockSpec(memory_space=pl.ANY)
    return pl.pallas_call(
        nothing,
        in_specs=[anywhere] * (1 + len(after)),
        out_specs=anywhere,
        out_shape=jax.ShapeDtypeStruct(x.shape, x.dtype),
        input_output_aliases={0: 0},
        cost_estimate=pl.CostEstimate(flops=0, bytes_accessed=0, transcendentals=0),
    )(x, *after)


def pass_on_kernel(shard, has_flow, own_ref, other_ref, *refs):
    out_ref = refs[-1]
    rows = out_ref.shape[1]
    here = slice(shard * rows, (shard + 1) * rows)
    total = own_ref[:, here].astype(jnp.float32) + other_ref[:, here].astype(jnp.float32)
    if has_flow:
        total = total + refs[0][...].astype(jnp.float32)
    out_ref[...] = total.astype(jnp.bfloat16)


def pass_on(shard, shards, own, other, flow, after):
    vmem = pl.BlockSpec(memory_space=pltpu.VMEM)
    flows = [] if flow is None else [flow]
    return pl.pallas_call(
        functools.partial(pass_on_kernel, shard, len(flows)),
        in_specs=[vmem] * (2 + len(flows)) + [pl.BlockSpec(memory_space=pl.ANY)] * len(after),
        out_specs=vmem,
        out_shape=jax.ShapeDtypeStruct(
            (2, own.shape[1] // shards, own.shape[2]), jnp.bfloat16
        ),
        compiler_params=pltpu.CompilerParams(vmem_limit_bytes=SMALL_VMEM),
        cost_estimate=pl.CostEstimate(
            flops=2 * own.size // shards, bytes_accessed=8 * own.size // shards, transcendentals=0
        ),
    )(own, other, *flows, *after)


def hidden_kernel(flow_ref, own_ref, other_ref, inverse_ref, *refs):
    rows = flow_ref.shape[1]
    inverse = inverse_ref[...]
    gate, up = [
        (
            own_ref[i, -rows:].astype(jnp.float32)
            + other_ref[i, -rows:].astype(jnp.float32)
            + flow_ref[i].astype(jnp.float32)
        )
        * inverse
        for i in range(2)
    ]
    refs[-1][...] = (gate / (1 + jnp.exp(-gate)) * up).astype(jnp.bfloat16)


def hidden_units(flow, own, other, inverse, after):
    _, rows, cols = flow.shape
    vmem = pl.BlockSpec(memory_space=pltpu.VMEM)
    return pl.pallas_call(
        hidden_kernel,
        in_specs=[vmem] * 4 + [pl.BlockSpec(memory_space=pl.ANY)] * len(after),
        out_specs=vmem,
        out_shape=jax.ShapeDtypeStruct((rows, cols), jnp.bfloat16),
        compiler_params=pltpu.CompilerParams(vmem_limit_bytes=SMALL_VMEM),
        cost_estimate=pl.CostEstimate(
            flops=16 * rows * cols, bytes_accessed=14 * rows * cols, transcendentals=rows * cols
        ),
    )(flow, own, other, inverse, *after)


def join_kernel(n_shards, *refs):
    out_ref = refs[-1]
    rows = refs[0].shape[0]
    for i, shard in enumerate(refs[:n_shards]):
        out_ref[i * rows : (i + 1) * rows] = shard[...]


def join(shards, after):
    rows, cols = shards[0].shape
    vmem = pl.BlockSpec(memory_space=pltpu.VMEM)
    return pl.pallas_call(
        functools.partial(join_kernel, len(shards)),
        in_specs=[vmem] * len(shards) + [pl.BlockSpec(memory_space=pl.ANY)] * len(after),
        out_specs=vmem,
        out_shape=jax.ShapeDtypeStruct((rows * len(shards), cols), jnp.bfloat16),
        compiler_params=pltpu.CompilerParams(vmem_limit_bytes=SMALL_VMEM),
        cost_estimate=pl.CostEstimate(
            flops=0, bytes_accessed=4 * rows * len(shards) * cols, transcendentals=0
        ),
    )(*shards, *after)


def down_kernel(has_total, n_outs, first_unit, units, place_ref, *refs):
    ours_ref, theirs_ref, weight_ref = refs[:3]
    is_last = n_outs > 1
    x_ref, held, sems, *rest = refs[len(refs) - 3 - is_last :]
    outs = refs[len(refs) - 3 - is_last - n_outs : len(refs) - 3 - is_last]
    total_ref = rest[0] if is_last else outs[0]
    half = ours_ref.shape[0]
    unit = held.shape[1]

    def copies(i, slot):
        here = pl.ds(pl.multiple_of((first_unit + i) * unit, unit), unit)
        return [pltpu.make_async_copy(weight_ref.at[here, :], held.at[slot], sems.at[slot])]

    def prepare():
        x_ref[:half] = ours_ref[...]
        x_ref[half:] = theirs_ref[...]
        total_ref[...] = refs[3][...] if has_total else jnp.zeros_like(total_ref)

    def compute(i, slot):
        x = x_ref[:, pl.ds(pl.multiple_of(i * unit, unit), unit)]
        total_ref[...] += jnp.dot(x, held[slot], preferred_element_type=jnp.float32)

    stream(units, copies, prepare, compute)
    if is_last:
        parts = place_ref.shape[0] // n_outs
        for i in range(n_outs * parts):
            out_ref = outs[i // parts]
            rows = out_ref.shape[0] // parts
            term = total_ref[pl.ds(pl.multiple_of(place_ref[i] * rows, rows), rows), :]
            out_ref[i % parts * rows : (i % parts + 1) * rows, :] = term.astype(out_ref.dtype)


def down(place, groups, ours, theirs, weight, total, unit, start, units, after, is_last):
    half, cols = ours.shape
    width = weight.shape[1]
    has_total = total is not None
    vmem = pl.BlockSpec(memory_space=pltpu.VMEM)
    rows = 2 * half // groups
    outs = [jax.ShapeDtypeStruct((2 * half, width), jnp.float32)]
    if is_last:
        outs = [jax.ShapeDtypeStruct((rows, width), jnp.float32)]
        outs += [jax.ShapeDtypeStruct((rows, width), jnp.bfloat16)] * (groups - 1)
    return pl.pallas_call(
        functools.partial(down_kernel, has_total, len(outs), start, units),
        in_specs=[pl.BlockSpec(memory_space=pltpu.SMEM), vmem, vmem]
        + [pl.BlockSpec(memory_space=pltpu.HBM)]
        + [vmem] * has_total
        + [pl.BlockSpec(memory_space=pl.ANY)] * len(after),
        out_specs=[vmem] * len(outs),
        out_shape=outs,
        scratch_shapes=[
            pltpu.VMEM((2 * half, cols), jnp.bfloat16),
            pltpu.VMEM((SLOTS, unit, width), jnp.bfloat16),
            pltpu.SemaphoreType.DMA((SLOTS,)),
        ]
        + [pltpu.VMEM((2 * half, width), jnp.float32)] * is_last,
        compiler_params=pltpu.CompilerParams(vmem_limit_bytes=VMEM),
        cost_estimate=pl.CostEstimate(
            flops=4 * half * units * unit * width,
            bytes_accessed=2 * units * unit * width + 16 * half * width,
            transcendentals=0,
        ),
    )(place, ours, theirs, weight, *([total] if has_total else []), *after)


def attend(residual_in, queries, key_cache, value_cache, key_new, value_new, lengths):
    cycle_size = lax.axis_size("blk")
    quarters = cycle_size // KV_HEADS
    per_kv = HEADS // KV_HEADS
    own_heads = HEADS // cycle_size
    head_size = key_cache.shape[3]
    seq_rows = residual_in.shape[0]
    positions_here = key_cache.shape[2]
    blk_index = lax.axis_index("blk")
    kv_head = blk_index // quarters
    quarter = blk_index % quarters
    score_scale = 1.0 / math.sqrt(head_size)
    group_queries = lax.dynamic_slice_in_dim(
        queries, kv_head * per_kv * head_size, per_kv * head_size, 1
    )
    group_queries = group_queries.astype(jnp.float32).reshape(seq_rows, per_kv, head_size)
    fresh_key = lax.dynamic_slice_in_dim(key_new, kv_head * head_size, head_size, 1).astype(
        jnp.float32
    )
    fresh_value = lax.dynamic_slice_in_dim(value_new, kv_head * head_size, head_size, 1).astype(
        jnp.float32
    )
    keys_here = key_cache[:, 0].astype(jnp.float32)
    values_here = value_cache[:, 0].astype(jnp.float32)
    scores = jnp.einsum("shd,spd->shp", group_queries, keys_here) * score_scale
    fresh_scores = jnp.einsum("shd,sd->sh", group_queries, fresh_key) * score_scale
    places = quarter * positions_here + jnp.arange(positions_here, dtype=jnp.int32)
    usable = (places[None, :] < lengths[:, None])[:, None, :]
    with_fresh = quarter == 0
    largest = jnp.maximum(
        jnp.max(jnp.where(usable, scores, -1e30), axis=2),
        jnp.where(with_fresh, fresh_scores, -1e30),
    )
    weights = jnp.where(usable, jnp.exp(scores - largest[..., None]), 0.0)
    fresh_weight = jnp.where(with_fresh, jnp.exp(fresh_scores - largest), 0.0)
    totals = jnp.sum(weights, axis=2) + fresh_weight
    weighted = (
        jnp.einsum("shp,spd->shd", weights, values_here)
        + fresh_weight[..., None] * fresh_value[:, None, :]
    )
    for bit_number in range(quarters.bit_length() - 1):
        peer_max, peer_total, peer_weighted = partner(
            (largest, totals, weighted), "blk", 1 << bit_number
        )
        merged = jnp.maximum(largest, peer_max)
        mine_factor = jnp.exp(largest - merged)
        peer_factor = jnp.exp(peer_max - merged)
        totals = totals * mine_factor + peer_total * peer_factor
        weighted = weighted * mine_factor[..., None] + peer_weighted * peer_factor[..., None]
        largest = merged
    attention = weighted / totals[..., None]
    own_output = lax.dynamic_slice_in_dim(attention, quarter * own_heads, own_heads, 1).reshape(
        seq_rows, own_heads * head_size
    )
    return residual_in.astype(jnp.float32) + own_output


def on_device(
    residual_in,
    queries,
    key_cache,
    value_cache,
    key_new,
    value_new,
    lengths,
    ffn_gain,
    gate_weight,
    up_weight,
    down_weight,
):
    groups = lax.axis_size("grp")
    group = lax.axis_index("grp")
    chips = lax.axis_size("blk") // 2
    chip, core = lax.axis_index("blk") // 2, lax.axis_index("blk") % 2
    rows = residual_in.shape[0]
    parts = 2 * chips // groups
    shard_rows = rows // parts

    wide = attend(residual_in, queries, key_cache, value_cache, key_new, value_new, lengths)

    tokens = (wide * ffn_gain.astype(jnp.float32)[None, :]).astype(jnp.bfloat16)
    blocks = [tokens] + [partner(tokens, "grp", i) for i in range(1, groups)]

    squares = jnp.sum(wide * wide, axis=1)
    for bit_number in range(lax.axis_size("blk").bit_length() - 1):
        squares = squares + partner(squares, "blk", 1 << bit_number)

    spot = jnp.where(chip % 2 == 1, (chip + 1) // 2, (chips - chip // 2) % chips)
    shard = jnp.arange(groups * parts, dtype=jnp.int32) ^ (group * parts)
    place = (spot - 1 - shard) % chips + jnp.where(shard // chips == core, 0, chips)
    own_shard = (core * chips + spot) ^ (group * parts)

    unit = gate_weight.shape[1] // sum(CHUNK_UNITS)
    edges = [sum(CHUNK_UNITS[:i]) for i in range(len(CHUNK_UNITS) + 1)]
    f32 = jnp.float32
    n_chunks = len(CHUNK_UNITS)
    inverse, total = None, None
    chunks = [{} for _ in range(n_chunks)]
    last = []

    order = [0, 2 * chips, 2 * chips - 1, *range(chips, 0, -1)]
    for turn in range(n_chunks + 2 * chips):
        for stage in order:
            k = turn - stage
            if stage == chips - 1:
                for j in range(1, chips - 1):
                    if 0 <= turn - chips - j < n_chunks:
                        last = last + [chunks[turn - chips - j]["hidden"][j]]
                if turn == 1:
                    last = last + squares
                    squares = jnp.stack(squares).reshape(groups * parts, shard_rows)
                    squares = lax.dynamic_index_in_dim(squares, own_shard, 0, keepdims=False)
                    inverse = lax.rsqrt(squares / D + 1e-05)[:, None]
            if not 0 <= k < n_chunks:
                continue
            units, chunk = CHUNK_UNITS[k], chunks[k]
            if stage == 0:
                ride = squares[None, :] if k == 0 else None
                keep, send, *rides = gate_up(
                    place, blocks, gate_weight, up_weight, unit, edges[k], units, last, ride
                )
                last = [keep]
                chunk.update(own=keep, flow=None)
                if k == 0:
                    squares = rides[0][0]
                    squares = [squares] + [partner(squares, "grp", i) for i in range(1, groups)]
            elif stage < chips:
                flow = pass_on(
                    stage - 1, chips, chunk["own"], chunk["other"], chunk["flow"], last
                )
                last = [flow]
                chunk["flow"] = along_ring(flow)
            elif stage == chips:
                hidden = hidden_units(chunk["flow"], chunk["own"], chunk["other"], inverse, last)
                last = [hidden]
                chunk["hidden"] = [hidden]
                for _ in range(1, chips):
                    chunk["hidden"].append(along_ring(chunk["hidden"][-1]))
            elif stage == 2 * chips - 1:
                ours = join(chunk["hidden"][1:] + chunk["hidden"][:1], last)
                last = [ours]
                chunk.update(ours=ours, theirs=partner(ours, "blk", 1))
            else:
                total, *terms = down(
                    place,
                    groups,
                    chunk["ours"],
                    chunk["theirs"],
                    down_weight,
                    total,
                    2 * unit,
                    edges[k] // 2,
                    units // 2,
                    last,
                    k == n_chunks - 1,
                )
                last = [total]
        if turn < n_chunks:
            send = hold(send, last) if turn > 0 else send
            last = [send]
            chunks[turn]["other"] = partner(send, "blk", 1)

    out = wide + total
    for i in range(1, groups):
        out = out + partner(terms[i - 1], "grp", i).astype(f32)
    return out


def solution(mesh):
    in_specs = (
        P("grp", "blk"),
        P("grp", None),
        P("grp", "blk", None, None),
        P("grp", "blk", None, None),
        P("grp", None),
        P("grp", None),
        P("grp"),
        P("blk"),
        P("blk", "grp"),
        P("blk", "grp"),
        P("grp", "blk"),
    )
    out_specs = P("grp", "blk")
    return jax.shard_map(
        on_device, mesh=mesh, in_specs=in_specs, out_specs=out_specs, check_vma=False
    )
```

profile of v0, /device:TPU:0, one launch (start us, length us, event | category | flops | bytes accessed | tf_op | source)
XLA Modules:
  0.0 199.4 jit_solution(5940602712727767503)
XLA Ops:
  0.0 1.6 copy-done
  3.5 2.0 select_reduce_fusion
  7.6 3.0 %collective-permute-start = (bf16[64,2048]{1,0:T(8,128)(2,1)S(1)}, bf16[64,2048]{1,0:T(8,128)(2,1)S(1)}, u32[]{:S(2)}, u32[]{:S(2)}) collective-permute-start(bf16[64,2048]{1,0:T(8,128)(2,1)S(1)} %get-tuple-element.30.refs_0_), channel_id=1, source_target_pairs={{0,8},{8,0},{16,24},{24,16},{1,9},{9,1},{17,25},{25,17},{2,10},{10... | collective-permute-start | bytes 786440 | tf_op jit(solution)/shard_map/ppermute | solution.py:21
  10.6 1.5 collective-permute-start.1
  12.5 1.1 collective-permute-done.3
  13.6 1.7 collective-permute-start.4
  15.3 1.8 collective-permute-done.4
  17.2 2.7 %collective-permute-start.5 = (f32[64]{0:T(128)S(1)}, f32[64]{0:T(128)S(1)}, u32[]{:S(2)}, u32[]{:S(2)}) collective-permute-start(f32[64]{0:T(128)S(1)} %add.103), channel_id=1, source_target_pairs={{0,4},{1,5},{2,6},{3,7},{4,0},{5,1},{6,2},{7,3},{8,12},{9,13},{10,... | collective-permute-start | bytes 776 | tf_op jit(solution)/shard_map/ppermute | solution.py:21
  19.9 1.7 collective-permute-done.5
  21.6 2.4 %collective-permute-done.1.refs_2_ = bf16[64,2048]{1,0:T(8,128)(2,1)S(1)} collective-permute-done((bf16[64,2048]{1,0:T(8,128)(2,1)S(1)}, bf16[64,2048]{1,0:T(8,128)(2,1)S(1)}, u32[]{:S(2)}, u32[]{:S(2)}) %collective-permute-start.1) | collective-permute-done | bytes 262176 | tf_op jit(solution)/shard_map/ppermute | solution.py:21
  24.0 8.5 %shard_map.109 = (bf16[2,128,2048]{2,1,0:T(8,128)(2,1)S(1)}, bf16[2,128,2048]{2,1,0:T(8,128)(2,1)S(1)}, f32[1,64]{1,0:T(1,128)S(1)}) custom-call(s32[8]{0:T(128)S(1)} %fusion.9.place_ref, bf16[64,2048]{1,0:T(8,128)(2,1)S(1)} %get-tuple-element.30.refs_0_, bf16[64,2048]{1,0:T(8,128)(2,1)S(1)} %collective-permute-done.refs_1_, ...), custom_call_target="tpu_custom_call" | custom-call | flops 4294967296 | bytes 19922944 | tf_op jit(solution)/shard_map/pallas_call | solution.py:96
  32.6 1.3 collective-permute-start.7
  33.9 1.0 collective-permute-start.8
  34.9 1.3 collective-permute-start.9
  36.2 0.9 copy-done.12
  37.2 0.9 copy-done.17
  38.1 0.9 copy-done.20
  39.1 0.9 copy-done.23
  40.0 10.2 %shard_map.110 = (bf16[2,128,2560]{2,1,0:T(8,128)(2,1)S(1)}, bf16[2,128,2560]{2,1,0:T(8,128)(2,1)S(1)}) custom-call(s32[8]{0:T(128)S(1)} %fusion.9.place_ref, bf16[64,2048]{1,0:T(8,128)(2,1)S(1)} %copy-done.12, bf16[64,2048]{1,0:T(8,128)(2,1)S(1)} %copy-done.17, bf16[64,2048]{1,0:T(8,128)(2,1)S(1)} %copy-done.20, bf16[64,2048]{1,0:T(8,128)(2,1)S(1)} %copy-done.23, ...), custom_call_target="tpu_custom_call" | custom-call | flops 5368709120 | bytes 24641536 | tf_op jit(solution)/shard_map/pallas_call | solution.py:96
  50.2 1.0 copy-done.9
  52.3 1.6 collective-permute-start.11
  53.9 1.3 copy-done.10
  55.2 0.9 copy-done.13
  56.2 0.9 copy-done.18
  57.1 0.9 copy-done.21
  58.1 0.9 copy-done.24
  59.0 8.5 %shard_map.113 = (bf16[2,128,2048]{2,1,0:T(8,128)(2,1)S(1)}, bf16[2,128,2048]{2,1,0:T(8,128)(2,1)S(1)}) custom-call(s32[8]{0:T(128)S(1)} %fusion.9.place_ref, bf16[64,2048]{1,0:T(8,128)(2,1)S(1)} %copy-done.13, bf16[64,2048]{1,0:T(8,128)(2,1)S(1)} %copy-done.18, bf16[64,2048]{1,0:T(8,128)(2,1)S(1)} %copy-done.21, bf16[64,2048]{1,0:T(8,128)(2,1)S(1)} %copy-done.24, ...), custom_call_target="tpu_custom_call" | custom-call | flops 4294967296 | bytes 19922944 | tf_op jit(solution)/shard_map/pallas_call | solution.py:96
  68.6 1.1 copy-done.2
  70.6 2.6 %collective-permute-start.13 = (bf16[2,32,2560]{2,1,0:T(8,128)(2,1)}, bf16[2,32,2560]{2,1,0:T(8,128)(2,1)S(1)}, u32[]{:S(2)}, u32[]{:S(2)}) collective-permute-start(bf16[2,32,2560]{2,1,0:T(8,128)(2,1)} %copy-done.25), channel_id=1, source_target_pairs={{0,2},{1,3},{2,6},{3,7},{6,4},{7,5},{4,0},{5,1},{8,10},{9,11},{10,... | collective-permute-start | bytes 983048 | tf_op jit(solution)/shard_map/ppermute | solution.py:28
  73.8 13.5 %collective-permute-done.14.refs_0_ = bf16[2,32,2048]{2,1,0:T(8,128)(2,1)S(1)} collective-permute-done((bf16[2,32,2048]{2,1,0:T(8,128)(2,1)}, bf16[2,32,2048]{2,1,0:T(8,128)(2,1)S(1)}, u32[]{:S(2)}, u32[]{:S(2)}) %collective-permute-start.14) | collective-permute-done | bytes 262176 | tf_op jit(solution)/shard_map/ppermute | solution.py:28
  87.3 1.2 copy-done.7
  88.5 1.2 copy-done.15
  90.5 0.8 shard_map.118.refs_0_
  91.4 1.7 collective-permute-start.16
  93.0 1.4 collective-permute-start.17
  94.4 2.0 %shard_map.119.refs_0_ = bf16[2,32,2048]{2,1,0:T(8,128)(2,1)} custom-call(bf16[2,128,2048]{2,1,0:T(8,128)(2,1)S(1)} %get-tuple-element.21.refs_1_.own_ref, bf16[2,128,2048]{2,1,0:T(8,128)(2,1)} %collective-permute-done.12.other_ref, bf16[2,32,2560]{2,1,0:T(8,128)(2,1)} %shard_map.118.refs_0_), custom_call_target="tpu_custom_call" | custom-call | flops 262144 | bytes 1048576 | tf_op jit(solution)/shard_map/pallas_call | solution.py:149
  96.6 12.2 %collective-permute-done.17.flow_ref = bf16[2,32,2048]{2,1,0:T(8,128)(2,1)} collective-permute-done((bf16[2,32,2048]{2,1,0:T(8,128)(2,1)}, bf16[2,32,2048]{2,1,0:T(8,128)(2,1)}, u32[]{:S(2)}, u32[]{:S(2)}) %collective-permute-start.17) | collective-permute-done | bytes 262176 | tf_op jit(solution)/shard_map/ppermute | solution.py:28
  108.8 1.2 copy-done.8
  110.1 1.2 shard_map.120.refs_1_.refs_3_
  111.2 1.1 shard_map.121.refs_1_
  113.2 1.4 shard_map.122.refs_0_
  114.5 2.3 %collective-permute-start.18 = (bf16[2,32,2048]{2,1,0:T(8,128)(2,1)S(1)}, bf16[2,32,2048]{2,1,0:T(8,128)(2,1)S(1)}, u32[]{:S(2)}, u32[]{:S(2)}) collective-permute-start(bf16[2,32,2048]{2,1,0:T(8,128)(2,1)S(1)} %shard_map.122.refs_0_), channel_id=1, source_target_pairs={{0,2},{1,3},{2,6},{3,7},{6,4},{7,5},{4,0},{5,1},{8,10},{9,11},{10,... | collective-permute-start | bytes 786440 | tf_op jit(solution)/shard_map/ppermute | solution.py:28
  117.2 6.7 %collective-permute-done.19.flow_ref = bf16[2,32,2560]{2,1,0:T(8,128)(2,1)S(1)} collective-permute-done((bf16[2,32,2560]{2,1,0:T(8,128)(2,1)S(1)}, bf16[2,32,2560]{2,1,0:T(8,128)(2,1)S(1)}, u32[]{:S(2)}, u32[]{:S(2)}) %collective-permute-start.19) | collective-permute-done | bytes 327712 | tf_op jit(solution)/shard_map/ppermute | solution.py:28
  124.2 4.1 %collective-permute-done.20.refs_2_.refs_0_ = bf16[32,2048]{1,0:T(8,128)(2,1)S(1)} collective-permute-done((bf16[32,2048]{1,0:T(8,128)(2,1)S(1)}, bf16[32,2048]{1,0:T(8,128)(2,1)S(1)}, u32[]{:S(2)}, u32[]{:S(2)}) %collective-permute-start.20) | collective-permute-done | bytes 131104 | tf_op jit(solution)/shard_map/ppermute | solution.py:28
  128.3 1.3 shard_map.124.refs_0_
  130.4 2.2 %collective-permute-start.28 = (bf16[32,2048]{1,0:T(8,128)(2,1)S(1)}, bf16[32,2048]{1,0:T(8,128)(2,1)S(1)}, u32[]{:S(2)}, u32[]{:S(2)}) collective-permute-start(bf16[32,2048]{1,0:T(8,128)(2,1)S(1)} %collective-permute-done.20.refs_2_.refs_0_), channel_id=1, source_target_pairs={{0,2},{1,3},{2,6},{3,7},{6,4},{7,5},{4,0},{5,1},{8,10},{9,11},{10,... | collective-permute-start | bytes 393224 | tf_op jit(solution)/shard_map/ppermute | solution.py:28
  132.6 8.2 %collective-permute-done.28.refs_1_.refs_6_ = bf16[32,2048]{1,0:T(8,128)(2,1)S(1)} collective-permute-done((bf16[32,2048]{1,0:T(8,128)(2,1)S(1)}, bf16[32,2048]{1,0:T(8,128)(2,1)S(1)}, u32[]{:S(2)}, u32[]{:S(2)}) %collective-permute-start.28) | collective-permute-done | bytes 131104 | tf_op jit(solution)/shard_map/ppermute | solution.py:28
  141.5 1.4 shard_map.125.refs_4_.refs_3_
  142.9 3.8 %collective-permute-done.29.refs_2_ = bf16[32,2048]{1,0:T(8,128)(2,1)S(1)} collective-permute-done((bf16[32,2048]{1,0:T(8,128)(2,1)S(1)}, bf16[32,2048]{1,0:T(8,128)(2,1)S(1)}, u32[]{:S(2)}, u32[]{:S(2)}) %collective-permute-start.29) | collective-permute-done | bytes 131104 | tf_op jit(solution)/shard_map/ppermute | solution.py:28
  146.9 2.7 %collective-permute-start.22 = (bf16[32,2048]{1,0:T(8,128)(2,1)S(1)}, bf16[32,2048]{1,0:T(8,128)(2,1)S(1)}, u32[]{:S(2)}, u32[]{:S(2)}) collective-permute-start(bf16[32,2048]{1,0:T(8,128)(2,1)S(1)} %shard_map.125.refs_4_.refs_3_), channel_id=1, source_target_pairs={{0,2},{1,3},{2,6},{3,7},{6,4},{7,5},{4,0},{5,1},{8,10},{9,11},{10,... | collective-permute-start | bytes 393224 | tf_op jit(solution)/shard_map/ppermute | solution.py:28
  149.6 5.2 %collective-permute-done.26.refs_5_.refs_1_ = bf16[32,2560]{1,0:T(8,128)(2,1)S(1)} collective-permute-done((bf16[32,2560]{1,0:T(8,128)(2,1)S(1)}, bf16[32,2560]{1,0:T(8,128)(2,1)S(1)}, u32[]{:S(2)}, u32[]{:S(2)}) %collective-permute-start.26) | collective-permute-done | bytes 163872 | tf_op jit(solution)/shard_map/ppermute | solution.py:28
  154.8 2.4 %collective-permute-done.22.refs_4_.refs_0_ = bf16[32,2048]{1,0:T(8,128)(2,1)S(1)} collective-permute-done((bf16[32,2048]{1,0:T(8,128)(2,1)S(1)}, bf16[32,2048]{1,0:T(8,128)(2,1)S(1)}, u32[]{:S(2)}, u32[]{:S(2)}) %collective-permute-start.22) | collective-permute-done | bytes 131104 | tf_op jit(solution)/shard_map/ppermute | solution.py:28
  157.1 5.4 %shard_map.127.refs_4_.refs_3_ = f32[256,2048]{1,0:T(8,128)S(1)} custom-call(s32[8]{0:T(128)S(1)} %fusion.9.place_ref, bf16[128,2048]{1,0:T(8,128)(2,1)S(1)} %shard_map.126.refs_0_.refs_3_, bf16[128,2048]{1,0:T(8,128)(2,1)S(1)} %collective-permute-done.30.refs_1_, bf16[6656,2048]{1,0:T(8,128)(2,1)} %refs_2_.5, ...), custom_call_target="tpu_custom_call" | custom-call | flops 2147483648 | bytes 12582912 | tf_op jit(solution)/shard_map/pallas_call | solution.py:257
  163.0 6.4 %collective-permute-done.23.refs_5_.refs_1_ = bf16[32,2048]{1,0:T(8,128)(2,1)S(1)} collective-permute-done((bf16[32,2048]{1,0:T(8,128)(2,1)S(1)}, bf16[32,2048]{1,0:T(8,128)(2,1)S(1)}, u32[]{:S(2)}, u32[]{:S(2)}) %collective-permute-start.23) | collective-permute-done | bytes 131104 | tf_op jit(solution)/shard_map/ppermute | solution.py:28
  169.5 6.1 %shard_map.129.refs_4_.refs_3_ = f32[256,2048]{1,0:T(8,128)S(1)} custom-call(s32[8]{0:T(128)S(1)} %fusion.9.place_ref, bf16[128,2560]{1,0:T(8,128)(2,1)S(1)} %shard_map.128.refs_0_.refs_4_, bf16[128,2560]{1,0:T(8,128)(2,1)S(1)} %collective-permute-done.31.refs_1_, bf16[6656,2048]{1,0:T(8,128)(2,1)} %refs_2_.5, f32[256,2048]{1,0:T(8,128)S(1)} %shard_map.127.refs_4_.refs_3_, ...), custom_call_target="tpu_custom_call" | custom-call | flops 2684354560 | bytes 14680064 | tf_op jit(solution)/shard_map/pallas_call | solution.py:257
  175.8 1.9 collective-permute-done.32.refs_1_
  177.7 5.5 %shard_map.131 = (f32[64,2048]{1,0:T(8,128)S(1)}, bf16[64,2048]{1,0:T(8,128)(2,1)S(1)}, bf16[64,2048]{1,0:T(8,128)(2,1)S(1)}, bf16[64,2048]{1,0:T(8,128)(2,1)S(1)}) custom-call(s32[8]{0:T(128)S(1)} %fusion.9.place_ref, bf16[128,2048]{1,0:T(8,128)(2,1)S(1)} %shard_map.130.refs_0_.refs_4_, bf16[128,2048]{1,0:T(8,128)(2,1)S(1)} %collective-permute-done.32.refs_1_, ...), custom_call_target="tpu_custom_call" | custom-call | flops 2147483648 | bytes 12582912 | tf_op jit(solution)/shard_map/pallas_call | solution.py:257
  183.2 1.3 collective-permute-start.33
  184.5 1.0 collective-permute-start.34
  185.5 1.3 collective-permute-start.35
  186.7 5.7 %collective-permute-done.33 = bf16[64,2048]{1,0:T(8,128)(2,1)S(1)} collective-permute-done((bf16[64,2048]{1,0:T(8,128)(2,1)S(1)}, bf16[64,2048]{1,0:T(8,128)(2,1)S(1)}, u32[]{:S(2)}, u32[]{:S(2)}) %collective-permute-start.33) | collective-permute-done | bytes 262176 | tf_op jit(solution)/shard_map/ppermute | solution.py:21
  192.4 4.3 %collective-permute-done.34 = bf16[64,2048]{1,0:T(8,128)(2,1)S(1)} collective-permute-done((bf16[64,2048]{1,0:T(8,128)(2,1)S(1)}, bf16[64,2048]{1,0:T(8,128)(2,1)S(1)}, u32[]{:S(2)}, u32[]{:S(2)}) %collective-permute-start.34) | collective-permute-done | bytes 262176 | tf_op jit(solution)/shard_map/ppermute | solution.py:21
  196.7 1.5 collective-permute-done.35
  198.2 1.2 convert_add_fusion
  (121 shorter events, 12.9 us)
Async XLA Ops:
  0.0 1.6 copy-start
  1.6 5.0 %copy-start.32 = (bf16[2048]{0:T(1024)(128)(2,1)S(1)}, bf16[2048]{0:T(1024)(128)(2,1)}, u32[]{:S(2)}) copy-start(bf16[2048]{0:T(1024)(128)(2,1)} %param.18) | copy-start | bytes 12292
  1.6 5.0 %copy-start.33 = (bf16[64,1,64,128]{3,2,1,0:T(8,128)(2,1)S(1)}, bf16[64,1,64,128]{3,2,1,0:T(8,128)(2,1)}, u32[]{:S(2)}) copy-start(bf16[64,1,64,128]{3,2,1,0:T(8,128)(2,1)} %param.14) | copy-start | bytes 3145732
  5.4 1.9 copy-start.30
  7.3 3.3 %copy-start.28 = (f32[64,16,128]{2,1,0:T(8,128)}, f32[64,16,128]{2,1,0:T(8,128)S(1)}, u32[]{:S(2)}) copy-start(f32[64,16,128]{2,1,0:T(8,128)S(1)} %fusion) | copy-start | bytes 1572868
  7.6 24.9 %copy-start.11 = (bf16[64,2048]{1,0:T(8,128)(2,1)}, bf16[64,2048]{1,0:T(8,128)(2,1)S(1)}, u32[]{:S(2)}) copy-start(bf16[64,2048]{1,0:T(8,128)(2,1)S(1)} %get-tuple-element.30.refs_0_) | copy-start | bytes 786436
  7.6 14.0 %collective-permute-start = (bf16[64,2048]{1,0:T(8,128)(2,1)S(1)}, bf16[64,2048]{1,0:T(8,128)(2,1)S(1)}, u32[]{:S(2)}, u32[]{:S(2)}) collective-permute-start(bf16[64,2048]{1,0:T(8,128)(2,1)S(1)} %get-tuple-element.30.refs_0_), channel_id=1, source_target_pairs={{0,8},{8,0},{16,24},{24,16},{1,9},{9,1},{17,25},{25,17},{2,10},{10... | collective-permute-start | bytes 786440 | tf_op jit(solution)/shard_map/ppermute | solution.py:21
  10.6 13.4 %collective-permute-start.1 = (bf16[64,2048]{1,0:T(8,128)(2,1)S(1)}, bf16[64,2048]{1,0:T(8,128)(2,1)S(1)}, u32[]{:S(2)}, u32[]{:S(2)}) collective-permute-start(bf16[64,2048]{1,0:T(8,128)(2,1)S(1)} %get-tuple-element.30.refs_0_), channel_id=1, source_target_pairs={{0,16},{8,24},{16,0},{24,8},{1,17},{9,25},{17,1},{25,9},{2,18},{10... | collective-permute-start | bytes 786440 | tf_op jit(solution)/shard_map/ppermute | solution.py:21
  12.1 11.9 %collective-permute-start.2 = (bf16[64,2048]{1,0:T(8,128)(2,1)S(1)}, bf16[64,2048]{1,0:T(8,128)(2,1)S(1)}, u32[]{:S(2)}, u32[]{:S(2)}) collective-permute-start(bf16[64,2048]{1,0:T(8,128)(2,1)S(1)} %get-tuple-element.30.refs_0_), channel_id=1, source_target_pairs={{0,24},{8,16},{16,8},{24,0},{1,25},{9,17},{17,9},{25,1},{2,26},{10... | collective-permute-start | bytes 786440 | tf_op jit(solution)/shard_map/ppermute | solution.py:21
  12.5 1.1 collective-permute-start.3
  13.6 3.5 %collective-permute-start.4 = (f32[64]{0:T(128)S(1)}, f32[64]{0:T(128)S(1)}, u32[]{:S(2)}, u32[]{:S(2)}) collective-permute-start(f32[64]{0:T(128)S(1)} %add.102), channel_id=1, source_target_pairs={{0,2},{1,3},{2,0},{3,1},{4,6},{5,7},{6,4},{7,5},{8,10},{9,11},{10,... | collective-permute-start | bytes 776 | tf_op jit(solution)/shard_map/ppermute | solution.py:21
  17.2 4.4 %collective-permute-start.5 = (f32[64]{0:T(128)S(1)}, f32[64]{0:T(128)S(1)}, u32[]{:S(2)}, u32[]{:S(2)}) collective-permute-start(f32[64]{0:T(128)S(1)} %add.103), channel_id=1, source_target_pairs={{0,4},{1,5},{2,6},{3,7},{4,0},{5,1},{6,2},{7,3},{8,12},{9,13},{10,... | collective-permute-start | bytes 776 | tf_op jit(solution)/shard_map/ppermute | solution.py:21
  21.6 10.9 %copy-start.16 = (bf16[64,2048]{1,0:T(8,128)(2,1)}, bf16[64,2048]{1,0:T(8,128)(2,1)S(1)}, u32[]{:S(2)}) copy-start(bf16[64,2048]{1,0:T(8,128)(2,1)S(1)} %collective-permute-done.refs_1_) | copy-start | bytes 786436
  24.0 8.5 %copy-start.19 = (bf16[64,2048]{1,0:T(8,128)(2,1)}, bf16[64,2048]{1,0:T(8,128)(2,1)S(1)}, u32[]{:S(2)}) copy-start(bf16[64,2048]{1,0:T(8,128)(2,1)S(1)} %collective-permute-done.1.refs_2_) | copy-start | bytes 786436
  24.0 8.5 %copy-start.22 = (bf16[64,2048]{1,0:T(8,128)(2,1)}, bf16[64,2048]{1,0:T(8,128)(2,1)S(1)}, u32[]{:S(2)}) copy-start(bf16[64,2048]{1,0:T(8,128)(2,1)S(1)} %collective-permute-done.2.refs_3_) | copy-start | bytes 786436
  32.6 17.6 %collective-permute-start.6 = (bf16[2,128,2048]{2,1,0:T(8,128)(2,1)S(1)}, bf16[2,128,2048]{2,1,0:T(8,128)(2,1)S(1)}, u32[]{:S(2)}, u32[]{:S(2)}) collective-permute-start(bf16[2,128,2048]{2,1,0:T(8,128)(2,1)S(1)} %get-tuple-element.16.refs_6_), channel_id=1, source_target_pairs={{0,1},{1,0},{2,3},{3,2},{4,5},{5,4},{6,7},{7,6},{8,9},{9,8},{10,11... | collective-permute-start | bytes 3145736 | tf_op jit(solution)/shard_map/ppermute | solution.py:21
  32.6 17.5 %collective-permute-start.7 = (f32[64]{0:T(128)S(1)}, f32[64]{0:T(128)S(1)}, u32[]{:S(2)}, u32[]{:S(2)}) collective-permute-start(f32[64]{0:T(128)S(1)} %bitcast.34), channel_id=1, source_target_pairs={{0,8},{8,0},{16,24},{24,16},{1,9},{9,1},{17,25},{25,17},{2,10},{10... | collective-permute-start | bytes 776 | tf_op jit(solution)/shard_map/ppermute | solution.py:21
  33.9 16.3 %collective-permute-start.8 = (f32[64]{0:T(128)S(1)}, f32[64]{0:T(128)S(1)}, u32[]{:S(2)}, u32[]{:S(2)}) collective-permute-start(f32[64]{0:T(128)S(1)} %bitcast.35), channel_id=1, source_target_pairs={{0,16},{8,24},{16,0},{24,8},{1,17},{9,25},{17,1},{25,9},{2,18},{10... | collective-permute-start | bytes 776 | tf_op jit(solution)/shard_map/ppermute | solution.py:21
  34.9 15.3 %collective-permute-start.9 = (f32[64]{0:T(128)S(1)}, f32[64]{0:T(128)S(1)}, u32[]{:S(2)}, u32[]{:S(2)}) collective-permute-start(f32[64]{0:T(128)S(1)} %bitcast.36), channel_id=1, source_target_pairs={{0,24},{8,16},{16,8},{24,0},{1,25},{9,17},{17,9},{25,1},{2,26},{10... | collective-permute-start | bytes 776 | tf_op jit(solution)/shard_map/ppermute | solution.py:21
  36.2 0.9 copy-start.12
  37.2 0.9 copy-start.17
  38.1 0.9 copy-start.20
  39.1 0.9 copy-start.23
  50.2 1.1 copy-start.9
  51.3 1.1 copy-start.5
  52.3 15.3 %collective-permute-start.10 = (bf16[2,128,2560]{2,1,0:T(8,128)(2,1)}, bf16[2,128,2560]{2,1,0:T(8,128)(2,1)S(1)}, u32[]{:S(2)}, u32[]{:S(2)}) collective-permute-start(bf16[2,128,2560]{2,1,0:T(8,128)(2,1)} %shard_map.112.refs_6_), channel_id=1, source_target_pairs={{0,1},{1,0},{2,3},{3,2},{4,5},{5,4},{6,7},{7,6},{8,9},{9,8},{10,11... | collective-permute-start | bytes 3932168 | tf_op jit(solution)/shard_map/ppermute | solution.py:21
  52.3 15.2 %copy-start.6 = (bf16[2,128,2048]{2,1,0:T(8,128)(2,1)S(1)}, bf16[2,128,2048]{2,1,0:T(8,128)(2,1)}, u32[]{:S(2)}) copy-start(bf16[2,128,2048]{2,1,0:T(8,128)(2,1)} %copy-done.5) | copy-start | bytes 3145732
  52.3 15.2 %collective-permute-start.11 = (bf16[2,32,2048]{2,1,0:T(8,128)(2,1)}, bf16[2,32,2048]{2,1,0:T(8,128)(2,1)S(1)}, u32[]{:S(2)}, u32[]{:S(2)}) collective-permute-start(bf16[2,32,2048]{2,1,0:T(8,128)(2,1)} %copy-done.27), channel_id=1, source_target_pairs={{0,2},{1,3},{2,6},{3,7},{6,4},{7,5},{4,0},{5,1},{8,10},{9,11},{10,... | collective-permute-start | bytes 786440 | tf_op jit(solution)/shard_map/ppermute | solution.py:28
  53.9 1.3 copy-start.10
  55.2 0.9 copy-start.13
  67.5 1.0 copy-start.14
  68.6 1.1 copy-start.2
  70.4 20.1 %copy-start.3 = (bf16[2,128,2560]{2,1,0:T(8,128)(2,1)S(1)}, bf16[2,128,2560]{2,1,0:T(8,128)(2,1)}, u32[]{:S(2)}) copy-start(bf16[2,128,2560]{2,1,0:T(8,128)(2,1)} %copy-done.2) | copy-start | bytes 3932164
  70.4 24.0 %collective-permute-start.12 = (bf16[2,128,2048]{2,1,0:T(8,128)(2,1)}, bf16[2,128,2048]{2,1,0:T(8,128)(2,1)}, u32[]{:S(2)}, u32[]{:S(2)}) collective-permute-start(bf16[2,128,2048]{2,1,0:T(8,128)(2,1)} %shard_map.116.refs_1_), channel_id=1, source_target_pairs={{0,1},{1,0},{2,3},{3,2},{4,5},{5,4},{6,7},{7,6},{8,9},{9,8},{10,11... | collective-permute-start | bytes 3145736 | tf_op jit(solution)/shard_map/ppermute | solution.py:21
  70.6 19.9 %collective-permute-start.13 = (bf16[2,32,2560]{2,1,0:T(8,128)(2,1)}, bf16[2,32,2560]{2,1,0:T(8,128)(2,1)S(1)}, u32[]{:S(2)}, u32[]{:S(2)}) collective-permute-start(bf16[2,32,2560]{2,1,0:T(8,128)(2,1)} %copy-done.25), channel_id=1, source_target_pairs={{0,2},{1,3},{2,6},{3,7},{6,4},{7,5},{4,0},{5,1},{8,10},{9,11},{10,... | collective-permute-start | bytes 983048 | tf_op jit(solution)/shard_map/ppermute | solution.py:28
  73.2 14.0 %collective-permute-start.14 = (bf16[2,32,2048]{2,1,0:T(8,128)(2,1)}, bf16[2,32,2048]{2,1,0:T(8,128)(2,1)S(1)}, u32[]{:S(2)}, u32[]{:S(2)}) collective-permute-start(bf16[2,32,2048]{2,1,0:T(8,128)(2,1)} %copy-done.26), channel_id=1, source_target_pairs={{0,2},{1,3},{2,6},{3,7},{6,4},{7,5},{4,0},{5,1},{8,10},{9,11},{10,... | collective-permute-start | bytes 786440 | tf_op jit(solution)/shard_map/ppermute | solution.py:28
  87.3 1.2 copy-start.7
  88.5 1.2 copy-start.15
  91.4 19.9 %collective-permute-start.16 = (bf16[2,32,2560]{2,1,0:T(8,128)(2,1)}, bf16[2,32,2560]{2,1,0:T(8,128)(2,1)}, u32[]{:S(2)}, u32[]{:S(2)}) collective-permute-start(bf16[2,32,2560]{2,1,0:T(8,128)(2,1)} %shard_map.118.refs_0_), channel_id=1, source_target_pairs={{0,2},{1,3},{2,6},{3,7},{6,4},{7,5},{4,0},{5,1},{8,10},{9,11},{10,... | collective-permute-start | bytes 983048 | tf_op jit(solution)/shard_map/ppermute | solution.py:28
  93.0 15.8 %collective-permute-start.17 = (bf16[2,32,2048]{2,1,0:T(8,128)(2,1)}, bf16[2,32,2048]{2,1,0:T(8,128)(2,1)}, u32[]{:S(2)}, u32[]{:S(2)}) collective-permute-start(bf16[2,32,2048]{2,1,0:T(8,128)(2,1)} %shard_map.117.refs_1_), channel_id=1, source_target_pairs={{0,2},{1,3},{2,6},{3,7},{6,4},{7,5},{4,0},{5,1},{8,10},{9,11},{10,... | collective-permute-start | bytes 786440 | tf_op jit(solution)/shard_map/ppermute | solution.py:28
  96.4 16.8 %collective-permute-start.15 = (bf16[2,32,2048]{2,1,0:T(8,128)(2,1)}, bf16[2,32,2048]{2,1,0:T(8,128)(2,1)}, u32[]{:S(2)}, u32[]{:S(2)}) collective-permute-start(bf16[2,32,2048]{2,1,0:T(8,128)(2,1)} %shard_map.119.refs_0_), channel_id=1, source_target_pairs={{0,2},{1,3},{2,6},{3,7},{6,4},{7,5},{4,0},{5,1},{8,10},{9,11},{10,... | collective-permute-start | bytes 786440 | tf_op jit(solution)/shard_map/ppermute | solution.py:28
  96.6 14.6 %copy-start.4 = (bf16[2,128,2560]{2,1,0:T(8,128)(2,1)S(1)}, bf16[2,128,2560]{2,1,0:T(8,128)(2,1)}, u32[]{:S(2)}) copy-start(bf16[2,128,2560]{2,1,0:T(8,128)(2,1)} %copy-done.2) | copy-start | bytes 3932164
  108.8 1.2 copy-start.8
  112.3 11.6 %collective-permute-start.19 = (bf16[2,32,2560]{2,1,0:T(8,128)(2,1)S(1)}, bf16[2,32,2560]{2,1,0:T(8,128)(2,1)S(1)}, u32[]{:S(2)}, u32[]{:S(2)}) collective-permute-start(bf16[2,32,2560]{2,1,0:T(8,128)(2,1)S(1)} %shard_map.121.refs_1_), channel_id=1, source_target_pairs={{0,2},{1,3},{2,6},{3,7},{6,4},{7,5},{4,0},{5,1},{8,10},{9,11},{10,... | collective-permute-start | bytes 983048 | tf_op jit(solution)/shard_map/ppermute | solution.py:28
  114.5 13.8 %collective-permute-start.18 = (bf16[2,32,2048]{2,1,0:T(8,128)(2,1)S(1)}, bf16[2,32,2048]{2,1,0:T(8,128)(2,1)S(1)}, u32[]{:S(2)}, u32[]{:S(2)}) collective-permute-start(bf16[2,32,2048]{2,1,0:T(8,128)(2,1)S(1)} %shard_map.122.refs_0_), channel_id=1, source_target_pairs={{0,2},{1,3},{2,6},{3,7},{6,4},{7,5},{4,0},{5,1},{8,10},{9,11},{10,... | collective-permute-start | bytes 786440 | tf_op jit(solution)/shard_map/ppermute | solution.py:28
  116.8 11.5 %collective-permute-start.20 = (bf16[32,2048]{1,0:T(8,128)(2,1)S(1)}, bf16[32,2048]{1,0:T(8,128)(2,1)S(1)}, u32[]{:S(2)}, u32[]{:S(2)}) collective-permute-start(bf16[32,2048]{1,0:T(8,128)(2,1)S(1)} %shard_map.120.refs_1_.refs_3_), channel_id=1, source_target_pairs={{0,2},{1,3},{2,6},{3,7},{6,4},{7,5},{4,0},{5,1},{8,10},{9,11},{10,... | collective-permute-start | bytes 393224 | tf_op jit(solution)/shard_map/ppermute | solution.py:28
  129.6 11.8 %collective-permute-start.21 = (bf16[2,32,2048]{2,1,0:T(8,128)(2,1)S(1)}, bf16[2,32,2048]{2,1,0:T(8,128)(2,1)S(1)}, u32[]{:S(2)}, u32[]{:S(2)}) collective-permute-start(bf16[2,32,2048]{2,1,0:T(8,128)(2,1)S(1)} %shard_map.124.refs_0_), channel_id=1, source_target_pairs={{0,2},{1,3},{2,6},{3,7},{6,4},{7,5},{4,0},{5,1},{8,10},{9,11},{10,... | collective-permute-start | bytes 786440 | tf_op jit(solution)/shard_map/ppermute | solution.py:28
  130.4 10.4 %collective-permute-start.28 = (bf16[32,2048]{1,0:T(8,128)(2,1)S(1)}, bf16[32,2048]{1,0:T(8,128)(2,1)S(1)}, u32[]{:S(2)}, u32[]{:S(2)}) collective-permute-start(bf16[32,2048]{1,0:T(8,128)(2,1)S(1)} %collective-permute-done.20.refs_2_.refs_0_), channel_id=1, source_target_pairs={{0,2},{1,3},{2,6},{3,7},{6,4},{7,5},{4,0},{5,1},{8,10},{9,11},{10,... | collective-permute-start | bytes 393224 | tf_op jit(solution)/shard_map/ppermute | solution.py:28
  132.6 14.1 %collective-permute-start.25 = (bf16[32,2560]{1,0:T(8,128)(2,1)S(1)}, bf16[32,2560]{1,0:T(8,128)(2,1)S(1)}, u32[]{:S(2)}, u32[]{:S(2)}) collective-permute-start(bf16[32,2560]{1,0:T(8,128)(2,1)S(1)} %shard_map.123.refs_1_.refs_3_), channel_id=1, source_target_pairs={{0,2},{1,3},{2,6},{3,7},{6,4},{7,5},{4,0},{5,1},{8,10},{9,11},{10,... | collective-permute-start | bytes 491528 | tf_op jit(solution)/shard_map/ppermute | solution.py:28
  140.8 5.9 %collective-permute-start.29 = (bf16[32,2048]{1,0:T(8,128)(2,1)S(1)}, bf16[32,2048]{1,0:T(8,128)(2,1)S(1)}, u32[]{:S(2)}, u32[]{:S(2)}) collective-permute-start(bf16[32,2048]{1,0:T(8,128)(2,1)S(1)} %collective-permute-done.28.refs_1_.refs_6_), channel_id=1, source_target_pairs={{0,2},{1,3},{2,6},{3,7},{6,4},{7,5},{4,0},{5,1},{8,10},{9,11},{10,... | collective-permute-start | bytes 393224 | tf_op jit(solution)/shard_map/ppermute | solution.py:28
  146.7 10.4 %collective-permute-start.30 = (bf16[128,2048]{1,0:T(8,128)(2,1)S(1)}, bf16[128,2048]{1,0:T(8,128)(2,1)S(1)}, u32[]{:S(2)}, u32[]{:S(2)}) collective-permute-start(bf16[128,2048]{1,0:T(8,128)(2,1)S(1)} %shard_map.126.refs_0_.refs_3_), channel_id=1, source_target_pairs={{0,1},{1,0},{2,3},{3,2},{4,5},{5,4},{6,7},{7,6},{8,9},{9,8},{10,11... | collective-permute-start | bytes 1572872 | tf_op jit(solution)/shard_map/ppermute | solution.py:21
  146.8 8.0 %collective-permute-start.26 = (bf16[32,2560]{1,0:T(8,128)(2,1)S(1)}, bf16[32,2560]{1,0:T(8,128)(2,1)S(1)}, u32[]{:S(2)}, u32[]{:S(2)}) collective-permute-start(bf16[32,2560]{1,0:T(8,128)(2,1)S(1)} %collective-permute-done.25.refs_5_.refs_0_), channel_id=1, source_target_pairs={{0,2},{1,3},{2,6},{3,7},{6,4},{7,5},{4,0},{5,1},{8,10},{9,11},{10,... | collective-permute-start | bytes 491528 | tf_op jit(solution)/shard_map/ppermute | solution.py:28
  146.9 10.2 %collective-permute-start.22 = (bf16[32,2048]{1,0:T(8,128)(2,1)S(1)}, bf16[32,2048]{1,0:T(8,128)(2,1)S(1)}, u32[]{:S(2)}, u32[]{:S(2)}) collective-permute-start(bf16[32,2048]{1,0:T(8,128)(2,1)S(1)} %shard_map.125.refs_4_.refs_3_), channel_id=1, source_target_pairs={{0,2},{1,3},{2,6},{3,7},{6,4},{7,5},{4,0},{5,1},{8,10},{9,11},{10,... | collective-permute-start | bytes 393224 | tf_op jit(solution)/shard_map/ppermute | solution.py:28
  154.8 7.7 %collective-permute-start.27 = (bf16[32,2560]{1,0:T(8,128)(2,1)S(1)}, bf16[32,2560]{1,0:T(8,128)(2,1)S(1)}, u32[]{:S(2)}, u32[]{:S(2)}) collective-permute-start(bf16[32,2560]{1,0:T(8,128)(2,1)S(1)} %collective-permute-done.26.refs_5_.refs_1_), channel_id=1, source_target_pairs={{0,2},{1,3},{2,6},{3,7},{6,4},{7,5},{4,0},{5,1},{8,10},{9,11},{10,... | collective-permute-start | bytes 491528 | tf_op jit(solution)/shard_map/ppermute | solution.py:28
  162.6 6.9 %collective-permute-start.31 = (bf16[128,2560]{1,0:T(8,128)(2,1)S(1)}, bf16[128,2560]{1,0:T(8,128)(2,1)S(1)}, u32[]{:S(2)}, u32[]{:S(2)}) collective-permute-start(bf16[128,2560]{1,0:T(8,128)(2,1)S(1)} %shard_map.128.refs_0_.refs_4_), channel_id=1, source_target_pairs={{0,1},{1,0},{2,3},{3,2},{4,5},{5,4},{6,7},{7,6},{8,9},{9,8},{10,11... | collective-permute-start | bytes 1966088 | tf_op jit(solution)/shard_map/ppermute | solution.py:21
  162.7 6.8 %collective-permute-start.23 = (bf16[32,2048]{1,0:T(8,128)(2,1)S(1)}, bf16[32,2048]{1,0:T(8,128)(2,1)S(1)}, u32[]{:S(2)}, u32[]{:S(2)}) collective-permute-start(bf16[32,2048]{1,0:T(8,128)(2,1)S(1)} %collective-permute-done.22.refs_4_.refs_0_), channel_id=1, source_target_pairs={{0,2},{1,3},{2,6},{3,7},{6,4},{7,5},{4,0},{5,1},{8,10},{9,11},{10,... | collective-permute-start | bytes 393224 | tf_op jit(solution)/shard_map/ppermute | solution.py:28
  169.4 6.2 %collective-permute-start.24 = (bf16[32,2048]{1,0:T(8,128)(2,1)S(1)}, bf16[32,2048]{1,0:T(8,128)(2,1)S(1)}, u32[]{:S(2)}, u32[]{:S(2)}) collective-permute-start(bf16[32,2048]{1,0:T(8,128)(2,1)S(1)} %collective-permute-done.23.refs_5_.refs_1_), channel_id=1, source_target_pairs={{0,2},{1,3},{2,6},{3,7},{6,4},{7,5},{4,0},{5,1},{8,10},{9,11},{10,... | collective-permute-start | bytes 393224 | tf_op jit(solution)/shard_map/ppermute | solution.py:28
  175.7 22.6 %copy-start.29 = (f32[64,16,128]{2,1,0:T(8,128)S(1)}, f32[64,16,128]{2,1,0:T(8,128)}, u32[]{:S(2)}) copy-start(f32[64,16,128]{2,1,0:T(8,128)} %copy-done.28) | copy-start | bytes 1572868
  175.7 22.5 %copy-start.31 = (bf16[64,2048]{1,0:T(8,128)(2,1)S(1)}, bf16[64,2048]{1,0:T(8,128)(2,1)}, u32[]{:S(2)}) copy-start(bf16[64,2048]{1,0:T(8,128)(2,1)} %param.11) | copy-start | bytes 786436
  175.7 2.0 collective-permute-start.32
  177.7 21.7 %copy-start.1 = (bf16[64,16384]{1,0:T(8,128)(2,1)S(1)}, bf16[64,16384]{1,0:T(8,128)(2,1)}, u32[]{:S(2)}) copy-start(bf16[64,16384]{1,0:T(8,128)(2,1)} %param.12) | copy-start | bytes 6291460
  183.2 9.2 %collective-permute-start.33 = (bf16[64,2048]{1,0:T(8,128)(2,1)S(1)}, bf16[64,2048]{1,0:T(8,128)(2,1)S(1)}, u32[]{:S(2)}, u32[]{:S(2)}) collective-permute-start(bf16[64,2048]{1,0:T(8,128)(2,1)S(1)} %get-tuple-element.24), channel_id=1, source_target_pairs={{0,8},{8,0},{16,24},{24,16},{1,9},{9,1},{17,25},{25,17},{2,10},{10... | collective-permute-start | bytes 786440 | tf_op jit(solution)/shard_map/ppermute | solution.py:21
  184.5 12.2 %collective-permute-start.34 = (bf16[64,2048]{1,0:T(8,128)(2,1)S(1)}, bf16[64,2048]{1,0:T(8,128)(2,1)S(1)}, u32[]{:S(2)}, u32[]{:S(2)}) collective-permute-start(bf16[64,2048]{1,0:T(8,128)(2,1)S(1)} %get-tuple-element.25), channel_id=1, source_target_pairs={{0,16},{8,24},{16,0},{24,8},{1,17},{9,25},{17,1},{25,9},{2,18},{10... | collective-permute-start | bytes 786440 | tf_op jit(solution)/shard_map/ppermute | solution.py:21
  185.5 12.7 %collective-permute-start.35 = (bf16[64,2048]{1,0:T(8,128)(2,1)S(1)}, bf16[64,2048]{1,0:T(8,128)(2,1)S(1)}, u32[]{:S(2)}, u32[]{:S(2)}) collective-permute-start(bf16[64,2048]{1,0:T(8,128)(2,1)S(1)} %get-tuple-element.26), channel_id=1, source_target_pairs={{0,24},{8,16},{16,8},{24,0},{1,25},{9,17},{17,9},{25,1},{2,26},{10... | collective-permute-start | bytes 786440 | tf_op jit(solution)/shard_map/ppermute | solution.py:21
  (6 other events, 5.3 us)
where the time goes:
time: 200 us; the launch traced here: 199 us
  waiting for transfers between devices  82.9 us (41%)
  Pallas kernels  54.8 us (27%)
  starting transfers between devices  35 us (18%)
  local copies, waits for them, and re-layouts  19.9 us (10%)
  other arithmetic  3.44 us (2%)
  matrix products  2.91 us (1%)
    ppermute x18, waiting for transfers between devices, along_ring(): lax.ppermute(x, 'blk', [(2 * a + c, 2 * b + c) for a, b in hops for c in...  62.5 us
    pallas_call x3, Pallas kernels, gate_up(): pl.pallas_call(functools.partial(gate_up_kernel, len(blocks), len(rides),...  27.1 us
    ppermute x18, waiting for transfers between devices, partner(): lax.ppermute(x, axis, [(i, i ^ distance) for i in range(lax.axis_size(axi...  20.4 us
    unnamed x70, local copies, waits for them, and re-layouts  19 us
    ppermute x18, starting transfers between devices, along_ring(): lax.ppermute(x, 'blk', [(2 * a + c, 2 * b + c) for a, b in hops for c in...  18 us
    pallas_call x3, Pallas kernels, down(): pl.pallas_call(functools.partial(down_kernel, has_total, len(outs), start...  17 us
    ppermute x18, starting transfers between devices, partner(): lax.ppermute(x, axis, [(i, i ^ distance) for i in range(lax.axis_size(axi...  16.9 us
    pallas_call x9, Pallas kernels, pass_on(): pl.pallas_call(functools.partial(pass_on_kernel, shard, len(flows)), in_s...  7.69 us
  transfers between devices with their start and end apart: 36, of which 17 were waited for; matrix products, arithmetic and copies ran while one was open for 0% of the time, Pallas kernels for 20%

commit v1 on v0

--- a/solution.py
+++ b/solution.py
@@ -12,7 +12,7 @@
 HEADS = 128
 KV_HEADS = 8
 CHUNK_UNITS = (8, 10, 8)
-SLOTS = 3
+SLOTS = 4
 VMEM = 38 * 1024 * 1024
 SMALL_VMEM = 8 * 1024 * 1024
 
@@ -33,20 +33,26 @@
         for copy in copies(i, slot):
             copy.start()
 
-    for i in range(min(SLOTS - 1, units)):
+    for i in range(min(2, units)):
         start(i, i)
     prepare()
 
     def step(i, _):
+        slot = lax.rem(i, SLOTS)
+        for copy in copies(i, slot):
+            copy.wait()
+
+        @pl.when(i == 0)
+        def _():
+            for later in range(2, min(SLOTS - 1, units)):
+                start(later, later)
+
         later = i + SLOTS - 1
 
         @pl.when(later < units)
         def _():
             start(later, lax.rem(later, SLOTS))
 
-        slot = lax.rem(i, SLOTS)
-        for copy in copies(i, slot):
-            copy.wait()
         compute(i, slot)
         return 0
 
@@ -59,7 +65,7 @@
     x_ref, held, sems = rest[-3:]
     half = keep_ref.shape[1]
     unit = held.shape[3]
-    parts = place_ref.shape[0] // n_blocks
+    parts = (place_ref.shape[0] - 1) // n_blocks
     rows = blocks[0].shape[0] // parts
 
     def copies(i, slot):
@@ -129,6 +135,7 @@
         out_specs=anywhere,
         out_shape=jax.ShapeDtypeStruct(x.shape, x.dtype),
         input_output_aliases={0: 0},
+        compiler_params=pltpu.CompilerParams(vmem_limit_bytes=SMALL_VMEM),
         cost_estimate=pl.CostEstimate(flops=0, bytes_accessed=0, transcendentals=0),
     )(x, *after)
 
@@ -160,9 +167,13 @@
     )(own, other, *flows, *after)
 
 
-def hidden_kernel(flow_ref, own_ref, other_ref, inverse_ref, *refs):
+def hidden_kernel(n_squares, width, place_ref, flow_ref, own_ref, other_ref, *refs):
+    squares, out_ref, all_ref = refs[:n_squares], refs[-2], refs[-1]
     rows = flow_ref.shape[1]
-    inverse = inverse_ref[...]
+    for i, square in enumerate(squares):
+        all_ref[i * square.shape[0] : (i + 1) * square.shape[0]] = square[...]
+    here = pl.ds(pl.multiple_of(place_ref[place_ref.shape[0] - 1] * rows, rows), rows)
+    inverse = lax.rsqrt(all_ref[here, :] / width + 1e-05)
     gate, up = [
         (
             own_ref[i, -rows:].astype(jnp.float32)
@@ -172,22 +183,25 @@
         * inverse
         for i in range(2)
     ]
-    refs[-1][...] = (gate / (1 + jnp.exp(-gate)) * up).astype(jnp.bfloat16)
-
-
-def hidden_units(flow, own, other, inverse, after):
+    out_ref[...] = (gate / (1 + jnp.exp(-gate)) * up).astype(jnp.bfloat16)
+
+
+def hidden_units(place, flow, own, other, squares, after):
     _, rows, cols = flow.shape
     vmem = pl.BlockSpec(memory_space=pltpu.VMEM)
     return pl.pallas_call(
-        hidden_kernel,
-        in_specs=[vmem] * 4 + [pl.BlockSpec(memory_space=pl.ANY)] * len(after),
+        functools.partial(hidden_kernel, len(squares), D),
+        in_specs=[pl.BlockSpec(memory_space=pltpu.SMEM)]
+        + [vmem] * (3 + len(squares))
+        + [pl.BlockSpec(memory_space=pl.ANY)] * len(after),
         out_specs=vmem,
         out_shape=jax.ShapeDtypeStruct((rows, cols), jnp.bfloat16),
+        scratch_shapes=[pltpu.VMEM((len(squares) * squares[0].shape[0], 1), jnp.float32)],
         compiler_params=pltpu.CompilerParams(vmem_limit_bytes=SMALL_VMEM),
         cost_estimate=pl.CostEstimate(
             flops=16 * rows * cols, bytes_accessed=14 * rows * cols, transcendentals=rows * cols
         ),
-    )(flow, own, other, inverse, *after)
+    )(place, flow, own, other, *squares, *after)
 
 
 def join_kernel(n_shards, *refs):
@@ -236,7 +250,7 @@
 
     stream(units, copies, prepare, compute)
     if is_last:
-        parts = place_ref.shape[0] // n_outs
+        parts = (place_ref.shape[0] - 1) // n_outs
         for i in range(n_outs * parts):
             out_ref = outs[i // parts]
             rows = out_ref.shape[0] // parts
@@ -353,14 +367,13 @@
     chip, core = lax.axis_index("blk") // 2, lax.axis_index("blk") % 2
     rows = residual_in.shape[0]
     parts = 2 * chips // groups
-    shard_rows = rows // parts
 
     wide = attend(residual_in, queries, key_cache, value_cache, key_new, value_new, lengths)
 
     tokens = (wide * ffn_gain.astype(jnp.float32)[None, :]).astype(jnp.bfloat16)
     blocks = [tokens] + [partner(tokens, "grp", i) for i in range(1, groups)]
 
-    squares = jnp.sum(wide * wide, axis=1)
+    squares = jnp.sum(wide * wide, axis=1, keepdims=True)
     for bit_number in range(lax.axis_size("blk").bit_length() - 1):
         squares = squares + partner(squares, "blk", 1 << bit_number)
 
@@ -368,40 +381,40 @@
     shard = jnp.arange(groups * parts, dtype=jnp.int32) ^ (group * parts)
     place = (spot - 1 - shard) % chips + jnp.where(shard // chips == core, 0, chips)
     own_shard = (core * chips + spot) ^ (group * parts)
+    place = jnp.concatenate([place, own_shard[None]]).astype(jnp.int32)
 
     unit = gate_weight.shape[1] // sum(CHUNK_UNITS)
     edges = [sum(CHUNK_UNITS[:i]) for i in range(len(CHUNK_UNITS) + 1)]
     f32 = jnp.float32
     n_chunks = len(CHUNK_UNITS)
-    inverse, total = None, None
+    total = None
     chunks = [{} for _ in range(n_chunks)]
     last = []
 
-    order = [0, 2 * chips, 2 * chips - 1, *range(chips, 0, -1)]
+    flowing = [0, 2 * chips, 2 * chips - 1, chips, None, *range(chips - 1, 0, -1)]
+    closing = [2 * chips, None, 2 * chips - 1]
     for turn in range(n_chunks + 2 * chips):
-        for stage in order:
-            k = turn - stage
-            if stage == chips - 1:
+        for stage in flowing if turn < n_chunks + chips else closing:
+            if stage is None:
                 for j in range(1, chips - 1):
                     if 0 <= turn - chips - j < n_chunks:
                         last = last + [chunks[turn - chips - j]["hidden"][j]]
                 if turn == 1:
                     last = last + squares
-                    squares = jnp.stack(squares).reshape(groups * parts, shard_rows)
-                    squares = lax.dynamic_index_in_dim(squares, own_shard, 0, keepdims=False)
-                    inverse = lax.rsqrt(squares / D + 1e-05)[:, None]
+                continue
+            k = turn - stage
             if not 0 <= k < n_chunks:
                 continue
             units, chunk = CHUNK_UNITS[k], chunks[k]
             if stage == 0:
-                ride = squares[None, :] if k == 0 else None
+                ride = squares if k == 0 else None
                 keep, send, *rides = gate_up(
                     place, blocks, gate_weight, up_weight, unit, edges[k], units, last, ride
                 )
                 last = [keep]
                 chunk.update(own=keep, flow=None)
                 if k == 0:
-                    squares = rides[0][0]
+                    squares = rides[0]
                     squares = [squares] + [partner(squares, "grp", i) for i in range(1, groups)]
             elif stage < chips:
                 flow = pass_on(
@@ -410,7 +423,9 @@
                 last = [flow]
                 chunk["flow"] = along_ring(flow)
             elif stage == chips:
-                hidden = hidden_units(chunk["flow"], chunk["own"], chunk["other"], inverse, last)
+                hidden = hidden_units(
+                    place, chunk["flow"], chunk["own"], chunk["other"], squares, last
+                )
                 last = [hidden]
                 chunk["hidden"] = [hidden]
                 for _ in range(1, chips):

time: 200 us -> 176 us (0.88)
  local copies, waits for them, and re-layouts: 19.9 us -> 2.49 us
  starting transfers between devices: 35 us -> 45.4 us
  waiting for transfers between devices: 82.9 us -> 74.4 us
  Pallas kernels: 54.8 us -> 46.6 us
    unnamed x70 -> x12, local copies, waits for them, and re-layouts: 19 us -> 1.67 us
    ppermute x18, starting transfers between devices: 18 us -> 28 us  [along_ring(): lax.ppermute(x, 'blk', [(2 * a + c, 2 * b + c) for a, b in hops for c in...]
    ppermute x18, waiting for transfers between devices: 62.5 us -> 53.7 us  [along_ring(): lax.ppermute(x, 'blk', [(2 * a + c, 2 * b + c) for a, b in hops for c in...]
    pallas_call x9, Pallas kernels: 7.69 us -> 0.84 us  [pass_on(): pl.pallas_call(functools.partial(pass_on_kernel, shard, len(flows)), in_s...]
  transfers between devices with their start and end apart: 36 -> 36, of which waited for: 17 -> 19; matrix products, arithmetic and copies ran while one was open for 0% -> 0% of each run, Pallas kernels for 20% -> 18%
where the time goes in v1:
time: 176 us
  waiting for transfers between devices  74.4 us (42%)
  Pallas kernels  46.6 us (26%)
  starting transfers between devices  45.4 us (26%)
  other arithmetic  3.5 us (2%)
  matrix products  2.91 us (2%)
  local copies, waits for them, and re-layouts  2.49 us (1%)
    ppermute x18, waiting for transfers between devices, along_ring(): lax.ppermute(x, 'blk', [(2 * a + c, 2 * b + c) for a, b in hops for c in...  53.7 us
    ppermute x18, starting transfers between devices, along_ring(): lax.ppermute(x, 'blk', [(2 * a + c, 2 * b + c) for a, b in hops for c in...  28 us
    pallas_call x3, Pallas kernels, gate_up(): pl.pallas_call(functools.partial(gate_up_kernel, len(blocks), len(rides),...  26.2 us
    ppermute x18, waiting for transfers between devices, partner(): lax.ppermute(x, axis, [(i, i ^ distance) for i in range(lax.axis_size(axi...  20.7 us
    ppermute x18, starting transfers between devices, partner(): lax.ppermute(x, axis, [(i, i ^ distance) for i in range(lax.axis_size(axi...  17.5 us
    pallas_call x3, Pallas kernels, down(): pl.pallas_call(functools.partial(down_kernel, has_total, len(outs), start...  17.1 us
  transfers between devices with their start and end apart: 36, of which 19 were waited for; matrix products, arithmetic and copies ran while one was open for 0% of the time, Pallas kernels for 18%

profile of v1, /device:TPU:0, one launch (start us, length us, event | category | flops | bytes accessed | tf_op | source)
XLA Modules:
  0.0 175.8 jit_solution(13453403831620709594)
XLA Ops:
  0.0 1.6 copy-done
  1.7 0.8 iota_compare_fusion
  2.5 0.7 dynamic-slice_bitcast_fusion.1
  3.2 0.2 fusion.7
  3.5 2.0 %select_reduce_fusion = (f32[64,16]{1,0:T(8,128)S(1)}, f32[64,16,64]{2,1,0:T(8,128)S(1)}) fusion(pred[64,64]{1,0:T(8,128)(4,1)S(1)} %iota_compare_fusion, bf16[64,16,128]{2,1,0:T(8,128)(2,1)S(1)} %bitcast.31, bf16[64,1,64,128]{3,2,1,0:T(8,128)(2,1)} %param.13), kind=kOutput, calls=%fused_computation.10 | convolution fusion | flops 16972800 | bytes 1581056 | tf_op jit(solution)/shard_map/shd,spd->shp/dot_general | solution.py:318
  5.5 0.4 fusion.3
  5.9 0.7 dynamic-slice_convert_fusion
  6.6 0.7 fusion
  7.3 0.3 multiply_reduce_fusion
  7.6 3.0 %collective-permute-start = (bf16[64,2048]{1,0:T(8,128)(2,1)S(1)}, bf16[64,2048]{1,0:T(8,128)(2,1)S(1)}, u32[]{:S(2)}, u32[]{:S(2)}) collective-permute-start(bf16[64,2048]{1,0:T(8,128)(2,1)S(1)} %get-tuple-element.30.refs_0_), channel_id=1, source_target_pairs={{0,8},{8,0},{16,24},{24,16},{1,9},{9,1},{17,25},{25,17},{2,10},{10... | collective-permute-start | bytes 786440 | tf_op jit(solution)/shard_map/ppermute | solution.py:21
  10.6 1.5 collective-permute-start.1
  12.4 1.1 collective-permute-done.3
  13.5 2.0 %collective-permute-start.4 = (f32[64,1]{1,0:T(8,128)S(1)}, f32[64,1]{1,0:T(8,128)S(1)}, u32[]{:S(2)}, u32[]{:S(2)}) collective-permute-start(f32[64,1]{1,0:T(8,128)S(1)} %add.85), channel_id=1, source_target_pairs={{0,2},{1,3},{2,0},{3,1},{4,6},{5,7},{6,4},{7,5},{8,10},{9,11},{10,... | collective-permute-start | bytes 776 | tf_op jit(solution)/shard_map/ppermute | solution.py:21
  15.5 1.9 %collective-permute-done.4 = f32[64,1]{1,0:T(8,128)S(1)} collective-permute-done((f32[64,1]{1,0:T(8,128)S(1)}, f32[64,1]{1,0:T(8,128)S(1)}, u32[]{:S(2)}, u32[]{:S(2)}) %collective-permute-start.4) | collective-permute-done | bytes 288 | tf_op jit(solution)/shard_map/ppermute | solution.py:21
  17.4 3.0 %collective-permute-start.5 = (f32[64,1]{1,0:T(8,128)S(1)}, f32[64,1]{1,0:T(8,128)S(1)}, u32[]{:S(2)}, u32[]{:S(2)}) collective-permute-start(f32[64,1]{1,0:T(8,128)S(1)} %add.86), channel_id=1, source_target_pairs={{0,4},{1,5},{2,6},{3,7},{4,0},{5,1},{6,2},{7,3},{8,12},{9,13},{10,... | collective-permute-start | bytes 776 | tf_op jit(solution)/shard_map/ppermute | solution.py:21
  20.5 1.9 %collective-permute-done.5 = f32[64,1]{1,0:T(8,128)S(1)} collective-permute-done((f32[64,1]{1,0:T(8,128)S(1)}, f32[64,1]{1,0:T(8,128)S(1)}, u32[]{:S(2)}, u32[]{:S(2)}) %collective-permute-start.5) | collective-permute-done | bytes 288 | tf_op jit(solution)/shard_map/ppermute | solution.py:21
  22.4 1.6 collective-permute-done.1.refs_2_
  24.0 8.3 %shard_map.109 = (bf16[2,128,2048]{2,1,0:T(8,128)(2,1)S(1)}, bf16[2,128,2048]{2,1,0:T(8,128)(2,1)S(1)}, f32[64,1]{1,0:T(8,128)S(1)}) custom-call(s32[9]{0:T(128)S(1)} %pad_add_fusion.place_ref, bf16[64,2048]{1,0:T(8,128)(2,1)S(1)} %get-tuple-element.30.refs_0_, bf16[64,2048]{1,0:T(8,128)(2,1)S(1)} %collective-permute-done.refs_1_, ...), custom_call_target="tpu_custom_call" | custom-call | flops 4294967296 | bytes 19922944 | tf_op jit(solution)/shard_map/pallas_call | solution.py:102
  32.4 1.3 collective-permute-start.7
  33.7 0.8 collective-permute-start.8
  34.5 1.4 collective-permute-start.9
  35.9 9.7 %shard_map.110 = (bf16[2,128,2560]{2,1,0:T(8,128)(2,1)S(1)}, bf16[2,128,2560]{2,1,0:T(8,128)(2,1)S(1)}) custom-call(s32[9]{0:T(128)S(1)} %pad_add_fusion.place_ref, bf16[64,2048]{1,0:T(8,128)(2,1)S(1)} %get-tuple-element.30.refs_0_, bf16[64,2048]{1,0:T(8,128)(2,1)S(1)} %collective-permute-done.refs_1_, bf16[64,2048]{1,0:T(8,128)(2,1)S(1)} %collective-permute-done.1.refs_2_, ...), custom_call_target="tpu_custom_call" | custom-call | flops 5368709120 | bytes 24641536 | tf_op jit(solution)/shard_map/pallas_call | solution.py:102
  45.8 1.6 collective-permute-start.11
  47.4 8.2 %shard_map.113 = (bf16[2,128,2048]{2,1,0:T(8,128)(2,1)S(1)}, bf16[2,128,2048]{2,1,0:T(8,128)(2,1)S(1)}) custom-call(s32[9]{0:T(128)S(1)} %pad_add_fusion.place_ref, bf16[64,2048]{1,0:T(8,128)(2,1)S(1)} %get-tuple-element.30.refs_0_, bf16[64,2048]{1,0:T(8,128)(2,1)S(1)} %collective-permute-done.refs_1_, bf16[64,2048]{1,0:T(8,128)(2,1)S(1)} %collective-permute-done.1.refs_2_, ...), custom_call_target="tpu_custom_call" | custom-call | flops 4294967296 | bytes 19922944 | tf_op jit(solution)/shard_map/pallas_call | solution.py:102
  56.1 2.6 %collective-permute-start.13 = (bf16[2,32,2560]{2,1,0:T(8,128)(2,1)S(1)}, bf16[2,32,2560]{2,1,0:T(8,128)(2,1)S(1)}, u32[]{:S(2)}, u32[]{:S(2)}) collective-permute-start(bf16[2,32,2560]{2,1,0:T(8,128)(2,1)S(1)} %shard_map.115.refs_1_), channel_id=1, source_target_pairs={{0,2},{1,3},{2,6},{3,7},{6,4},{7,5},{4,0},{5,1},{8,10},{9,11},{10,... | collective-permute-start | bytes 983048 | tf_op jit(solution)/shard_map/ppermute | solution.py:28
  58.7 1.2 collective-permute-start.14
  59.9 12.7 %collective-permute-done.14.refs_0_ = bf16[2,32,2048]{2,1,0:T(8,128)(2,1)S(1)} collective-permute-done((bf16[2,32,2048]{2,1,0:T(8,128)(2,1)S(1)}, bf16[2,32,2048]{2,1,0:T(8,128)(2,1)S(1)}, u32[]{:S(2)}, u32[]{:S(2)}) %collective-permute-start.14) | collective-permute-done | bytes 262176 | tf_op jit(solution)/shard_map/ppermute | solution.py:28
  72.8 1.7 collective-permute-start.16
  74.6 2.2 %collective-permute-start.17 = (bf16[2,32,2048]{2,1,0:T(8,128)(2,1)S(1)}, bf16[2,32,2048]{2,1,0:T(8,128)(2,1)S(1)}, u32[]{:S(2)}, u32[]{:S(2)}) collective-permute-start(bf16[2,32,2048]{2,1,0:T(8,128)(2,1)S(1)} %shard_map.117.refs_1_), channel_id=1, source_target_pairs={{0,2},{1,3},{2,6},{3,7},{6,4},{7,5},{4,0},{5,1},{8,10},{9,11},{10,... | collective-permute-start | bytes 786440 | tf_op jit(solution)/shard_map/ppermute | solution.py:28
  77.0 13.1 %collective-permute-done.17.flow_ref = bf16[2,32,2048]{2,1,0:T(8,128)(2,1)S(1)} collective-permute-done((bf16[2,32,2048]{2,1,0:T(8,128)(2,1)S(1)}, bf16[2,32,2048]{2,1,0:T(8,128)(2,1)S(1)}, u32[]{:S(2)}, u32[]{:S(2)}) %collective-permute-start.17) | collective-permute-done | bytes 262176 | tf_op jit(solution)/shard_map/ppermute | solution.py:28
  90.0 0.8 shard_map.120.refs_1_.refs_3_
  91.0 0.8 collective-permute-start.19
  91.8 3.9 %collective-permute-done.15.refs_0_ = bf16[2,32,2048]{2,1,0:T(8,128)(2,1)S(1)} collective-permute-done((bf16[2,32,2048]{2,1,0:T(8,128)(2,1)S(1)}, bf16[2,32,2048]{2,1,0:T(8,128)(2,1)S(1)}, u32[]{:S(2)}, u32[]{:S(2)}) %collective-permute-start.15) | collective-permute-done | bytes 262176 | tf_op jit(solution)/shard_map/ppermute | solution.py:28
  95.8 0.8 collective-permute-start.18
  96.6 3.1 %collective-permute-start.20 = (bf16[32,2048]{1,0:T(8,128)(2,1)S(1)}, bf16[32,2048]{1,0:T(8,128)(2,1)S(1)}, u32[]{:S(2)}, u32[]{:S(2)}) collective-permute-start(bf16[32,2048]{1,0:T(8,128)(2,1)S(1)} %shard_map.120.refs_1_.refs_3_), channel_id=1, source_target_pairs={{0,2},{1,3},{2,6},{3,7},{6,4},{7,5},{4,0},{5,1},{8,10},{9,11},{10,... | collective-permute-start | bytes 393224 | tf_op jit(solution)/shard_map/ppermute | solution.py:28
  99.7 3.0 %collective-permute-done.19.flow_ref = bf16[2,32,2560]{2,1,0:T(8,128)(2,1)S(1)} collective-permute-done((bf16[2,32,2560]{2,1,0:T(8,128)(2,1)S(1)}, bf16[2,32,2560]{2,1,0:T(8,128)(2,1)S(1)}, u32[]{:S(2)}, u32[]{:S(2)}) %collective-permute-start.19) | collective-permute-done | bytes 327712 | tf_op jit(solution)/shard_map/ppermute | solution.py:28
  102.7 0.8 shard_map.123.refs_1_.refs_3_
  103.5 6.1 %collective-permute-done.20.refs_2_.refs_0_ = bf16[32,2048]{1,0:T(8,128)(2,1)S(1)} collective-permute-done((bf16[32,2048]{1,0:T(8,128)(2,1)S(1)}, bf16[32,2048]{1,0:T(8,128)(2,1)S(1)}, u32[]{:S(2)}, u32[]{:S(2)}) %collective-permute-start.20) | collective-permute-done | bytes 131104 | tf_op jit(solution)/shard_map/ppermute | solution.py:28
  109.7 0.8 collective-permute-start.21
  110.6 3.2 %collective-permute-start.25 = (bf16[32,2560]{1,0:T(8,128)(2,1)S(1)}, bf16[32,2560]{1,0:T(8,128)(2,1)S(1)}, u32[]{:S(2)}, u32[]{:S(2)}) collective-permute-start(bf16[32,2560]{1,0:T(8,128)(2,1)S(1)} %shard_map.123.refs_1_.refs_3_), channel_id=1, source_target_pairs={{0,2},{1,3},{2,6},{3,7},{6,4},{7,5},{4,0},{5,1},{8,10},{9,11},{10,... | collective-permute-start | bytes 491528 | tf_op jit(solution)/shard_map/ppermute | solution.py:28
  113.9 8.7 %collective-permute-done.25.refs_5_.refs_0_ = bf16[32,2560]{1,0:T(8,128)(2,1)S(1)} collective-permute-done((bf16[32,2560]{1,0:T(8,128)(2,1)S(1)}, bf16[32,2560]{1,0:T(8,128)(2,1)S(1)}, u32[]{:S(2)}, u32[]{:S(2)}) %collective-permute-start.25) | collective-permute-done | bytes 163872 | tf_op jit(solution)/shard_map/ppermute | solution.py:28
  122.6 0.6 collective-permute-start.26
  123.2 2.2 %collective-permute-done.28.refs_1_.refs_6_ = bf16[32,2048]{1,0:T(8,128)(2,1)S(1)} collective-permute-done((bf16[32,2048]{1,0:T(8,128)(2,1)S(1)}, bf16[32,2048]{1,0:T(8,128)(2,1)S(1)}, u32[]{:S(2)}, u32[]{:S(2)}) %collective-permute-start.28) | collective-permute-done | bytes 131104 | tf_op jit(solution)/shard_map/ppermute | solution.py:28
  125.4 1.2 collective-permute-start.29
  126.6 0.8 shard_map.125.refs_4_.refs_3_
  127.4 2.9 %collective-permute-start.22 = (bf16[32,2048]{1,0:T(8,128)(2,1)S(1)}, bf16[32,2048]{1,0:T(8,128)(2,1)S(1)}, u32[]{:S(2)}, u32[]{:S(2)}) collective-permute-start(bf16[32,2048]{1,0:T(8,128)(2,1)S(1)} %shard_map.125.refs_4_.refs_3_), channel_id=1, source_target_pairs={{0,2},{1,3},{2,6},{3,7},{6,4},{7,5},{4,0},{5,1},{8,10},{9,11},{10,... | collective-permute-start | bytes 393224 | tf_op jit(solution)/shard_map/ppermute | solution.py:28
  130.2 1.4 collective-permute-done.29.refs_2_
  131.6 1.7 collective-permute-done.22.refs_7_.refs_0_
  133.4 2.0 %collective-permute-start.27 = (bf16[32,2560]{1,0:T(8,128)(2,1)S(1)}, bf16[32,2560]{1,0:T(8,128)(2,1)S(1)}, u32[]{:S(2)}, u32[]{:S(2)}) collective-permute-start(bf16[32,2560]{1,0:T(8,128)(2,1)S(1)} %collective-permute-done.26.refs_8_.refs_1_), channel_id=1, source_target_pairs={{0,2},{1,3},{2,6},{3,7},{6,4},{7,5},{4,0},{5,1},{8,10},{9,11},{10,... | collective-permute-start | bytes 491528 | tf_op jit(solution)/shard_map/ppermute | solution.py:28
  135.4 1.9 %collective-permute-start.23 = (bf16[32,2048]{1,0:T(8,128)(2,1)S(1)}, bf16[32,2048]{1,0:T(8,128)(2,1)S(1)}, u32[]{:S(2)}, u32[]{:S(2)}) collective-permute-start(bf16[32,2048]{1,0:T(8,128)(2,1)S(1)} %collective-permute-done.22.refs_7_.refs_0_), channel_id=1, source_target_pairs={{0,2},{1,3},{2,6},{3,7},{6,4},{7,5},{4,0},{5,1},{8,10},{9,11},{10,... | collective-permute-start | bytes 393224 | tf_op jit(solution)/shard_map/ppermute | solution.py:28
  137.3 5.4 %shard_map.127.refs_4_.refs_3_ = f32[256,2048]{1,0:T(8,128)S(1)} custom-call(s32[9]{0:T(128)S(1)} %pad_add_fusion.place_ref, bf16[128,2048]{1,0:T(8,128)(2,1)S(1)} %shard_map.126.refs_0_.refs_3_, bf16[128,2048]{1,0:T(8,128)(2,1)S(1)} %collective-permute-done.30.refs_1_, bf16[6656,2048]{1,0:T(8,128)(2,1)} %refs_2_.5, ...), custom_call_target="tpu_custom_call" | custom-call | flops 2147483648 | bytes 12582912 | tf_op jit(solution)/shard_map/pallas_call | solution.py:271
  142.7 1.0 collective-permute-done.23.refs_5_.refs_1_
  143.8 1.1 collective-permute-start.24
  144.9 1.0 collective-permute-done.31.refs_1_
  145.9 6.2 %shard_map.129.refs_4_.refs_3_ = f32[256,2048]{1,0:T(8,128)S(1)} custom-call(s32[9]{0:T(128)S(1)} %pad_add_fusion.place_ref, bf16[128,2560]{1,0:T(8,128)(2,1)S(1)} %shard_map.128.refs_0_.refs_4_, bf16[128,2560]{1,0:T(8,128)(2,1)S(1)} %collective-permute-done.31.refs_1_, bf16[6656,2048]{1,0:T(8,128)(2,1)} %refs_2_.5, ...), custom_call_target="tpu_custom_call" | custom-call | flops 2684354560 | bytes 14680064 | tf_op jit(solution)/shard_map/pallas_call | solution.py:271
  152.3 1.8 %collective-permute-done.32.refs_1_ = bf16[128,2048]{1,0:T(8,128)(2,1)S(1)} collective-permute-done((bf16[128,2048]{1,0:T(8,128)(2,1)S(1)}, bf16[128,2048]{1,0:T(8,128)(2,1)S(1)}, u32[]{:S(2)}, u32[]{:S(2)}) %collective-permute-start.32) | collective-permute-done | bytes 524320 | tf_op jit(solution)/shard_map/ppermute | solution.py:21
  154.1 5.6 %shard_map.131 = (f32[64,2048]{1,0:T(8,128)S(1)}, bf16[64,2048]{1,0:T(8,128)(2,1)S(1)}, bf16[64,2048]{1,0:T(8,128)(2,1)S(1)}, bf16[64,2048]{1,0:T(8,128)(2,1)S(1)}) custom-call(s32[9]{0:T(128)S(1)} %pad_add_fusion.place_ref, bf16[128,2048]{1,0:T(8,128)(2,1)S(1)} %shard_map.130.refs_0_.refs_4_, bf16[128,2048]{1,0:T(8,128)(2,1)S(1)} %collective-permute-done.32.refs_1_, ...), custom_call_target="tpu_custom_call" | custom-call | flops 2147483648 | bytes 12582912 | tf_op jit(solution)/shard_map/pallas_call | solution.py:271
  159.7 1.3 collective-permute-start.33
  161.0 0.8 collective-permute-start.34
  161.8 1.4 collective-permute-start.35
  163.2 5.7 %collective-permute-done.33 = bf16[64,2048]{1,0:T(8,128)(2,1)S(1)} collective-permute-done((bf16[64,2048]{1,0:T(8,128)(2,1)S(1)}, bf16[64,2048]{1,0:T(8,128)(2,1)S(1)}, u32[]{:S(2)}, u32[]{:S(2)}) %collective-permute-start.33) | collective-permute-done | bytes 262176 | tf_op jit(solution)/shard_map/ppermute | solution.py:21
  168.9 4.1 %collective-permute-done.34 = bf16[64,2048]{1,0:T(8,128)(2,1)S(1)} collective-permute-done((bf16[64,2048]{1,0:T(8,128)(2,1)S(1)}, bf16[64,2048]{1,0:T(8,128)(2,1)S(1)}, u32[]{:S(2)}, u32[]{:S(2)}) %collective-permute-start.34) | collective-permute-done | bytes 262176 | tf_op jit(solution)/shard_map/ppermute | solution.py:21
  173.0 1.6 collective-permute-done.35
  174.7 1.2 convert_add_fusion
  (61 shorter events, 2.3 us)
Async XLA Ops:
  0.0 1.6 copy-start
  1.6 5.0 %copy-start.3 = (bf16[2048]{0:T(1024)(128)(2,1)S(1)}, bf16[2048]{0:T(1024)(128)(2,1)}, u32[]{:S(2)}) copy-start(bf16[2048]{0:T(1024)(128)(2,1)} %param.18) | copy-start | bytes 12292
  1.6 5.0 %copy-start.4 = (bf16[64,1,64,128]{3,2,1,0:T(8,128)(2,1)S(1)}, bf16[64,1,64,128]{3,2,1,0:T(8,128)(2,1)}, u32[]{:S(2)}) copy-start(bf16[64,1,64,128]{3,2,1,0:T(8,128)(2,1)} %param.14) | copy-start | bytes 3145732
  5.4 1.9 %copy-start.2 = (bf16[64,2048]{1,0:T(8,128)(2,1)S(1)}, bf16[64,2048]{1,0:T(8,128)(2,1)}, u32[]{:S(2)}) copy-start(bf16[64,2048]{1,0:T(8,128)(2,1)} %param.11) | copy-start | bytes 786436
  7.6 14.8 %collective-permute-start = (bf16[64,2048]{1,0:T(8,128)(2,1)S(1)}, bf16[64,2048]{1,0:T(8,128)(2,1)S(1)}, u32[]{:S(2)}, u32[]{:S(2)}) collective-permute-start(bf16[64,2048]{1,0:T(8,128)(2,1)S(1)} %get-tuple-element.30.refs_0_), channel_id=1, source_target_pairs={{0,8},{8,0},{16,24},{24,16},{1,9},{9,1},{17,25},{25,17},{2,10},{10... | collective-permute-start | bytes 786440 | tf_op jit(solution)/shard_map/ppermute | solution.py:21
  10.6 13.4 %collective-permute-start.1 = (bf16[64,2048]{1,0:T(8,128)(2,1)S(1)}, bf16[64,2048]{1,0:T(8,128)(2,1)S(1)}, u32[]{:S(2)}, u32[]{:S(2)}) collective-permute-start(bf16[64,2048]{1,0:T(8,128)(2,1)S(1)} %get-tuple-element.30.refs_0_), channel_id=1, source_target_pairs={{0,16},{8,24},{16,0},{24,8},{1,17},{9,25},{17,1},{25,9},{2,18},{10... | collective-permute-start | bytes 786440 | tf_op jit(solution)/shard_map/ppermute | solution.py:21
  12.1 11.9 %collective-permute-start.2 = (bf16[64,2048]{1,0:T(8,128)(2,1)S(1)}, bf16[64,2048]{1,0:T(8,128)(2,1)S(1)}, u32[]{:S(2)}, u32[]{:S(2)}) collective-permute-start(bf16[64,2048]{1,0:T(8,128)(2,1)S(1)} %get-tuple-element.30.refs_0_), channel_id=1, source_target_pairs={{0,24},{8,16},{16,8},{24,0},{1,25},{9,17},{17,9},{25,1},{2,26},{10... | collective-permute-start | bytes 786440 | tf_op jit(solution)/shard_map/ppermute | solution.py:21
  12.2 1.2 collective-permute-start.3
  13.5 3.9 %collective-permute-start.4 = (f32[64,1]{1,0:T(8,128)S(1)}, f32[64,1]{1,0:T(8,128)S(1)}, u32[]{:S(2)}, u32[]{:S(2)}) collective-permute-start(f32[64,1]{1,0:T(8,128)S(1)} %add.85), channel_id=1, source_target_pairs={{0,2},{1,3},{2,0},{3,1},{4,6},{5,7},{6,4},{7,5},{8,10},{9,11},{10,... | collective-permute-start | bytes 776 | tf_op jit(solution)/shard_map/ppermute | solution.py:21
  17.4 5.0 %collective-permute-start.5 = (f32[64,1]{1,0:T(8,128)S(1)}, f32[64,1]{1,0:T(8,128)S(1)}, u32[]{:S(2)}, u32[]{:S(2)}) collective-permute-start(f32[64,1]{1,0:T(8,128)S(1)} %add.86), channel_id=1, source_target_pairs={{0,4},{1,5},{2,6},{3,7},{4,0},{5,1},{6,2},{7,3},{8,12},{9,13},{10,... | collective-permute-start | bytes 776 | tf_op jit(solution)/shard_map/ppermute | solution.py:21
  32.3 13.3 %collective-permute-start.6 = (bf16[2,128,2048]{2,1,0:T(8,128)(2,1)S(1)}, bf16[2,128,2048]{2,1,0:T(8,128)(2,1)S(1)}, u32[]{:S(2)}, u32[]{:S(2)}) collective-permute-start(bf16[2,128,2048]{2,1,0:T(8,128)(2,1)S(1)} %get-tuple-element.16.refs_6_), channel_id=1, source_target_pairs={{0,1},{1,0},{2,3},{3,2},{4,5},{5,4},{6,7},{7,6},{8,9},{9,8},{10,11... | collective-permute-start | bytes 3145736 | tf_op jit(solution)/shard_map/ppermute | solution.py:21
  32.4 13.2 %collective-permute-start.7 = (f32[64,1]{1,0:T(8,128)S(1)}, f32[64,1]{1,0:T(8,128)S(1)}, u32[]{:S(2)}, u32[]{:S(2)}) collective-permute-start(f32[64,1]{1,0:T(8,128)S(1)} %get-tuple-element.20.refs_1_.refs_0_), channel_id=1, source_target_pairs={{0,8},{8,0},{16,24},{24,16},{1,9},{9,1},{17,25},{25,17},{2,10},{10... | collective-permute-start | bytes 776 | tf_op jit(solution)/shard_map/ppermute | solution.py:21
  33.7 11.9 %collective-permute-start.8 = (f32[64,1]{1,0:T(8,128)S(1)}, f32[64,1]{1,0:T(8,128)S(1)}, u32[]{:S(2)}, u32[]{:S(2)}) collective-permute-start(f32[64,1]{1,0:T(8,128)S(1)} %get-tuple-element.20.refs_1_.refs_0_), channel_id=1, source_target_pairs={{0,16},{8,24},{16,0},{24,8},{1,17},{9,25},{17,1},{25,9},{2,18},{10... | collective-permute-start | bytes 776 | tf_op jit(solution)/shard_map/ppermute | solution.py:21
  34.5 11.1 %collective-permute-start.9 = (f32[64,1]{1,0:T(8,128)S(1)}, f32[64,1]{1,0:T(8,128)S(1)}, u32[]{:S(2)}, u32[]{:S(2)}) collective-permute-start(f32[64,1]{1,0:T(8,128)S(1)} %get-tuple-element.20.refs_1_.refs_0_), channel_id=1, source_target_pairs={{0,24},{8,16},{16,8},{24,0},{1,25},{9,17},{17,9},{25,1},{2,26},{10... | collective-permute-start | bytes 776 | tf_op jit(solution)/shard_map/ppermute | solution.py:21
  45.7 10.1 %collective-permute-start.10 = (bf16[2,128,2560]{2,1,0:T(8,128)(2,1)S(1)}, bf16[2,128,2560]{2,1,0:T(8,128)(2,1)S(1)}, u32[]{:S(2)}, u32[]{:S(2)}) collective-permute-start(bf16[2,128,2560]{2,1,0:T(8,128)(2,1)S(1)} %shard_map.112.refs_6_), channel_id=1, source_target_pairs={{0,1},{1,0},{2,3},{3,2},{4,5},{5,4},{6,7},{7,6},{8,9},{9,8},{10,11... | collective-permute-start | bytes 3932168 | tf_op jit(solution)/shard_map/ppermute | solution.py:21
  45.8 9.9 %collective-permute-start.11 = (bf16[2,32,2048]{2,1,0:T(8,128)(2,1)S(1)}, bf16[2,32,2048]{2,1,0:T(8,128)(2,1)S(1)}, u32[]{:S(2)}, u32[]{:S(2)}) collective-permute-start(bf16[2,32,2048]{2,1,0:T(8,128)(2,1)S(1)} %shard_map.111.refs_1_), channel_id=1, source_target_pairs={{0,2},{1,3},{2,6},{3,7},{6,4},{7,5},{4,0},{5,1},{8,10},{9,11},{10,... | collective-permute-start | bytes 786440 | tf_op jit(solution)/shard_map/ppermute | solution.py:28
  55.9 20.9 %collective-permute-start.12 = (bf16[2,128,2048]{2,1,0:T(8,128)(2,1)S(1)}, bf16[2,128,2048]{2,1,0:T(8,128)(2,1)S(1)}, u32[]{:S(2)}, u32[]{:S(2)}) collective-permute-start(bf16[2,128,2048]{2,1,0:T(8,128)(2,1)S(1)} %shard_map.116.refs_1_), channel_id=1, source_target_pairs={{0,1},{1,0},{2,3},{3,2},{4,5},{5,4},{6,7},{7,6},{8,9},{9,8},{10,11... | collective-permute-start | bytes 3145736 | tf_op jit(solution)/shard_map/ppermute | solution.py:21
  56.1 16.6 %collective-permute-start.13 = (bf16[2,32,2560]{2,1,0:T(8,128)(2,1)S(1)}, bf16[2,32,2560]{2,1,0:T(8,128)(2,1)S(1)}, u32[]{:S(2)}, u32[]{:S(2)}) collective-permute-start(bf16[2,32,2560]{2,1,0:T(8,128)(2,1)S(1)} %shard_map.115.refs_1_), channel_id=1, source_target_pairs={{0,2},{1,3},{2,6},{3,7},{6,4},{7,5},{4,0},{5,1},{8,10},{9,11},{10,... | collective-permute-start | bytes 983048 | tf_op jit(solution)/shard_map/ppermute | solution.py:28
  58.7 13.9 %collective-permute-start.14 = (bf16[2,32,2048]{2,1,0:T(8,128)(2,1)S(1)}, bf16[2,32,2048]{2,1,0:T(8,128)(2,1)S(1)}, u32[]{:S(2)}, u32[]{:S(2)}) collective-permute-start(bf16[2,32,2048]{2,1,0:T(8,128)(2,1)S(1)} %shard_map.114.refs_0_), channel_id=1, source_target_pairs={{0,2},{1,3},{2,6},{3,7},{6,4},{7,5},{4,0},{5,1},{8,10},{9,11},{10,... | collective-permute-start | bytes 786440 | tf_op jit(solution)/shard_map/ppermute | solution.py:28
  72.8 18.0 %collective-permute-start.16 = (bf16[2,32,2560]{2,1,0:T(8,128)(2,1)S(1)}, bf16[2,32,2560]{2,1,0:T(8,128)(2,1)S(1)}, u32[]{:S(2)}, u32[]{:S(2)}) collective-permute-start(bf16[2,32,2560]{2,1,0:T(8,128)(2,1)S(1)} %shard_map.118.refs_0_), channel_id=1, source_target_pairs={{0,2},{1,3},{2,6},{3,7},{6,4},{7,5},{4,0},{5,1},{8,10},{9,11},{10,... | collective-permute-start | bytes 983048 | tf_op jit(solution)/shard_map/ppermute | solution.py:28
  74.6 15.5 %collective-permute-start.17 = (bf16[2,32,2048]{2,1,0:T(8,128)(2,1)S(1)}, bf16[2,32,2048]{2,1,0:T(8,128)(2,1)S(1)}, u32[]{:S(2)}, u32[]{:S(2)}) collective-permute-start(bf16[2,32,2048]{2,1,0:T(8,128)(2,1)S(1)} %shard_map.117.refs_1_), channel_id=1, source_target_pairs={{0,2},{1,3},{2,6},{3,7},{6,4},{7,5},{4,0},{5,1},{8,10},{9,11},{10,... | collective-permute-start | bytes 786440 | tf_op jit(solution)/shard_map/ppermute | solution.py:28
  76.8 18.8 %collective-permute-start.15 = (bf16[2,32,2048]{2,1,0:T(8,128)(2,1)S(1)}, bf16[2,32,2048]{2,1,0:T(8,128)(2,1)S(1)}, u32[]{:S(2)}, u32[]{:S(2)}) collective-permute-start(bf16[2,32,2048]{2,1,0:T(8,128)(2,1)S(1)} %shard_map.119.refs_4_), channel_id=1, source_target_pairs={{0,2},{1,3},{2,6},{3,7},{6,4},{7,5},{4,0},{5,1},{8,10},{9,11},{10,... | collective-permute-start | bytes 786440 | tf_op jit(solution)/shard_map/ppermute | solution.py:28
  91.0 11.7 %collective-permute-start.19 = (bf16[2,32,2560]{2,1,0:T(8,128)(2,1)S(1)}, bf16[2,32,2560]{2,1,0:T(8,128)(2,1)S(1)}, u32[]{:S(2)}, u32[]{:S(2)}) collective-permute-start(bf16[2,32,2560]{2,1,0:T(8,128)(2,1)S(1)} %shard_map.121.refs_1_), channel_id=1, source_target_pairs={{0,2},{1,3},{2,6},{3,7},{6,4},{7,5},{4,0},{5,1},{8,10},{9,11},{10,... | collective-permute-start | bytes 983048 | tf_op jit(solution)/shard_map/ppermute | solution.py:28
  95.8 13.9 %collective-permute-start.18 = (bf16[2,32,2048]{2,1,0:T(8,128)(2,1)S(1)}, bf16[2,32,2048]{2,1,0:T(8,128)(2,1)S(1)}, u32[]{:S(2)}, u32[]{:S(2)}) collective-permute-start(bf16[2,32,2048]{2,1,0:T(8,128)(2,1)S(1)} %shard_map.122.refs_4_), channel_id=1, source_target_pairs={{0,2},{1,3},{2,6},{3,7},{6,4},{7,5},{4,0},{5,1},{8,10},{9,11},{10,... | collective-permute-start | bytes 786440 | tf_op jit(solution)/shard_map/ppermute | solution.py:28
  96.6 13.0 %collective-permute-start.20 = (bf16[32,2048]{1,0:T(8,128)(2,1)S(1)}, bf16[32,2048]{1,0:T(8,128)(2,1)S(1)}, u32[]{:S(2)}, u32[]{:S(2)}) collective-permute-start(bf16[32,2048]{1,0:T(8,128)(2,1)S(1)} %shard_map.120.refs_1_.refs_3_), channel_id=1, source_target_pairs={{0,2},{1,3},{2,6},{3,7},{6,4},{7,5},{4,0},{5,1},{8,10},{9,11},{10,... | collective-permute-start | bytes 393224 | tf_op jit(solution)/shard_map/ppermute | solution.py:28
  109.7 16.9 %collective-permute-start.21 = (bf16[2,32,2048]{2,1,0:T(8,128)(2,1)S(1)}, bf16[2,32,2048]{2,1,0:T(8,128)(2,1)S(1)}, u32[]{:S(2)}, u32[]{:S(2)}) collective-permute-start(bf16[2,32,2048]{2,1,0:T(8,128)(2,1)S(1)} %shard_map.124.refs_4_), channel_id=1, source_target_pairs={{0,2},{1,3},{2,6},{3,7},{6,4},{7,5},{4,0},{5,1},{8,10},{9,11},{10,... | collective-permute-start | bytes 786440 | tf_op jit(solution)/shard_map/ppermute | solution.py:28
  110.6 12.0 %collective-permute-start.25 = (bf16[32,2560]{1,0:T(8,128)(2,1)S(1)}, bf16[32,2560]{1,0:T(8,128)(2,1)S(1)}, u32[]{:S(2)}, u32[]{:S(2)}) collective-permute-start(bf16[32,2560]{1,0:T(8,128)(2,1)S(1)} %shard_map.123.refs_1_.refs_3_), channel_id=1, source_target_pairs={{0,2},{1,3},{2,6},{3,7},{6,4},{7,5},{4,0},{5,1},{8,10},{9,11},{10,... | collective-permute-start | bytes 491528 | tf_op jit(solution)/shard_map/ppermute | solution.py:28
  113.8 11.6 %collective-permute-start.28 = (bf16[32,2048]{1,0:T(8,128)(2,1)S(1)}, bf16[32,2048]{1,0:T(8,128)(2,1)S(1)}, u32[]{:S(2)}, u32[]{:S(2)}) collective-permute-start(bf16[32,2048]{1,0:T(8,128)(2,1)S(1)} %collective-permute-done.20.refs_2_.refs_0_), channel_id=1, source_target_pairs={{0,2},{1,3},{2,6},{3,7},{6,4},{7,5},{4,0},{5,1},{8,10},{9,11},{10,... | collective-permute-start | bytes 393224 | tf_op jit(solution)/shard_map/ppermute | solution.py:28
  122.6 9.0 %collective-permute-start.26 = (bf16[32,2560]{1,0:T(8,128)(2,1)S(1)}, bf16[32,2560]{1,0:T(8,128)(2,1)S(1)}, u32[]{:S(2)}, u32[]{:S(2)}) collective-permute-start(bf16[32,2560]{1,0:T(8,128)(2,1)S(1)} %collective-permute-done.25.refs_5_.refs_0_), channel_id=1, source_target_pairs={{0,2},{1,3},{2,6},{3,7},{6,4},{7,5},{4,0},{5,1},{8,10},{9,11},{10,... | collective-permute-start | bytes 491528 | tf_op jit(solution)/shard_map/ppermute | solution.py:28
  125.4 6.2 %collective-permute-start.29 = (bf16[32,2048]{1,0:T(8,128)(2,1)S(1)}, bf16[32,2048]{1,0:T(8,128)(2,1)S(1)}, u32[]{:S(2)}, u32[]{:S(2)}) collective-permute-start(bf16[32,2048]{1,0:T(8,128)(2,1)S(1)} %collective-permute-done.28.refs_1_.refs_6_), channel_id=1, source_target_pairs={{0,2},{1,3},{2,6},{3,7},{6,4},{7,5},{4,0},{5,1},{8,10},{9,11},{10,... | collective-permute-start | bytes 393224 | tf_op jit(solution)/shard_map/ppermute | solution.py:28
  127.4 5.9 %collective-permute-start.22 = (bf16[32,2048]{1,0:T(8,128)(2,1)S(1)}, bf16[32,2048]{1,0:T(8,128)(2,1)S(1)}, u32[]{:S(2)}, u32[]{:S(2)}) collective-permute-start(bf16[32,2048]{1,0:T(8,128)(2,1)S(1)} %shard_map.125.refs_4_.refs_3_), channel_id=1, source_target_pairs={{0,2},{1,3},{2,6},{3,7},{6,4},{7,5},{4,0},{5,1},{8,10},{9,11},{10,... | collective-permute-start | bytes 393224 | tf_op jit(solution)/shard_map/ppermute | solution.py:28
  133.3 4.0 %collective-permute-start.30 = (bf16[128,2048]{1,0:T(8,128)(2,1)S(1)}, bf16[128,2048]{1,0:T(8,128)(2,1)S(1)}, u32[]{:S(2)}, u32[]{:S(2)}) collective-permute-start(bf16[128,2048]{1,0:T(8,128)(2,1)S(1)} %shard_map.126.refs_0_.refs_3_), channel_id=1, source_target_pairs={{0,1},{1,0},{2,3},{3,2},{4,5},{5,4},{6,7},{7,6},{8,9},{9,8},{10,11... | collective-permute-start | bytes 1572872 | tf_op jit(solution)/shard_map/ppermute | solution.py:21
  133.4 9.3 %collective-permute-start.27 = (bf16[32,2560]{1,0:T(8,128)(2,1)S(1)}, bf16[32,2560]{1,0:T(8,128)(2,1)S(1)}, u32[]{:S(2)}, u32[]{:S(2)}) collective-permute-start(bf16[32,2560]{1,0:T(8,128)(2,1)S(1)} %collective-permute-done.26.refs_8_.refs_1_), channel_id=1, source_target_pairs={{0,2},{1,3},{2,6},{3,7},{6,4},{7,5},{4,0},{5,1},{8,10},{9,11},{10,... | collective-permute-start | bytes 491528 | tf_op jit(solution)/shard_map/ppermute | solution.py:28
  135.4 8.4 %collective-permute-start.23 = (bf16[32,2048]{1,0:T(8,128)(2,1)S(1)}, bf16[32,2048]{1,0:T(8,128)(2,1)S(1)}, u32[]{:S(2)}, u32[]{:S(2)}) collective-permute-start(bf16[32,2048]{1,0:T(8,128)(2,1)S(1)} %collective-permute-done.22.refs_7_.refs_0_), channel_id=1, source_target_pairs={{0,2},{1,3},{2,6},{3,7},{6,4},{7,5},{4,0},{5,1},{8,10},{9,11},{10,... | collective-permute-start | bytes 393224 | tf_op jit(solution)/shard_map/ppermute | solution.py:28
  143.8 2.2 %collective-permute-start.31 = (bf16[128,2560]{1,0:T(8,128)(2,1)S(1)}, bf16[128,2560]{1,0:T(8,128)(2,1)S(1)}, u32[]{:S(2)}, u32[]{:S(2)}) collective-permute-start(bf16[128,2560]{1,0:T(8,128)(2,1)S(1)} %shard_map.128.refs_0_.refs_4_), channel_id=1, source_target_pairs={{0,1},{1,0},{2,3},{3,2},{4,5},{5,4},{6,7},{7,6},{8,9},{9,8},{10,11... | collective-permute-start | bytes 1966088 | tf_op jit(solution)/shard_map/ppermute | solution.py:21
  143.8 8.3 %collective-permute-start.24 = (bf16[32,2048]{1,0:T(8,128)(2,1)S(1)}, bf16[32,2048]{1,0:T(8,128)(2,1)S(1)}, u32[]{:S(2)}, u32[]{:S(2)}) collective-permute-start(bf16[32,2048]{1,0:T(8,128)(2,1)S(1)} %collective-permute-done.23.refs_5_.refs_1_), channel_id=1, source_target_pairs={{0,2},{1,3},{2,6},{3,7},{6,4},{7,5},{4,0},{5,1},{8,10},{9,11},{10,... | collective-permute-start | bytes 393224 | tf_op jit(solution)/shard_map/ppermute | solution.py:28
  152.1 2.0 %collective-permute-start.32 = (bf16[128,2048]{1,0:T(8,128)(2,1)S(1)}, bf16[128,2048]{1,0:T(8,128)(2,1)S(1)}, u32[]{:S(2)}, u32[]{:S(2)}) collective-permute-start(bf16[128,2048]{1,0:T(8,128)(2,1)S(1)} %shard_map.130.refs_0_.refs_4_), channel_id=1, source_target_pairs={{0,1},{1,0},{2,3},{3,2},{4,5},{5,4},{6,7},{7,6},{8,9},{9,8},{10,11... | collective-permute-start | bytes 1572872 | tf_op jit(solution)/shard_map/ppermute | solution.py:21
  154.1 21.7 %copy-start.1 = (bf16[64,16384]{1,0:T(8,128)(2,1)S(1)}, bf16[64,16384]{1,0:T(8,128)(2,1)}, u32[]{:S(2)}) copy-start(bf16[64,16384]{1,0:T(8,128)(2,1)} %param.12) | copy-start | bytes 6291460
  159.7 9.2 %collective-permute-start.33 = (bf16[64,2048]{1,0:T(8,128)(2,1)S(1)}, bf16[64,2048]{1,0:T(8,128)(2,1)S(1)}, u32[]{:S(2)}, u32[]{:S(2)}) collective-permute-start(bf16[64,2048]{1,0:T(8,128)(2,1)S(1)} %get-tuple-element.24), channel_id=1, source_target_pairs={{0,8},{8,0},{16,24},{24,16},{1,9},{9,1},{17,25},{25,17},{2,10},{10... | collective-permute-start | bytes 786440 | tf_op jit(solution)/shard_map/ppermute | solution.py:21
  161.0 12.1 %collective-permute-start.34 = (bf16[64,2048]{1,0:T(8,128)(2,1)S(1)}, bf16[64,2048]{1,0:T(8,128)(2,1)S(1)}, u32[]{:S(2)}, u32[]{:S(2)}) collective-permute-start(bf16[64,2048]{1,0:T(8,128)(2,1)S(1)} %get-tuple-element.25), channel_id=1, source_target_pairs={{0,16},{8,24},{16,0},{24,8},{1,17},{9,25},{17,1},{25,9},{2,18},{10... | collective-permute-start | bytes 786440 | tf_op jit(solution)/shard_map/ppermute | solution.py:21
  161.8 12.9 %collective-permute-start.35 = (bf16[64,2048]{1,0:T(8,128)(2,1)S(1)}, bf16[64,2048]{1,0:T(8,128)(2,1)S(1)}, u32[]{:S(2)}, u32[]{:S(2)}) collective-permute-start(bf16[64,2048]{1,0:T(8,128)(2,1)S(1)} %get-tuple-element.26), channel_id=1, source_target_pairs={{0,24},{8,16},{16,8},{24,0},{1,25},{9,17},{17,9},{25,1},{2,26},{10... | collective-permute-start | bytes 786440 | tf_op jit(solution)/shard_map/ppermute | solution.py:21

commit v2 on v1

--- a/solution.py
+++ b/solution.py
@@ -11,8 +11,10 @@
 D = 16384
 HEADS = 128
 KV_HEADS = 8
-CHUNK_UNITS = (8, 10, 8)
+CHUNK_UNITS = (8, 12, 6)
 SLOTS = 4
+READY = 2
+READY_DOWN = 1
 VMEM = 38 * 1024 * 1024
 SMALL_VMEM = 8 * 1024 * 1024
 
@@ -28,45 +30,96 @@
     return lax.ppermute(x, "blk", [(2 * a + c, 2 * b + c) for a, b in hops for c in range(2)])
 
 
-def stream(units, copies, prepare, compute):
+def stream(units, ready, copies, ahead, prepare, compute):
+    ready = min(ready, units)
+    streamed = units - ready
+
     def start(i, slot):
-        for copy in copies(i, slot):
+        for copy in copies(ready + i, slot):
             copy.start()
 
-    for i in range(min(2, units)):
+    for i in range(min(2, streamed)):
         start(i, i)
     prepare()
+    for i in range(ready):
+        compute(i, None)
 
     def step(i, _):
         slot = lax.rem(i, SLOTS)
-        for copy in copies(i, slot):
+        for copy in copies(ready + i, slot):
             copy.wait()
 
         @pl.when(i == 0)
         def _():
-            for later in range(2, min(SLOTS - 1, units)):
+            for later in range(2, min(SLOTS - 1, streamed)):
                 start(later, later)
 
         later = i + SLOTS - 1
 
-        @pl.when(later < units)
+        @pl.when(later < streamed)
         def _():
             start(later, lax.rem(later, SLOTS))
 
-        compute(i, slot)
+        @pl.when(i == max(streamed - SLOTS + 1, 0))
+        def _():
+            for copy in ahead:
+                copy.start()
+
+        compute(ready + i, slot)
         return 0
 
-    lax.fori_loop(0, units, step, 0)
-
-
-def gate_up_kernel(n_blocks, has_ride, first_unit, units, place_ref, *refs):
-    blocks, gate_ref, up_ref = refs[:n_blocks], refs[n_blocks], refs[n_blocks + 1]
-    keep_ref, send_ref, *rest = refs[-5 - has_ride :]
-    x_ref, held, sems = rest[-3:]
+    lax.fori_loop(0, streamed, step, 0)
+    for copy in ahead:
+        copy.wait()
+
+
+def bring_kernel(n_weights, first_unit, by_rows, *refs):
+    weights, out_ref, sems = refs[:n_weights], refs[-2], refs[-1]
+    copies = tiles(weights, out_ref, sems, first_unit, by_rows)
+    for copy in copies:
+        copy.start()
+    for copy in copies:
+        copy.wait()
+
+
+def tiles(weights, out_ref, sems, first_unit, by_rows):
+    count, unit = out_ref.shape[0], out_ref.shape[1 if by_rows else 3]
+    copies = []
+    for i in range(count):
+        here = slice((first_unit + i) * unit, (first_unit + i + 1) * unit)
+        for j, weight in enumerate(weights):
+            source = weight.at[here, :] if by_rows else weight.at[:, here]
+            target = out_ref.at[i] if by_rows else out_ref.at[i, j]
+            copies.append(pltpu.make_async_copy(source, target, sems.at[i, j]))
+    return copies
+
+
+def bring(weights, shape, first_unit, by_rows, after):
+    return pl.pallas_call(
+        functools.partial(bring_kernel, len(weights), first_unit, by_rows),
+        in_specs=[pl.BlockSpec(memory_space=pltpu.HBM)] * len(weights)
+        + [pl.BlockSpec(memory_space=pl.ANY)] * len(after),
+        out_specs=pl.BlockSpec(memory_space=pltpu.VMEM),
+        out_shape=jax.ShapeDtypeStruct(shape, jnp.bfloat16),
+        scratch_shapes=[pltpu.SemaphoreType.DMA((shape[0], len(weights)))],
+        compiler_params=pltpu.CompilerParams(vmem_limit_bytes=VMEM),
+        cost_estimate=pl.CostEstimate(
+            flops=0, bytes_accessed=4 * math.prod(shape), transcendentals=0
+        ),
+    )(*weights, *after)
+
+
+def gate_up_kernel(n_blocks, has_ride, has_next, first_unit, units, place_ref, *refs):
+    blocks, (gate_ref, up_ref, ready_ref) = refs[:n_blocks], refs[n_blocks : n_blocks + 3]
+    keep_ref, send_ref, *rest = refs[len(refs) - 6 - has_ride - has_next :]
+    x_ref, held, sems, next_sems = rest[-4:]
     half = keep_ref.shape[1]
     unit = held.shape[3]
     parts = (place_ref.shape[0] - 1) // n_blocks
     rows = blocks[0].shape[0] // parts
+    ahead = []
+    if has_next:
+        ahead = tiles((gate_ref, up_ref), rest[has_ride], next_sems, first_unit + units, False)
 
     def copies(i, slot):
         columns = pl.ds(pl.multiple_of((first_unit + i) * unit, unit), unit)
@@ -77,42 +130,47 @@
 
     def prepare():
         if has_ride:
-            rest[0][...] = refs[n_blocks + 2][...]
+            rest[0][...] = refs[n_blocks + 3][...]
         for i in range(n_blocks * parts):
             to = pl.ds(pl.multiple_of(place_ref[i] * rows, rows), rows)
             x_ref[to, :] = blocks[i // parts][i % parts * rows : (i % parts + 1) * rows, :]
 
     def compute(i, slot):
-        columns = pl.ds(pl.multiple_of(i * unit, unit), unit)
+        columns = pl.ds(i * unit if slot is None else pl.multiple_of(i * unit, unit), unit)
         for j in range(2):
-            y = jnp.dot(x_ref[...], held[slot, j], preferred_element_type=jnp.float32)
+            weight = ready_ref[i, j] if slot is None else held[slot, j]
+            y = jnp.dot(x_ref[...], weight, preferred_element_type=jnp.float32)
             keep_ref[j, :, columns] = y[:half].astype(jnp.bfloat16)
             send_ref[j, :, columns] = y[half:].astype(jnp.bfloat16)
 
-    stream(units, copies, prepare, compute)
-
-
-def gate_up(place, blocks, gate_weight, up_weight, unit, start, units, after, ride=None):
+    stream(units, ready_ref.shape[0], copies, ahead, prepare, compute)
+
+
+def gate_up(
+    place, blocks, gate_weight, up_weight, ready, unit, start, units, after, has_next, ride=None
+):
     rows, depth = blocks[0].shape
     total = rows * len(blocks)
     cols = units * unit
     rides = [] if ride is None else [ride]
     vmem = pl.BlockSpec(memory_space=pltpu.VMEM)
-    anywhere = pl.BlockSpec(memory_space=pl.ANY)
-    return pl.pallas_call(
-        functools.partial(gate_up_kernel, len(blocks), len(rides), start, units),
+    outs = [jax.ShapeDtypeStruct((2, total // 2, cols), jnp.bfloat16)] * 2
+    outs += [jax.ShapeDtypeStruct(r.shape, r.dtype) for r in rides]
+    outs += [jax.ShapeDtypeStruct(ready.shape, ready.dtype)] * has_next
+    return pl.pallas_call(
+        functools.partial(gate_up_kernel, len(blocks), len(rides), has_next, start, units),
         in_specs=[pl.BlockSpec(memory_space=pltpu.SMEM)]
         + [vmem] * len(blocks)
         + [pl.BlockSpec(memory_space=pltpu.HBM)] * 2
-        + [vmem] * len(rides)
-        + [anywhere] * len(after),
-        out_specs=[vmem] * (2 + len(rides)),
-        out_shape=[jax.ShapeDtypeStruct((2, total // 2, cols), jnp.bfloat16)] * 2
-        + [jax.ShapeDtypeStruct(r.shape, r.dtype) for r in rides],
+        + [vmem] * (1 + len(rides))
+        + [pl.BlockSpec(memory_space=pl.ANY)] * len(after),
+        out_specs=[vmem] * len(outs),
+        out_shape=outs,
         scratch_shapes=[
             pltpu.VMEM((total, depth), jnp.bfloat16),
             pltpu.VMEM((SLOTS, 2, depth, unit), jnp.bfloat16),
             pltpu.SemaphoreType.DMA((SLOTS, 2)),
+            pltpu.SemaphoreType.DMA((READY, 2)),
         ],
         compiler_params=pltpu.CompilerParams(vmem_limit_bytes=VMEM),
         cost_estimate=pl.CostEstimate(
@@ -120,7 +178,7 @@
             bytes_accessed=4 * depth * cols + 2 * total * depth + 4 * total * cols,
             transcendentals=0,
         ),
-    )(place, *blocks, gate_weight, up_weight, *rides, *after)
+    )(place, *blocks, gate_weight, up_weight, ready, *rides, *after)
 
 
 def nothing(*refs):
@@ -227,13 +285,14 @@
 
 
 def down_kernel(has_total, n_outs, first_unit, units, place_ref, *refs):
-    ours_ref, theirs_ref, weight_ref = refs[:3]
-    is_last = n_outs > 1
-    x_ref, held, sems, *rest = refs[len(refs) - 3 - is_last :]
-    outs = refs[len(refs) - 3 - is_last - n_outs : len(refs) - 3 - is_last]
+    ours_ref, theirs_ref, weight_ref, ready_ref = refs[:4]
+    is_last = n_outs > 2
+    x_ref, held, sems, next_sems, *rest = refs[len(refs) - 4 - is_last :]
+    outs = refs[len(refs) - 4 - is_last - n_outs : len(refs) - 4 - is_last]
     total_ref = rest[0] if is_last else outs[0]
     half = ours_ref.shape[0]
     unit = held.shape[1]
+    ahead = [] if is_last else tiles((weight_ref,), outs[1], next_sems, first_unit + units, True)
 
     def copies(i, slot):
         here = pl.ds(pl.multiple_of((first_unit + i) * unit, unit), unit)
@@ -242,13 +301,14 @@
     def prepare():
         x_ref[:half] = ours_ref[...]
         x_ref[half:] = theirs_ref[...]
-        total_ref[...] = refs[3][...] if has_total else jnp.zeros_like(total_ref)
+        total_ref[...] = refs[4][...] if has_total else jnp.zeros_like(total_ref)
 
     def compute(i, slot):
-        x = x_ref[:, pl.ds(pl.multiple_of(i * unit, unit), unit)]
-        total_ref[...] += jnp.dot(x, held[slot], preferred_element_type=jnp.float32)
-
-    stream(units, copies, prepare, compute)
+        columns = pl.ds(i * unit if slot is None else pl.multiple_of(i * unit, unit), unit)
+        weight = ready_ref[i] if slot is None else held[slot]
+        total_ref[...] += jnp.dot(x_ref[:, columns], weight, preferred_element_type=jnp.float32)
+
+    stream(units, ready_ref.shape[0], copies, ahead, prepare, compute)
     if is_last:
         parts = (place_ref.shape[0] - 1) // n_outs
         for i in range(n_outs * parts):
@@ -258,20 +318,23 @@
             out_ref[i % parts * rows : (i % parts + 1) * rows, :] = term.astype(out_ref.dtype)
 
 
-def down(place, groups, ours, theirs, weight, total, unit, start, units, after, is_last):
+def down(place, groups, ours, theirs, weight, ready, total, unit, start, units, after, is_last):
     half, cols = ours.shape
     width = weight.shape[1]
     has_total = total is not None
     vmem = pl.BlockSpec(memory_space=pltpu.VMEM)
     rows = 2 * half // groups
-    outs = [jax.ShapeDtypeStruct((2 * half, width), jnp.float32)]
+    outs = [
+        jax.ShapeDtypeStruct((2 * half, width), jnp.float32),
+        jax.ShapeDtypeStruct(ready.shape, ready.dtype),
+    ]
     if is_last:
         outs = [jax.ShapeDtypeStruct((rows, width), jnp.float32)]
         outs += [jax.ShapeDtypeStruct((rows, width), jnp.bfloat16)] * (groups - 1)
     return pl.pallas_call(
         functools.partial(down_kernel, has_total, len(outs), start, units),
         in_specs=[pl.BlockSpec(memory_space=pltpu.SMEM), vmem, vmem]
-        + [pl.BlockSpec(memory_space=pltpu.HBM)]
+        + [pl.BlockSpec(memory_space=pltpu.HBM), vmem]
         + [vmem] * has_total
         + [pl.BlockSpec(memory_space=pl.ANY)] * len(after),
         out_specs=[vmem] * len(outs),
@@ -280,6 +343,7 @@
             pltpu.VMEM((2 * half, cols), jnp.bfloat16),
             pltpu.VMEM((SLOTS, unit, width), jnp.bfloat16),
             pltpu.SemaphoreType.DMA((SLOTS,)),
+            pltpu.SemaphoreType.DMA((READY_DOWN, 1)),
         ]
         + [pltpu.VMEM((2 * half, width), jnp.float32)] * is_last,
         compiler_params=pltpu.CompilerParams(vmem_limit_bytes=VMEM),
@@ -288,7 +352,7 @@
             bytes_accessed=2 * units * unit * width + 16 * half * width,
             transcendentals=0,
         ),
-    )(place, ours, theirs, weight, *([total] if has_total else []), *after)
+    )(place, ours, theirs, weight, ready, *([total] if has_total else []), *after)
 
 
 def attend(residual_in, queries, key_cache, value_cache, key_new, value_new, lengths):
@@ -389,68 +453,72 @@
     n_chunks = len(CHUNK_UNITS)
     total = None
     chunks = [{} for _ in range(n_chunks)]
-    last = []
+    ready = bring((gate_weight, up_weight), (READY, 2, tokens.shape[1], unit), 0, False, [tokens])
+    last = [ready]
+
+    def turn_of(k, stage):
+        return k + stage - (k == 0 and stage > 0)
 
     flowing = [0, 2 * chips, 2 * chips - 1, chips, None, *range(chips - 1, 0, -1)]
     closing = [2 * chips, None, 2 * chips - 1]
     for turn in range(n_chunks + 2 * chips):
+        if turn == n_chunks:
+            shape = (READY_DOWN, 2 * unit, down_weight.shape[1])
+            ready = bring((down_weight,), shape, 0, True, last)
+            last = [ready]
         for stage in flowing if turn < n_chunks + chips else closing:
             if stage is None:
-                for j in range(1, chips - 1):
-                    if 0 <= turn - chips - j < n_chunks:
-                        last = last + [chunks[turn - chips - j]["hidden"][j]]
+                for k in range(n_chunks):
+                    for j in range(1, chips - 1):
+                        if turn_of(k, chips + j) == turn:
+                            last = last + [chunks[k]["hidden"][j]]
                 if turn == 1:
                     last = last + squares
                 continue
-            k = turn - stage
-            if not 0 <= k < n_chunks:
-                continue
-            units, chunk = CHUNK_UNITS[k], chunks[k]
-            if stage == 0:
-                ride = squares if k == 0 else None
-                keep, send, *rides = gate_up(
-                    place, blocks, gate_weight, up_weight, unit, edges[k], units, last, ride
-                )
-                last = [keep]
-                chunk.update(own=keep, flow=None)
-                if k == 0:
-                    squares = rides[0]
-                    squares = [squares] + [partner(squares, "grp", i) for i in range(1, groups)]
-            elif stage < chips:
-                flow = pass_on(
-                    stage - 1, chips, chunk["own"], chunk["other"], chunk["flow"], last
-                )
-                last = [flow]
-                chunk["flow"] = along_ring(flow)
-            elif stage == chips:
-                hidden = hidden_units(
-                    place, chunk["flow"], chunk["own"], chunk["other"], squares, last
-                )
-                last = [hidden]
-                chunk["hidden"] = [hidden]
-                for _ in range(1, chips):
-                    chunk["hidden"].append(along_ring(chunk["hidden"][-1]))
-            elif stage == 2 * chips - 1:
-                ours = join(chunk["hidden"][1:] + chunk["hidden"][:1], last)
-                last = [ours]
-                chunk.update(ours=ours, theirs=partner(ours, "blk", 1))
-            else:
-                total, *terms = down(
-                    place,
-                    groups,
-                    chunk["ours"],
-                    chunk["theirs"],
-                    down_weight,
-                    total,
-                    2 * unit,
-                    edges[k] // 2,
-                    units // 2,
-                    last,
-                    k == n_chunks - 1,
-                )
-                last = [total]
-        if turn < n_chunks:
-            send = hold(send, last) if turn > 0 else send
+            for k in range(n_chunks):
+                if turn_of(k, stage) != turn:
+                    continue
+                units, chunk = CHUNK_UNITS[k], chunks[k]
+                is_last = k == n_chunks - 1
+                if stage == 0:
+                    ride = squares if k == 0 else None
+                    keep, send, *rest = gate_up(
+                        place, blocks, gate_weight, up_weight, ready, unit, edges[k], units, last,
+                        not is_last, ride,
+                    )
+                    ready = rest[-1] if rest else None
+                    last = [keep]
+                    chunk.update(own=keep, flow=None)
+                    if k == 0:
+                        chunk["other"] = partner(send, "blk", 1)
+                        squares = [rest[0]] + [partner(rest[0], "grp", i) for i in range(1, groups)]
+                elif stage < chips:
+                    flow = pass_on(
+                        stage - 1, chips, chunk["own"], chunk["other"], chunk["flow"], last
+                    )
+                    last = [flow]
+                    chunk["flow"] = along_ring(flow)
+                elif stage == chips:
+                    hidden = hidden_units(
+                        place, chunk["flow"], chunk["own"], chunk["other"], squares, last
+                    )
+                    last = [hidden]
+                    chunk["hidden"] = [hidden]
+                    for _ in range(1, chips):
+                        chunk["hidden"].append(along_ring(chunk["hidden"][-1]))
+                elif stage == 2 * chips - 1:
+                    ours = join(chunk["hidden"][1:] + chunk["hidden"][:1], last)
+                    last = [ours]
+                    chunk.update(ours=ours, theirs=partner(ours, "blk", 1))
+                else:
+                    total, *terms = down(
+                        place, groups, chunk["ours"], chunk["theirs"], down_weight, ready, total,
+                        2 * unit, edges[k] // 2, units // 2, last, is_last,
+                    )
+                    ready = terms[0]
+                    last = [total]
+        if 0 < turn < n_chunks:
+            send = hold(send, last)
             last = [send]
             chunks[turn]["other"] = partner(send, "blk", 1)
 

time: 176 us -> 176 us (level)
  starting transfers between devices: 45.4 us -> 38.5 us
  waiting for transfers between devices: 74.4 us -> 79.5 us
    ppermute x18, waiting for transfers between devices: 53.7 us -> 61 us  [along_ring(): lax.ppermute(x, 'blk', [(2 * a + c, 2 * b + c) for a, b in hops for c in...]
    ppermute x18, starting transfers between devices: 28 us -> 21.2 us  [along_ring(): lax.ppermute(x, 'blk', [(2 * a + c, 2 * b + c) for a, b in hops for c in...]
    pallas_call x0 -> x2, Pallas kernels: none -> 3.85 us  [bring(): pl.pallas_call(functools.partial(bring_kernel, len(weights), first_unit,...]
    ppermute x18, waiting for transfers between devices: 20.7 us -> 18.6 us  [partner(): lax.ppermute(x, axis, [(i, i ^ distance) for i in range(lax.axis_size(axi...]
    pallas_call x3, Pallas kernels: 17.1 us -> 15.2 us  [down(): pl.pallas_call(functools.partial(down_kernel, has_total, len(outs), start...]
  transfers between devices with their start and end apart: 36 -> 36, of which waited for: 19 -> 19; matrix products, arithmetic and copies ran while one was open for 0% -> 0% of each run, Pallas kernels for 18% -> 20%
where the time goes in v2:
time: 176 us
  waiting for transfers between devices  79.5 us (45%)
  Pallas kernels  48.2 us (27%)
  starting transfers between devices  38.5 us (22%)
  other arithmetic  3.5 us (2%)
  matrix products  2.91 us (2%)
  local copies, waits for them, and re-layouts  2.49 us (1%)
    ppermute x18, waiting for transfers between devices, along_ring(): lax.ppermute(x, 'blk', [(2 * a + c, 2 * b + c) for a, b in hops for c in...  61 us
    pallas_call x3, Pallas kernels, gate_up(): pl.pallas_call(functools.partial(gate_up_kernel, len(blocks), len(rides),...  25.8 us
    ppermute x18, starting transfers between devices, along_ring(): lax.ppermute(x, 'blk', [(2 * a + c, 2 * b + c) for a, b in hops for c in...  21.2 us
    ppermute x18, waiting for transfers between devices, partner(): lax.ppermute(x, axis, [(i, i ^ distance) for i in range(lax.axis_size(axi...  18.6 us
    ppermute x18, starting transfers between devices, partner(): lax.ppermute(x, axis, [(i, i ^ distance) for i in range(lax.axis_size(axi...  17.3 us
    pallas_call x3, Pallas kernels, down(): pl.pallas_call(functools.partial(down_kernel, has_total, len(outs), start...  15.2 us
    pallas_call x2, Pallas kernels, bring(): pl.pallas_call(functools.partial(bring_kernel, len(weights), first_unit,...  3.85 us
  transfers between devices with their start and end apart: 36, of which 19 were waited for; matrix products, arithmetic and copies ran while one was open for 0% of the time, Pallas kernels for 20%

profile of v2, /device:TPU:0, one launch (start us, length us, event | category | flops | bytes accessed | tf_op | source)
XLA Modules:
  0.0 175.7 jit_solution(11657760979937269508)
XLA Ops:
  0.0 1.6 copy-done
  1.7 0.8 iota_compare_fusion
  2.5 0.7 dynamic-slice_bitcast_fusion.1
  3.2 0.2 fusion.7
  3.5 2.0 %select_reduce_fusion = (f32[64,16]{1,0:T(8,128)S(1)}, f32[64,16,64]{2,1,0:T(8,128)S(1)}) fusion(pred[64,64]{1,0:T(8,128)(4,1)S(1)} %iota_compare_fusion, bf16[64,16,128]{2,1,0:T(8,128)(2,1)S(1)} %bitcast.31, bf16[64,1,64,128]{3,2,1,0:T(8,128)(2,1)} %param.13), kind=kOutput, calls=%fused_computation.10 | convolution fusion | flops 16972800 | bytes 1581056 | tf_op jit(solution)/shard_map/shd,spd->shp/dot_general | solution.py:382
  5.5 0.4 fusion.3
  5.9 0.7 dynamic-slice_convert_fusion
  6.6 0.7 fusion
  7.3 0.3 multiply_reduce_fusion
  7.6 3.0 %collective-permute-start = (bf16[64,2048]{1,0:T(8,128)(2,1)S(1)}, bf16[64,2048]{1,0:T(8,128)(2,1)S(1)}, u32[]{:S(2)}, u32[]{:S(2)}) collective-permute-start(bf16[64,2048]{1,0:T(8,128)(2,1)S(1)} %get-tuple-element.42.refs_2_.refs_0_), channel_id=1, source_target_pairs={{0,8},{8,0},{16,24},{24,16},{1,9},{9,1},{17,25},{25,17},{2,10},{10... | collective-permute-start | bytes 786440 | tf_op jit(solution)/shard_map/ppermute | solution.py:23
  10.6 1.5 collective-permute-start.1
  12.4 1.1 collective-permute-done.3
  13.5 2.0 %collective-permute-start.4 = (f32[64,1]{1,0:T(8,128)S(1)}, f32[64,1]{1,0:T(8,128)S(1)}, u32[]{:S(2)}, u32[]{:S(2)}) collective-permute-start(f32[64,1]{1,0:T(8,128)S(1)} %add.85), channel_id=1, source_target_pairs={{0,2},{1,3},{2,0},{3,1},{4,6},{5,7},{6,4},{7,5},{8,10},{9,11},{10,... | collective-permute-start | bytes 776 | tf_op jit(solution)/shard_map/ppermute | solution.py:23
  15.5 1.9 %collective-permute-done.4 = f32[64,1]{1,0:T(8,128)S(1)} collective-permute-done((f32[64,1]{1,0:T(8,128)S(1)}, f32[64,1]{1,0:T(8,128)S(1)}, u32[]{:S(2)}, u32[]{:S(2)}) %collective-permute-start.4) | collective-permute-done | bytes 288 | tf_op jit(solution)/shard_map/ppermute | solution.py:23
  17.4 3.0 %collective-permute-start.5 = (f32[64,1]{1,0:T(8,128)S(1)}, f32[64,1]{1,0:T(8,128)S(1)}, u32[]{:S(2)}, u32[]{:S(2)}) collective-permute-start(f32[64,1]{1,0:T(8,128)S(1)} %add.86), channel_id=1, source_target_pairs={{0,4},{1,5},{2,6},{3,7},{4,0},{5,1},{6,2},{7,3},{8,12},{9,13},{10,... | collective-permute-start | bytes 776 | tf_op jit(solution)/shard_map/ppermute | solution.py:23
  20.5 2.3 %shard_map.109.refs_6_.refs_8_ = bf16[2,2,2048,256]{3,2,1,0:T(8,128)(2,1)S(1)} custom-call(bf16[2048,6656]{1,0:T(8,128)(2,1)} %refs_4_.5, bf16[2048,6656]{1,0:T(8,128)(2,1)} %refs_5_.5, bf16[64,2048]{1,0:T(8,128)(2,1)S(1)} %get-tuple-element.42.refs_2_.refs_0_), custom_call_target="tpu_custom_call" | custom-call | bytes 8388608 | tf_op jit(solution)/shard_map/pallas_call | solution.py:98
  22.8 1.2 collective-permute-done.1.refs_2_
  24.0 8.3 %shard_map.110 = (bf16[2,128,2048]{2,1,0:T(8,128)(2,1)S(1)}, bf16[2,128,2048]{2,1,0:T(8,128)(2,1)S(1)}, f32[64,1]{1,0:T(8,128)S(1)}, bf16[2,2,2048,256]{3,2,1,0:T(8,128)(2,1)S(1)}) custom-call(s32[9]{0:T(128)S(1)} %pad_add_fusion.place_ref, bf16[64,2048]{1,0:T(8,128)(2,1)S(1)} %get-tuple-element.42.refs_2_.refs_0_, ...), custom_call_target="tpu_custom_call" | custom-call | flops 4294967296 | bytes 19922944 | tf_op jit(solution)/shard_map/pallas_call | solution.py:160
  32.3 1.6 collective-permute-start.10
  33.9 1.5 collective-permute-start.8
  35.4 0.5 collective-permute-start.9
  36.0 1.6 collective-permute-start.7
  37.6 11.0 %shard_map.112 = (bf16[2,128,3072]{2,1,0:T(8,128)(2,1)S(1)}, bf16[2,128,3072]{2,1,0:T(8,128)(2,1)S(1)}, bf16[2,2,2048,256]{3,2,1,0:T(8,128)(2,1)S(1)}) custom-call(s32[9]{0:T(128)S(1)} %pad_add_fusion.place_ref, bf16[64,2048]{1,0:T(8,128)(2,1)S(1)} %get-tuple-element.42.refs_2_.refs_0_, bf16[64,2048]{1,0:T(8,128)(2,1)S(1)} %collective-permute-done.refs_1_, ...), custom_call_target="tpu_custom_call" | custom-call | flops 6442450944 | bytes 29360128 | tf_op jit(solution)/shard_map/pallas_call | solution.py:160
  48.9 2.6 %collective-permute-start.12 = (bf16[2,32,2048]{2,1,0:T(8,128)(2,1)S(1)}, bf16[2,32,2048]{2,1,0:T(8,128)(2,1)S(1)}, u32[]{:S(2)}, u32[]{:S(2)}) collective-permute-start(bf16[2,32,2048]{2,1,0:T(8,128)(2,1)S(1)} %shard_map.113.refs_1_), channel_id=1, source_target_pairs={{0,2},{1,3},{2,6},{3,7},{6,4},{7,5},{4,0},{5,1},{8,10},{9,11},{10,... | collective-permute-start | bytes 786440 | tf_op jit(solution)/shard_map/ppermute | solution.py:30
  51.5 6.5 %shard_map.115 = (bf16[2,128,1536]{2,1,0:T(8,128)(2,1)S(1)}, bf16[2,128,1536]{2,1,0:T(8,128)(2,1)S(1)}) custom-call(s32[9]{0:T(128)S(1)} %pad_add_fusion.place_ref, bf16[64,2048]{1,0:T(8,128)(2,1)S(1)} %get-tuple-element.42.refs_2_.refs_0_, bf16[64,2048]{1,0:T(8,128)(2,1)S(1)} %collective-permute-done.refs_1_, ...), custom_call_target="tpu_custom_call" | custom-call | flops 3221225472 | bytes 15204352 | tf_op jit(solution)/shard_map/pallas_call | solution.py:160
  58.0 0.5 collective-permute-done.12.refs_0_
  58.8 1.7 collective-permute-start.14
  60.5 1.4 collective-permute-start.15
  61.9 1.6 shard_map.119.refs_4_.refs_3_
  63.5 13.3 %collective-permute-done.15.flow_ref = bf16[2,32,2048]{2,1,0:T(8,128)(2,1)S(1)} collective-permute-done((bf16[2,32,2048]{2,1,0:T(8,128)(2,1)S(1)}, bf16[2,32,2048]{2,1,0:T(8,128)(2,1)S(1)}, u32[]{:S(2)}, u32[]{:S(2)}) %collective-permute-start.15) | collective-permute-done | bytes 262176 | tf_op jit(solution)/shard_map/ppermute | solution.py:30
  76.8 0.8 shard_map.120.refs_1_.refs_3_
  77.6 0.1 shard_map.121.refs_0_
  77.8 0.8 collective-permute-start.17
  78.6 2.2 %collective-permute-start.18 = (bf16[32,2048]{1,0:T(8,128)(2,1)S(1)}, bf16[32,2048]{1,0:T(8,128)(2,1)S(1)}, u32[]{:S(2)}, u32[]{:S(2)}) collective-permute-start(bf16[32,2048]{1,0:T(8,128)(2,1)S(1)} %shard_map.120.refs_1_.refs_3_), channel_id=1, source_target_pairs={{0,2},{1,3},{2,6},{3,7},{6,4},{7,5},{4,0},{5,1},{8,10},{9,11},{10,... | collective-permute-start | bytes 393224 | tf_op jit(solution)/shard_map/ppermute | solution.py:30
  80.9 11.3 %collective-permute-done.18.refs_2_.refs_0_ = bf16[32,2048]{1,0:T(8,128)(2,1)S(1)} collective-permute-done((bf16[32,2048]{1,0:T(8,128)(2,1)S(1)}, bf16[32,2048]{1,0:T(8,128)(2,1)S(1)}, u32[]{:S(2)}, u32[]{:S(2)}) %collective-permute-start.18) | collective-permute-done | bytes 131104 | tf_op jit(solution)/shard_map/ppermute | solution.py:30
  92.2 0.1 shard_map.123.refs_1_
  92.4 3.0 %collective-permute-start.16 = (bf16[2,32,1536]{2,1,0:T(8,128)(2,1)S(1)}, bf16[2,32,1536]{2,1,0:T(8,128)(2,1)S(1)}, u32[]{:S(2)}, u32[]{:S(2)}) collective-permute-start(bf16[2,32,1536]{2,1,0:T(8,128)(2,1)S(1)} %shard_map.122.refs_1_), channel_id=1, source_target_pairs={{0,2},{1,3},{2,6},{3,7},{6,4},{7,5},{4,0},{5,1},{8,10},{9,11},{10,... | collective-permute-start | bytes 589832 | tf_op jit(solution)/shard_map/ppermute | solution.py:30
  95.5 13.2 %collective-permute-done.16.refs_0_ = bf16[2,32,1536]{2,1,0:T(8,128)(2,1)S(1)} collective-permute-done((bf16[2,32,1536]{2,1,0:T(8,128)(2,1)S(1)}, bf16[2,32,1536]{2,1,0:T(8,128)(2,1)S(1)}, u32[]{:S(2)}, u32[]{:S(2)}) %collective-permute-start.16) | collective-permute-done | bytes 196640 | tf_op jit(solution)/shard_map/ppermute | solution.py:30
  108.8 2.5 %collective-permute-done.21.refs_2_.refs_1_ = bf16[32,2048]{1,0:T(8,128)(2,1)S(1)} collective-permute-done((bf16[32,2048]{1,0:T(8,128)(2,1)S(1)}, bf16[32,2048]{1,0:T(8,128)(2,1)S(1)}, u32[]{:S(2)}, u32[]{:S(2)}) %collective-permute-start.21) | collective-permute-done | bytes 131104 | tf_op jit(solution)/shard_map/ppermute | solution.py:30
  111.4 0.5 collective-permute-start.23
  111.9 0.9 shard_map.125.refs_1_.refs_3_
  112.8 3.0 %collective-permute-done.19.refs_0_ = bf16[2,32,1536]{2,1,0:T(8,128)(2,1)S(1)} collective-permute-done((bf16[2,32,1536]{2,1,0:T(8,128)(2,1)S(1)}, bf16[2,32,1536]{2,1,0:T(8,128)(2,1)S(1)}, u32[]{:S(2)}, u32[]{:S(2)}) %collective-permute-start.19) | collective-permute-done | bytes 196640 | tf_op jit(solution)/shard_map/ppermute | solution.py:30
  115.8 1.5 collective-permute-done.23.refs_2_
  117.4 3.0 %collective-permute-start.22 = (bf16[2,32,1536]{2,1,0:T(8,128)(2,1)S(1)}, bf16[2,32,1536]{2,1,0:T(8,128)(2,1)S(1)}, u32[]{:S(2)}, u32[]{:S(2)}) collective-permute-start(bf16[2,32,1536]{2,1,0:T(8,128)(2,1)S(1)} %shard_map.126.refs_4_), channel_id=1, source_target_pairs={{0,2},{1,3},{2,6},{3,7},{6,4},{7,5},{4,0},{5,1},{8,10},{9,11},{10,... | collective-permute-start | bytes 589832 | tf_op jit(solution)/shard_map/ppermute | solution.py:30
  120.5 5.6 %collective-permute-done.27.refs_5_.refs_0_ = bf16[32,3072]{1,0:T(8,128)(2,1)S(1)} collective-permute-done((bf16[32,3072]{1,0:T(8,128)(2,1)S(1)}, bf16[32,3072]{1,0:T(8,128)(2,1)S(1)}, u32[]{:S(2)}, u32[]{:S(2)}) %collective-permute-start.27) | collective-permute-done | bytes 196640 | tf_op jit(solution)/shard_map/ppermute | solution.py:30
  126.0 4.2 %collective-permute-done.22.flow_ref = bf16[2,32,1536]{2,1,0:T(8,128)(2,1)S(1)} collective-permute-done((bf16[2,32,1536]{2,1,0:T(8,128)(2,1)S(1)}, bf16[2,32,1536]{2,1,0:T(8,128)(2,1)S(1)}, u32[]{:S(2)}, u32[]{:S(2)}) %collective-permute-start.22) | collective-permute-done | bytes 196640 | tf_op jit(solution)/shard_map/ppermute | solution.py:30
  130.2 0.7 shard_map.128.refs_4_.refs_3_
  131.0 5.5 %collective-permute-done.24.refs_6_.refs_0_ = bf16[32,1536]{1,0:T(8,128)(2,1)S(1)} collective-permute-done((bf16[32,1536]{1,0:T(8,128)(2,1)S(1)}, bf16[32,1536]{1,0:T(8,128)(2,1)S(1)}, u32[]{:S(2)}, u32[]{:S(2)}) %collective-permute-start.24) | collective-permute-done | bytes 98336 | tf_op jit(solution)/shard_map/ppermute | solution.py:30
  136.5 3.0 %collective-permute-start.29 = (bf16[32,3072]{1,0:T(8,128)(2,1)S(1)}, bf16[32,3072]{1,0:T(8,128)(2,1)S(1)}, u32[]{:S(2)}, u32[]{:S(2)}) collective-permute-start(bf16[32,3072]{1,0:T(8,128)(2,1)S(1)} %collective-permute-done.28.refs_1_.refs_5_), channel_id=1, source_target_pairs={{0,2},{1,3},{2,6},{3,7},{6,4},{7,5},{4,0},{5,1},{8,10},{9,11},{10,... | collective-permute-start | bytes 589832 | tf_op jit(solution)/shard_map/ppermute | solution.py:30
  139.6 4.7 %shard_map.129 = (f32[256,2048]{1,0:T(8,128)S(1)}, bf16[1,512,2048]{2,1,0:T(8,128)(2,1)S(1)}) custom-call(s32[9]{0:T(128)S(1)} %pad_add_fusion.place_ref, bf16[128,2048]{1,0:T(8,128)(2,1)S(1)} %shard_map.127.refs_4_.refs_0_, bf16[128,2048]{1,0:T(8,128)(2,1)S(1)} %collective-permute-done.30.refs_1_, bf16[6656,2048]{1,0:T(8,128)(2,1)} %refs_2_.5, ...), custom_call_target="tpu_custom_call" | custom-call | flops 2147483648 | bytes 12582912 | tf_op jit(solution)/shard_map/pallas_call | solution.py:334
  144.2 0.4 collective-permute-done.29.refs_2_
  144.8 0.9 collective-permute-start.26
  145.7 1.4 collective-permute-done.31.refs_1_
  147.1 6.7 %shard_map.131 = (f32[256,2048]{1,0:T(8,128)S(1)}, bf16[1,512,2048]{2,1,0:T(8,128)(2,1)S(1)}) custom-call(s32[9]{0:T(128)S(1)} %pad_add_fusion.place_ref, bf16[128,3072]{1,0:T(8,128)(2,1)S(1)} %shard_map.130.refs_0_.refs_5_, bf16[128,3072]{1,0:T(8,128)(2,1)S(1)} %collective-permute-done.31.refs_1_, bf16[6656,2048]{1,0:T(8,128)(2,1)} %refs_2_.5, ...), custom_call_target="tpu_custom_call" | custom-call | flops 3221225472 | bytes 16777216 | tf_op jit(solution)/shard_map/pallas_call | solution.py:334
  153.9 0.2 collective-permute-start.32
  154.1 1.6 collective-permute-done.32.refs_1_
  155.7 3.8 %shard_map.133 = (f32[64,2048]{1,0:T(8,128)S(1)}, bf16[64,2048]{1,0:T(8,128)(2,1)S(1)}, bf16[64,2048]{1,0:T(8,128)(2,1)S(1)}, bf16[64,2048]{1,0:T(8,128)(2,1)S(1)}) custom-call(s32[9]{0:T(128)S(1)} %pad_add_fusion.place_ref, bf16[128,1536]{1,0:T(8,128)(2,1)S(1)} %shard_map.132.refs_0_.refs_5_, bf16[128,1536]{1,0:T(8,128)(2,1)S(1)} %collective-permute-done.32.refs_1_, ...), custom_call_target="tpu_custom_call" | custom-call | flops 1610612736 | bytes 10485760 | tf_op jit(solution)/shard_map/pallas_call | solution.py:334
  159.5 1.3 collective-permute-start.33
  160.8 0.8 collective-permute-start.34
  161.6 1.4 collective-permute-start.35
  163.0 5.7 %collective-permute-done.33 = bf16[64,2048]{1,0:T(8,128)(2,1)S(1)} collective-permute-done((bf16[64,2048]{1,0:T(8,128)(2,1)S(1)}, bf16[64,2048]{1,0:T(8,128)(2,1)S(1)}, u32[]{:S(2)}, u32[]{:S(2)}) %collective-permute-start.33) | collective-permute-done | bytes 262176 | tf_op jit(solution)/shard_map/ppermute | solution.py:23
  168.7 4.1 %collective-permute-done.34 = bf16[64,2048]{1,0:T(8,128)(2,1)S(1)} collective-permute-done((bf16[64,2048]{1,0:T(8,128)(2,1)S(1)}, bf16[64,2048]{1,0:T(8,128)(2,1)S(1)}, u32[]{:S(2)}, u32[]{:S(2)}) %collective-permute-start.34) | collective-permute-done | bytes 262176 | tf_op jit(solution)/shard_map/ppermute | solution.py:23
  172.8 1.6 collective-permute-done.35
  174.5 1.2 convert_add_fusion
  (63 shorter events, 1.7 us)
Async XLA Ops:
  0.0 1.6 copy-start
  1.6 5.0 %copy-start.3 = (bf16[2048]{0:T(1024)(128)(2,1)S(1)}, bf16[2048]{0:T(1024)(128)(2,1)}, u32[]{:S(2)}) copy-start(bf16[2048]{0:T(1024)(128)(2,1)} %param.18) | copy-start | bytes 12292
  1.6 5.0 %copy-start.4 = (bf16[64,1,64,128]{3,2,1,0:T(8,128)(2,1)S(1)}, bf16[64,1,64,128]{3,2,1,0:T(8,128)(2,1)}, u32[]{:S(2)}) copy-start(bf16[64,1,64,128]{3,2,1,0:T(8,128)(2,1)} %param.14) | copy-start | bytes 3145732
  5.4 1.9 %copy-start.2 = (bf16[64,2048]{1,0:T(8,128)(2,1)S(1)}, bf16[64,2048]{1,0:T(8,128)(2,1)}, u32[]{:S(2)}) copy-start(bf16[64,2048]{1,0:T(8,128)(2,1)} %param.11) | copy-start | bytes 786436
  7.6 15.2 %collective-permute-start = (bf16[64,2048]{1,0:T(8,128)(2,1)S(1)}, bf16[64,2048]{1,0:T(8,128)(2,1)S(1)}, u32[]{:S(2)}, u32[]{:S(2)}) collective-permute-start(bf16[64,2048]{1,0:T(8,128)(2,1)S(1)} %get-tuple-element.42.refs_2_.refs_0_), channel_id=1, source_target_pairs={{0,8},{8,0},{16,24},{24,16},{1,9},{9,1},{17,25},{25,17},{2,10},{10... | collective-permute-start | bytes 786440 | tf_op jit(solution)/shard_map/ppermute | solution.py:23
  10.6 13.4 %collective-permute-start.1 = (bf16[64,2048]{1,0:T(8,128)(2,1)S(1)}, bf16[64,2048]{1,0:T(8,128)(2,1)S(1)}, u32[]{:S(2)}, u32[]{:S(2)}) collective-permute-start(bf16[64,2048]{1,0:T(8,128)(2,1)S(1)} %get-tuple-element.42.refs_2_.refs_0_), channel_id=1, source_target_pairs={{0,16},{8,24},{16,0},{24,8},{1,17},{9,25},{17,1},{25,9},{2,18},{10... | collective-permute-start | bytes 786440 | tf_op jit(solution)/shard_map/ppermute | solution.py:23
  12.1 11.9 %collective-permute-start.2 = (bf16[64,2048]{1,0:T(8,128)(2,1)S(1)}, bf16[64,2048]{1,0:T(8,128)(2,1)S(1)}, u32[]{:S(2)}, u32[]{:S(2)}) collective-permute-start(bf16[64,2048]{1,0:T(8,128)(2,1)S(1)} %get-tuple-element.42.refs_2_.refs_0_), channel_id=1, source_target_pairs={{0,24},{8,16},{16,8},{24,0},{1,25},{9,17},{17,9},{25,1},{2,26},{10... | collective-permute-start | bytes 786440 | tf_op jit(solution)/shard_map/ppermute | solution.py:23
  12.2 1.2 collective-permute-start.3
  13.5 3.9 %collective-permute-start.4 = (f32[64,1]{1,0:T(8,128)S(1)}, f32[64,1]{1,0:T(8,128)S(1)}, u32[]{:S(2)}, u32[]{:S(2)}) collective-permute-start(f32[64,1]{1,0:T(8,128)S(1)} %add.85), channel_id=1, source_target_pairs={{0,2},{1,3},{2,0},{3,1},{4,6},{5,7},{6,4},{7,5},{8,10},{9,11},{10,... | collective-permute-start | bytes 776 | tf_op jit(solution)/shard_map/ppermute | solution.py:23
  17.4 5.4 %collective-permute-start.5 = (f32[64,1]{1,0:T(8,128)S(1)}, f32[64,1]{1,0:T(8,128)S(1)}, u32[]{:S(2)}, u32[]{:S(2)}) collective-permute-start(f32[64,1]{1,0:T(8,128)S(1)} %add.86), channel_id=1, source_target_pairs={{0,4},{1,5},{2,6},{3,7},{4,0},{5,1},{6,2},{7,3},{8,12},{9,13},{10,... | collective-permute-start | bytes 776 | tf_op jit(solution)/shard_map/ppermute | solution.py:23
  32.3 3.6 %collective-permute-start.6 = (bf16[2,128,2048]{2,1,0:T(8,128)(2,1)S(1)}, bf16[2,128,2048]{2,1,0:T(8,128)(2,1)S(1)}, u32[]{:S(2)}, u32[]{:S(2)}) collective-permute-start(bf16[2,128,2048]{2,1,0:T(8,128)(2,1)S(1)} %get-tuple-element.24), channel_id=1, source_target_pairs={{0,1},{1,0},{2,3},{3,2},{4,5},{5,4},{6,7},{7,6},{8,9},{9,8},{10,11... | collective-permute-start | bytes 3145736 | tf_op jit(solution)/shard_map/ppermute | solution.py:23
  32.3 16.3 %collective-permute-start.10 = (f32[64,1]{1,0:T(8,128)S(1)}, f32[64,1]{1,0:T(8,128)S(1)}, u32[]{:S(2)}, u32[]{:S(2)}) collective-permute-start(f32[64,1]{1,0:T(8,128)S(1)} %get-tuple-element.28.refs_2_.refs_0_), channel_id=1, source_target_pairs={{0,24},{8,16},{16,8},{24,0},{1,25},{9,17},{17,9},{25,1},{2,26},{10... | collective-permute-start | bytes 776 | tf_op jit(solution)/shard_map/ppermute | solution.py:23
  33.9 14.8 %collective-permute-start.8 = (f32[64,1]{1,0:T(8,128)S(1)}, f32[64,1]{1,0:T(8,128)S(1)}, u32[]{:S(2)}, u32[]{:S(2)}) collective-permute-start(f32[64,1]{1,0:T(8,128)S(1)} %get-tuple-element.28.refs_2_.refs_0_), channel_id=1, source_target_pairs={{0,8},{8,0},{16,24},{24,16},{1,9},{9,1},{17,25},{25,17},{2,10},{10... | collective-permute-start | bytes 776 | tf_op jit(solution)/shard_map/ppermute | solution.py:23
  35.4 13.3 %collective-permute-start.9 = (f32[64,1]{1,0:T(8,128)S(1)}, f32[64,1]{1,0:T(8,128)S(1)}, u32[]{:S(2)}, u32[]{:S(2)}) collective-permute-start(f32[64,1]{1,0:T(8,128)S(1)} %get-tuple-element.28.refs_2_.refs_0_), channel_id=1, source_target_pairs={{0,16},{8,24},{16,0},{24,8},{1,17},{9,25},{17,1},{25,9},{2,18},{10... | collective-permute-start | bytes 776 | tf_op jit(solution)/shard_map/ppermute | solution.py:23
  36.0 12.7 %collective-permute-start.7 = (bf16[2,32,2048]{2,1,0:T(8,128)(2,1)S(1)}, bf16[2,32,2048]{2,1,0:T(8,128)(2,1)S(1)}, u32[]{:S(2)}, u32[]{:S(2)}) collective-permute-start(bf16[2,32,2048]{2,1,0:T(8,128)(2,1)S(1)} %shard_map.111.refs_7_), channel_id=1, source_target_pairs={{0,2},{1,3},{2,6},{3,7},{6,4},{7,5},{4,0},{5,1},{8,10},{9,11},{10,... | collective-permute-start | bytes 786440 | tf_op jit(solution)/shard_map/ppermute | solution.py:30
  48.8 9.8 %collective-permute-start.11 = (bf16[2,128,3072]{2,1,0:T(8,128)(2,1)S(1)}, bf16[2,128,3072]{2,1,0:T(8,128)(2,1)S(1)}, u32[]{:S(2)}, u32[]{:S(2)}) collective-permute-start(bf16[2,128,3072]{2,1,0:T(8,128)(2,1)S(1)} %shard_map.114.refs_7_), channel_id=1, source_target_pairs={{0,1},{1,0},{2,3},{3,2},{4,5},{5,4},{6,7},{7,6},{8,9},{9,8},{10,11... | collective-permute-start | bytes 4718600 | tf_op jit(solution)/shard_map/ppermute | solution.py:23
  48.9 9.6 %collective-permute-start.12 = (bf16[2,32,2048]{2,1,0:T(8,128)(2,1)S(1)}, bf16[2,32,2048]{2,1,0:T(8,128)(2,1)S(1)}, u32[]{:S(2)}, u32[]{:S(2)}) collective-permute-start(bf16[2,32,2048]{2,1,0:T(8,128)(2,1)S(1)} %shard_map.113.refs_1_), channel_id=1, source_target_pairs={{0,2},{1,3},{2,6},{3,7},{6,4},{7,5},{4,0},{5,1},{8,10},{9,11},{10,... | collective-permute-start | bytes 786440 | tf_op jit(solution)/shard_map/ppermute | solution.py:30
  58.7 22.1 %collective-permute-start.13 = (bf16[2,128,1536]{2,1,0:T(8,128)(2,1)S(1)}, bf16[2,128,1536]{2,1,0:T(8,128)(2,1)S(1)}, u32[]{:S(2)}, u32[]{:S(2)}) collective-permute-start(bf16[2,128,1536]{2,1,0:T(8,128)(2,1)S(1)} %shard_map.118.refs_1_), channel_id=1, source_target_pairs={{0,1},{1,0},{2,3},{3,2},{4,5},{5,4},{6,7},{7,6},{8,9},{9,8},{10,11... | collective-permute-start | bytes 2359304 | tf_op jit(solution)/shard_map/ppermute | solution.py:23
  58.8 18.8 %collective-permute-start.14 = (bf16[2,32,3072]{2,1,0:T(8,128)(2,1)S(1)}, bf16[2,32,3072]{2,1,0:T(8,128)(2,1)S(1)}, u32[]{:S(2)}, u32[]{:S(2)}) collective-permute-start(bf16[2,32,3072]{2,1,0:T(8,128)(2,1)S(1)} %shard_map.117.refs_1_), channel_id=1, source_target_pairs={{0,2},{1,3},{2,6},{3,7},{6,4},{7,5},{4,0},{5,1},{8,10},{9,11},{10,... | collective-permute-start | bytes 1179656 | tf_op jit(solution)/shard_map/ppermute | solution.py:30
  60.5 16.3 %collective-permute-start.15 = (bf16[2,32,2048]{2,1,0:T(8,128)(2,1)S(1)}, bf16[2,32,2048]{2,1,0:T(8,128)(2,1)S(1)}, u32[]{:S(2)}, u32[]{:S(2)}) collective-permute-start(bf16[2,32,2048]{2,1,0:T(8,128)(2,1)S(1)} %shard_map.116.refs_0_), channel_id=1, source_target_pairs={{0,2},{1,3},{2,6},{3,7},{6,4},{7,5},{4,0},{5,1},{8,10},{9,11},{10,... | collective-permute-start | bytes 786440 | tf_op jit(solution)/shard_map/ppermute | solution.py:30
  77.8 14.4 %collective-permute-start.17 = (bf16[2,32,3072]{2,1,0:T(8,128)(2,1)S(1)}, bf16[2,32,3072]{2,1,0:T(8,128)(2,1)S(1)}, u32[]{:S(2)}, u32[]{:S(2)}) collective-permute-start(bf16[2,32,3072]{2,1,0:T(8,128)(2,1)S(1)} %shard_map.121.refs_0_), channel_id=1, source_target_pairs={{0,2},{1,3},{2,6},{3,7},{6,4},{7,5},{4,0},{5,1},{8,10},{9,11},{10,... | collective-permute-start | bytes 1179656 | tf_op jit(solution)/shard_map/ppermute | solution.py:30
  78.6 13.6 %collective-permute-start.18 = (bf16[32,2048]{1,0:T(8,128)(2,1)S(1)}, bf16[32,2048]{1,0:T(8,128)(2,1)S(1)}, u32[]{:S(2)}, u32[]{:S(2)}) collective-permute-start(bf16[32,2048]{1,0:T(8,128)(2,1)S(1)} %shard_map.120.refs_1_.refs_3_), channel_id=1, source_target_pairs={{0,2},{1,3},{2,6},{3,7},{6,4},{7,5},{4,0},{5,1},{8,10},{9,11},{10,... | collective-permute-start | bytes 393224 | tf_op jit(solution)/shard_map/ppermute | solution.py:30
  92.3 19.5 %collective-permute-start.20 = (bf16[2,32,3072]{2,1,0:T(8,128)(2,1)S(1)}, bf16[2,32,3072]{2,1,0:T(8,128)(2,1)S(1)}, u32[]{:S(2)}, u32[]{:S(2)}) collective-permute-start(bf16[2,32,3072]{2,1,0:T(8,128)(2,1)S(1)} %shard_map.123.refs_1_), channel_id=1, source_target_pairs={{0,2},{1,3},{2,6},{3,7},{6,4},{7,5},{4,0},{5,1},{8,10},{9,11},{10,... | collective-permute-start | bytes 1179656 | tf_op jit(solution)/shard_map/ppermute | solution.py:30
  92.4 16.3 %collective-permute-start.16 = (bf16[2,32,1536]{2,1,0:T(8,128)(2,1)S(1)}, bf16[2,32,1536]{2,1,0:T(8,128)(2,1)S(1)}, u32[]{:S(2)}, u32[]{:S(2)}) collective-permute-start(bf16[2,32,1536]{2,1,0:T(8,128)(2,1)S(1)} %shard_map.122.refs_1_), channel_id=1, source_target_pairs={{0,2},{1,3},{2,6},{3,7},{6,4},{7,5},{4,0},{5,1},{8,10},{9,11},{10,... | collective-permute-start | bytes 589832 | tf_op jit(solution)/shard_map/ppermute | solution.py:30
  95.4 15.9 %collective-permute-start.21 = (bf16[32,2048]{1,0:T(8,128)(2,1)S(1)}, bf16[32,2048]{1,0:T(8,128)(2,1)S(1)}, u32[]{:S(2)}, u32[]{:S(2)}) collective-permute-start(bf16[32,2048]{1,0:T(8,128)(2,1)S(1)} %collective-permute-done.18.refs_2_.refs_0_), channel_id=1, source_target_pairs={{0,2},{1,3},{2,6},{3,7},{6,4},{7,5},{4,0},{5,1},{8,10},{9,11},{10,... | collective-permute-start | bytes 393224 | tf_op jit(solution)/shard_map/ppermute | solution.py:30
  108.8 6.9 %collective-permute-start.19 = (bf16[2,32,1536]{2,1,0:T(8,128)(2,1)S(1)}, bf16[2,32,1536]{2,1,0:T(8,128)(2,1)S(1)}, u32[]{:S(2)}, u32[]{:S(2)}) collective-permute-start(bf16[2,32,1536]{2,1,0:T(8,128)(2,1)S(1)} %shard_map.124.refs_4_), channel_id=1, source_target_pairs={{0,2},{1,3},{2,6},{3,7},{6,4},{7,5},{4,0},{5,1},{8,10},{9,11},{10,... | collective-permute-start | bytes 589832 | tf_op jit(solution)/shard_map/ppermute | solution.py:30
  111.4 5.9 %collective-permute-start.23 = (bf16[32,2048]{1,0:T(8,128)(2,1)S(1)}, bf16[32,2048]{1,0:T(8,128)(2,1)S(1)}, u32[]{:S(2)}, u32[]{:S(2)}) collective-permute-start(bf16[32,2048]{1,0:T(8,128)(2,1)S(1)} %collective-permute-done.21.refs_2_.refs_1_), channel_id=1, source_target_pairs={{0,2},{1,3},{2,6},{3,7},{6,4},{7,5},{4,0},{5,1},{8,10},{9,11},{10,... | collective-permute-start | bytes 393224 | tf_op jit(solution)/shard_map/ppermute | solution.py:30
  117.3 22.3 %collective-permute-start.30 = (bf16[128,2048]{1,0:T(8,128)(2,1)S(1)}, bf16[128,2048]{1,0:T(8,128)(2,1)S(1)}, u32[]{:S(2)}, u32[]{:S(2)}) collective-permute-start(bf16[128,2048]{1,0:T(8,128)(2,1)S(1)} %shard_map.127.refs_4_.refs_0_), channel_id=1, source_target_pairs={{0,1},{1,0},{2,3},{3,2},{4,5},{5,4},{6,7},{7,6},{8,9},{9,8},{10,11... | collective-permute-start | bytes 1572872 | tf_op jit(solution)/shard_map/ppermute | solution.py:23
  117.4 8.7 %collective-permute-start.27 = (bf16[32,3072]{1,0:T(8,128)(2,1)S(1)}, bf16[32,3072]{1,0:T(8,128)(2,1)S(1)}, u32[]{:S(2)}, u32[]{:S(2)}) collective-permute-start(bf16[32,3072]{1,0:T(8,128)(2,1)S(1)} %shard_map.125.refs_1_.refs_3_), channel_id=1, source_target_pairs={{0,2},{1,3},{2,6},{3,7},{6,4},{7,5},{4,0},{5,1},{8,10},{9,11},{10,... | collective-permute-start | bytes 589832 | tf_op jit(solution)/shard_map/ppermute | solution.py:30
  117.4 12.8 %collective-permute-start.22 = (bf16[2,32,1536]{2,1,0:T(8,128)(2,1)S(1)}, bf16[2,32,1536]{2,1,0:T(8,128)(2,1)S(1)}, u32[]{:S(2)}, u32[]{:S(2)}) collective-permute-start(bf16[2,32,1536]{2,1,0:T(8,128)(2,1)S(1)} %shard_map.126.refs_4_), channel_id=1, source_target_pairs={{0,2},{1,3},{2,6},{3,7},{6,4},{7,5},{4,0},{5,1},{8,10},{9,11},{10,... | collective-permute-start | bytes 589832 | tf_op jit(solution)/shard_map/ppermute | solution.py:30
  126.0 10.5 %collective-permute-start.28 = (bf16[32,3072]{1,0:T(8,128)(2,1)S(1)}, bf16[32,3072]{1,0:T(8,128)(2,1)S(1)}, u32[]{:S(2)}, u32[]{:S(2)}) collective-permute-start(bf16[32,3072]{1,0:T(8,128)(2,1)S(1)} %collective-permute-done.27.refs_5_.refs_0_), channel_id=1, source_target_pairs={{0,2},{1,3},{2,6},{3,7},{6,4},{7,5},{4,0},{5,1},{8,10},{9,11},{10,... | collective-permute-start | bytes 589832 | tf_op jit(solution)/shard_map/ppermute | solution.py:30
  130.9 5.6 %collective-permute-start.24 = (bf16[32,1536]{1,0:T(8,128)(2,1)S(1)}, bf16[32,1536]{1,0:T(8,128)(2,1)S(1)}, u32[]{:S(2)}, u32[]{:S(2)}) collective-permute-start(bf16[32,1536]{1,0:T(8,128)(2,1)S(1)} %shard_map.128.refs_4_.refs_3_), channel_id=1, source_target_pairs={{0,2},{1,3},{2,6},{3,7},{6,4},{7,5},{4,0},{5,1},{8,10},{9,11},{10,... | collective-permute-start | bytes 294920 | tf_op jit(solution)/shard_map/ppermute | solution.py:30
  136.5 7.7 %collective-permute-start.25 = (bf16[32,1536]{1,0:T(8,128)(2,1)S(1)}, bf16[32,1536]{1,0:T(8,128)(2,1)S(1)}, u32[]{:S(2)}, u32[]{:S(2)}) collective-permute-start(bf16[32,1536]{1,0:T(8,128)(2,1)S(1)} %collective-permute-done.24.refs_6_.refs_0_), channel_id=1, source_target_pairs={{0,2},{1,3},{2,6},{3,7},{6,4},{7,5},{4,0},{5,1},{8,10},{9,11},{10,... | collective-permute-start | bytes 294920 | tf_op jit(solution)/shard_map/ppermute | solution.py:30
  136.5 8.2 %collective-permute-start.29 = (bf16[32,3072]{1,0:T(8,128)(2,1)S(1)}, bf16[32,3072]{1,0:T(8,128)(2,1)S(1)}, u32[]{:S(2)}, u32[]{:S(2)}) collective-permute-start(bf16[32,3072]{1,0:T(8,128)(2,1)S(1)} %collective-permute-done.28.refs_1_.refs_5_), channel_id=1, source_target_pairs={{0,2},{1,3},{2,6},{3,7},{6,4},{7,5},{4,0},{5,1},{8,10},{9,11},{10,... | collective-permute-start | bytes 589832 | tf_op jit(solution)/shard_map/ppermute | solution.py:30
  144.7 2.4 %collective-permute-start.31 = (bf16[128,3072]{1,0:T(8,128)(2,1)S(1)}, bf16[128,3072]{1,0:T(8,128)(2,1)S(1)}, u32[]{:S(2)}, u32[]{:S(2)}) collective-permute-start(bf16[128,3072]{1,0:T(8,128)(2,1)S(1)} %shard_map.130.refs_0_.refs_5_), channel_id=1, source_target_pairs={{0,1},{1,0},{2,3},{3,2},{4,5},{5,4},{6,7},{7,6},{8,9},{9,8},{10,11... | collective-permute-start | bytes 2359304 | tf_op jit(solution)/shard_map/ppermute | solution.py:23
  144.8 9.0 %collective-permute-start.26 = (bf16[32,1536]{1,0:T(8,128)(2,1)S(1)}, bf16[32,1536]{1,0:T(8,128)(2,1)S(1)}, u32[]{:S(2)}, u32[]{:S(2)}) collective-permute-start(bf16[32,1536]{1,0:T(8,128)(2,1)S(1)} %collective-permute-done.25.refs_7_.refs_1_), channel_id=1, source_target_pairs={{0,2},{1,3},{2,6},{3,7},{6,4},{7,5},{4,0},{5,1},{8,10},{9,11},{10,... | collective-permute-start | bytes 294920 | tf_op jit(solution)/shard_map/ppermute | solution.py:30
  153.9 1.8 %collective-permute-start.32 = (bf16[128,1536]{1,0:T(8,128)(2,1)S(1)}, bf16[128,1536]{1,0:T(8,128)(2,1)S(1)}, u32[]{:S(2)}, u32[]{:S(2)}) collective-permute-start(bf16[128,1536]{1,0:T(8,128)(2,1)S(1)} %shard_map.132.refs_0_.refs_5_), channel_id=1, source_target_pairs={{0,1},{1,0},{2,3},{3,2},{4,5},{5,4},{6,7},{7,6},{8,9},{9,8},{10,11... | collective-permute-start | bytes 1179656 | tf_op jit(solution)/shard_map/ppermute | solution.py:23
  155.7 20.0 %copy-start.1 = (bf16[64,16384]{1,0:T(8,128)(2,1)S(1)}, bf16[64,16384]{1,0:T(8,128)(2,1)}, u32[]{:S(2)}) copy-start(bf16[64,16384]{1,0:T(8,128)(2,1)} %param.12) | copy-start | bytes 6291460
  159.5 9.2 %collective-permute-start.33 = (bf16[64,2048]{1,0:T(8,128)(2,1)S(1)}, bf16[64,2048]{1,0:T(8,128)(2,1)S(1)}, u32[]{:S(2)}, u32[]{:S(2)}) collective-permute-start(bf16[64,2048]{1,0:T(8,128)(2,1)S(1)} %get-tuple-element.36), channel_id=1, source_target_pairs={{0,8},{8,0},{16,24},{24,16},{1,9},{9,1},{17,25},{25,17},{2,10},{10... | collective-permute-start | bytes 786440 | tf_op jit(solution)/shard_map/ppermute | solution.py:23
  160.8 12.1 %collective-permute-start.34 = (bf16[64,2048]{1,0:T(8,128)(2,1)S(1)}, bf16[64,2048]{1,0:T(8,128)(2,1)S(1)}, u32[]{:S(2)}, u32[]{:S(2)}) collective-permute-start(bf16[64,2048]{1,0:T(8,128)(2,1)S(1)} %get-tuple-element.37), channel_id=1, source_target_pairs={{0,16},{8,24},{16,0},{24,8},{1,17},{9,25},{17,1},{25,9},{2,18},{10... | collective-permute-start | bytes 786440 | tf_op jit(solution)/shard_map/ppermute | solution.py:23
  161.6 12.9 %collective-permute-start.35 = (bf16[64,2048]{1,0:T(8,128)(2,1)S(1)}, bf16[64,2048]{1,0:T(8,128)(2,1)S(1)}, u32[]{:S(2)}, u32[]{:S(2)}) collective-permute-start(bf16[64,2048]{1,0:T(8,128)(2,1)S(1)} %get-tuple-element.38), channel_id=1, source_target_pairs={{0,24},{8,16},{16,8},{24,0},{1,25},{9,17},{17,9},{25,1},{2,26},{10... | collective-permute-start | bytes 786440 | tf_op jit(solution)/shard_map/ppermute | solution.py:23

commit v3 on v2

--- a/solution.py
+++ b/solution.py
@@ -11,7 +11,7 @@
 D = 16384
 HEADS = 128
 KV_HEADS = 8
-CHUNK_UNITS = (8, 12, 6)
+CHUNK_UNITS = (14, 12)
 SLOTS = 4
 READY = 2
 READY_DOWN = 1
@@ -83,13 +83,14 @@
 
 
 def tiles(weights, out_ref, sems, first_unit, by_rows):
-    count, unit = out_ref.shape[0], out_ref.shape[1 if by_rows else 3]
+    count = out_ref.shape[0]
+    unit = out_ref.shape[1] if by_rows else out_ref.shape[2] // len(weights)
     copies = []
     for i in range(count):
         here = slice((first_unit + i) * unit, (first_unit + i + 1) * unit)
         for j, weight in enumerate(weights):
             source = weight.at[here, :] if by_rows else weight.at[:, here]
-            target = out_ref.at[i] if by_rows else out_ref.at[i, j]
+            target = out_ref.at[i] if by_rows else out_ref.at[i, :, j * unit : (j + 1) * unit]
             copies.append(pltpu.make_async_copy(source, target, sems.at[i, j]))
     return copies
 
@@ -114,7 +115,7 @@
     keep_ref, send_ref, *rest = refs[len(refs) - 6 - has_ride - has_next :]
     x_ref, held, sems, next_sems = rest[-4:]
     half = keep_ref.shape[1]
-    unit = held.shape[3]
+    unit = held.shape[2] // 2
     parts = (place_ref.shape[0] - 1) // n_blocks
     rows = blocks[0].shape[0] // parts
     ahead = []
@@ -124,7 +125,9 @@
     def copies(i, slot):
         columns = pl.ds(pl.multiple_of((first_unit + i) * unit, unit), unit)
         return [
-            pltpu.make_async_copy(weight.at[:, columns], held.at[slot, j], sems.at[slot, j])
+            pltpu.make_async_copy(
+                weight.at[:, columns], held.at[slot, :, j * unit : (j + 1) * unit], sems.at[slot, j]
+            )
             for j, weight in enumerate((gate_ref, up_ref))
         ]
 
@@ -137,11 +140,12 @@
 
     def compute(i, slot):
         columns = pl.ds(i * unit if slot is None else pl.multiple_of(i * unit, unit), unit)
+        weights = ready_ref[i] if slot is None else held[slot]
+        y = jnp.dot(x_ref[...], weights, preferred_element_type=jnp.float32)
         for j in range(2):
-            weight = ready_ref[i, j] if slot is None else held[slot, j]
-            y = jnp.dot(x_ref[...], weight, preferred_element_type=jnp.float32)
-            keep_ref[j, :, columns] = y[:half].astype(jnp.bfloat16)
-            send_ref[j, :, columns] = y[half:].astype(jnp.bfloat16)
+            here = slice(j * unit, (j + 1) * unit)
+            keep_ref[j, :, columns] = y[:half, here].astype(jnp.bfloat16)
+            send_ref[j, :, columns] = y[half:, here].astype(jnp.bfloat16)
 
     stream(units, ready_ref.shape[0], copies, ahead, prepare, compute)
 
@@ -168,7 +172,7 @@
         out_shape=outs,
         scratch_shapes=[
             pltpu.VMEM((total, depth), jnp.bfloat16),
-            pltpu.VMEM((SLOTS, 2, depth, unit), jnp.bfloat16),
+            pltpu.VMEM((SLOTS, depth, 2 * unit), jnp.bfloat16),
             pltpu.SemaphoreType.DMA((SLOTS, 2)),
             pltpu.SemaphoreType.DMA((READY, 2)),
         ],
@@ -453,14 +457,15 @@
     n_chunks = len(CHUNK_UNITS)
     total = None
     chunks = [{} for _ in range(n_chunks)]
-    ready = bring((gate_weight, up_weight), (READY, 2, tokens.shape[1], unit), 0, False, [tokens])
+    shape = (READY, tokens.shape[1], 2 * unit)
+    ready = bring((gate_weight, up_weight), shape, 0, False, [tokens])
     last = [ready]
 
     def turn_of(k, stage):
         return k + stage - (k == 0 and stage > 0)
 
-    flowing = [0, 2 * chips, 2 * chips - 1, chips, None, *range(chips - 1, 0, -1)]
-    closing = [2 * chips, None, 2 * chips - 1]
+    flowing = [0, 2 * chips, chips, None, *range(chips - 1, 0, -1), 2 * chips - 1]
+    closing = [2 * chips, 2 * chips - 1, None]
     for turn in range(n_chunks + 2 * chips):
         if turn == n_chunks:
             shape = (READY_DOWN, 2 * unit, down_weight.shape[1])

time: 176 us -> 172 us (0.977)
  waiting for transfers between devices: 79.5 us -> 85 us
  Pallas kernels: 48.2 us -> 43 us
  starting transfers between devices: 38.5 us -> 36 us
    ppermute x18 -> x12, waiting for transfers between devices: 61 us -> 66.8 us  [along_ring(): lax.ppermute(x, 'blk', [(2 * a + c, 2 * b + c) for a, b in hops for c in...]
    pallas_call x3 -> x2, Pallas kernels: 25.8 us -> 23.2 us  [gate_up(): pl.pallas_call(functools.partial(gate_up_kernel, len(blocks), len(rides),...]
    ppermute x18 -> x12, starting transfers between devices: 21.2 us -> 19.1 us  [along_ring(): lax.ppermute(x, 'blk', [(2 * a + c, 2 * b + c) for a, b in hops for c in...]
    pallas_call x3 -> x2, Pallas kernels: 15.2 us -> 13.2 us  [down(): pl.pallas_call(functools.partial(down_kernel, has_total, len(outs), start...]
    ppermute x18 -> x16, waiting for transfers between devices: 18.6 us -> 18.2 us  [partner(): lax.ppermute(x, axis, [(i, i ^ distance) for i in range(lax.axis_size(axi...]
    ppermute x18 -> x16, starting transfers between devices: 17.3 us -> 17 us  [partner(): lax.ppermute(x, axis, [(i, i ^ distance) for i in range(lax.axis_size(axi...]
  transfers between devices with their start and end apart: 36 -> 28, of which waited for: 19 -> 18; matrix products, arithmetic and copies ran while one was open for 0% -> 0% of each run, Pallas kernels for 20% -> 14%
where the time goes in v3:
time: 172 us; the launch traced here: 171 us
  waiting for transfers between devices  85 us (49%)
  Pallas kernels  43 us (25%)
  starting transfers between devices  36 us (21%)
  other arithmetic  4.32 us (3%)
    ppermute x12, waiting for transfers between devices, along_ring(): lax.ppermute(x, 'blk', [(2 * a + c, 2 * b + c) for a, b in hops for c in...  66.8 us
    pallas_call x2, Pallas kernels, gate_up(): pl.pallas_call(functools.partial(gate_up_kernel, len(blocks), len(rides),...  23.2 us
    ppermute x12, starting transfers between devices, along_ring(): lax.ppermute(x, 'blk', [(2 * a + c, 2 * b + c) for a, b in hops for c in...  19.1 us
    ppermute x16, waiting for transfers between devices, partner(): lax.ppermute(x, axis, [(i, i ^ distance) for i in range(lax.axis_size(axi...  18.2 us
    ppermute x16, starting transfers between devices, partner(): lax.ppermute(x, axis, [(i, i ^ distance) for i in range(lax.axis_size(axi...  17 us
    pallas_call x2, Pallas kernels, down(): pl.pallas_call(functools.partial(down_kernel, has_total, len(outs), start...  13.2 us
    pallas_call x2, Pallas kernels, bring(): pl.pallas_call(functools.partial(bring_kernel, len(weights), first_unit,...  3.85 us
  transfers between devices with their start and end apart: 28, of which 18 were waited for; matrix products, arithmetic and copies ran while one was open for 0% of the time, Pallas kernels for 14%

profile of v3, /device:TPU:0, one launch (start us, length us, event | category | flops | bytes accessed | tf_op | source)
XLA Modules:
  0.0 171.4 jit_solution(17689317017494998909)
XLA Ops:
  0.0 0.9 iota_compare_fusion
  0.9 0.8 convert_element_type.27
  1.7 0.7 dynamic-slice_bitcast_fusion.1
  2.4 0.7 dynamic-slice_convert_fusion
  3.2 0.2 fusion.7
  3.4 0.7 select_reduce_fusion
  4.2 0.4 fusion.3
  4.6 0.7 fusion
  5.3 0.3 multiply_reduce_fusion
  5.6 4.0 %collective-permute-start.2 = (bf16[64,2048]{1,0:T(8,128)(2,1)S(1)}, bf16[64,2048]{1,0:T(8,128)(2,1)S(1)}, u32[]{:S(2)}, u32[]{:S(2)}) collective-permute-start(bf16[64,2048]{1,0:T(8,128)(2,1)S(1)} %get-tuple-element.32.refs_2_.refs_0_), channel_id=1, source_target_pairs={{0,24},{8,16},{16,8},{24,0},{1,25},{9,17},{17,9},{25,1},{2,26},{10... | collective-permute-start | bytes 786440 | tf_op jit(solution)/shard_map/ppermute | solution.py:23
  9.5 0.5 collective-permute-start.1
  10.1 0.1 collective-permute-start
  10.4 1.1 collective-permute-done.3
  11.5 2.0 %collective-permute-start.4 = (f32[64,1]{1,0:T(8,128)S(1)}, f32[64,1]{1,0:T(8,128)S(1)}, u32[]{:S(2)}, u32[]{:S(2)}) collective-permute-start(f32[64,1]{1,0:T(8,128)S(1)} %add.85), channel_id=1, source_target_pairs={{0,2},{1,3},{2,0},{3,1},{4,6},{5,7},{6,4},{7,5},{8,10},{9,11},{10,... | collective-permute-start | bytes 776 | tf_op jit(solution)/shard_map/ppermute | solution.py:23
  13.5 1.9 %collective-permute-done.4 = f32[64,1]{1,0:T(8,128)S(1)} collective-permute-done((f32[64,1]{1,0:T(8,128)S(1)}, f32[64,1]{1,0:T(8,128)S(1)}, u32[]{:S(2)}, u32[]{:S(2)}) %collective-permute-start.4) | collective-permute-done | bytes 288 | tf_op jit(solution)/shard_map/ppermute | solution.py:23
  15.4 3.0 %collective-permute-start.5 = (f32[64,1]{1,0:T(8,128)S(1)}, f32[64,1]{1,0:T(8,128)S(1)}, u32[]{:S(2)}, u32[]{:S(2)}) collective-permute-start(f32[64,1]{1,0:T(8,128)S(1)} %add.86), channel_id=1, source_target_pairs={{0,4},{1,5},{2,6},{3,7},{4,0},{5,1},{6,2},{7,3},{8,12},{9,13},{10,... | collective-permute-start | bytes 776 | tf_op jit(solution)/shard_map/ppermute | solution.py:23
  18.5 2.3 %shard_map.109.refs_6_.refs_8_ = bf16[2,2048,512]{2,1,0:T(8,128)(2,1)S(1)} custom-call(bf16[2048,6656]{1,0:T(8,128)(2,1)} %refs_4_.3, bf16[2048,6656]{1,0:T(8,128)(2,1)} %refs_5_.3, bf16[64,2048]{1,0:T(8,128)(2,1)S(1)} %get-tuple-element.32.refs_2_.refs_0_), custom_call_target="tpu_custom_call" | custom-call | bytes 8388608 | tf_op jit(solution)/shard_map/pallas_call | solution.py:99
  20.8 0.7 collective-permute-done.1.refs_2_
  21.5 0.3 collective-permute-done.refs_1_
  21.8 12.4 %shard_map.110 = (bf16[2,128,3584]{2,1,0:T(8,128)(2,1)S(1)}, bf16[2,128,3584]{2,1,0:T(8,128)(2,1)S(1)}, f32[64,1]{1,0:T(8,128)S(1)}, bf16[2,2048,512]{2,1,0:T(8,128)(2,1)S(1)}) custom-call(s32[9]{0:T(128)S(1)} %pad_add_fusion.place_ref, bf16[64,2048]{1,0:T(8,128)(2,1)S(1)} %get-tuple-element.32.refs_2_.refs_0_, ...), custom_call_target="tpu_custom_call" | custom-call | flops 7516192768 | bytes 34078720 | tf_op jit(solution)/shard_map/pallas_call | solution.py:164
  34.3 1.6 collective-permute-start.10
  35.9 1.4 collective-permute-start.9
  37.3 0.5 collective-permute-start.8
  37.8 0.2 collective-permute-done.6.other_ref
  38.0 0.1 shard_map.111.refs_7_
  38.2 1.6 collective-permute-start.7
  39.8 10.8 %shard_map.112 = (bf16[2,128,3072]{2,1,0:T(8,128)(2,1)S(1)}, bf16[2,128,3072]{2,1,0:T(8,128)(2,1)S(1)}) custom-call(s32[9]{0:T(128)S(1)} %pad_add_fusion.place_ref, bf16[64,2048]{1,0:T(8,128)(2,1)S(1)} %get-tuple-element.32.refs_2_.refs_0_, bf16[64,2048]{1,0:T(8,128)(2,1)S(1)} %collective-permute-done.refs_1_, ...), custom_call_target="tpu_custom_call" | custom-call | flops 6442450944 | bytes 29360128 | tf_op jit(solution)/shard_map/pallas_call | solution.py:164
  50.6 1.1 collective-permute-done.7.refs_0_
  51.7 0.2 shard_map.113.refs_1_
  51.9 1.6 collective-permute-start.12
  53.5 1.6 shard_map.115.refs_1_.refs_3_
  55.1 10.6 %collective-permute-done.12.refs_0_ = bf16[2,32,3584]{2,1,0:T(8,128)(2,1)S(1)} collective-permute-done((bf16[2,32,3584]{2,1,0:T(8,128)(2,1)S(1)}, bf16[2,32,3584]{2,1,0:T(8,128)(2,1)S(1)}, u32[]{:S(2)}, u32[]{:S(2)}) %collective-permute-start.12) | collective-permute-done | bytes 458784 | tf_op jit(solution)/shard_map/ppermute | solution.py:30
  65.7 0.2 shard_map.116.refs_0_
  65.9 0.8 collective-permute-start.14
  66.8 3.4 %collective-permute-start.13 = (bf16[2,32,3072]{2,1,0:T(8,128)(2,1)S(1)}, bf16[2,32,3072]{2,1,0:T(8,128)(2,1)S(1)}, u32[]{:S(2)}, u32[]{:S(2)}) collective-permute-start(bf16[2,32,3072]{2,1,0:T(8,128)(2,1)S(1)} %shard_map.117.refs_4_), channel_id=1, source_target_pairs={{0,2},{1,3},{2,6},{3,7},{6,4},{7,5},{4,0},{5,1},{8,10},{9,11},{10,... | collective-permute-start | bytes 1179656 | tf_op jit(solution)/shard_map/ppermute | solution.py:30
  70.3 10.0 %collective-permute-done.14.flow_ref = bf16[2,32,3584]{2,1,0:T(8,128)(2,1)S(1)} collective-permute-done((bf16[2,32,3584]{2,1,0:T(8,128)(2,1)S(1)}, bf16[2,32,3584]{2,1,0:T(8,128)(2,1)S(1)}, u32[]{:S(2)}, u32[]{:S(2)}) %collective-permute-start.14) | collective-permute-done | bytes 458784 | tf_op jit(solution)/shard_map/ppermute | solution.py:30
  80.3 1.0 shard_map.118.refs_1_.refs_3_
  81.3 6.1 %collective-permute-done.13.refs_0_ = bf16[2,32,3072]{2,1,0:T(8,128)(2,1)S(1)} collective-permute-done((bf16[2,32,3072]{2,1,0:T(8,128)(2,1)S(1)}, bf16[2,32,3072]{2,1,0:T(8,128)(2,1)S(1)}, u32[]{:S(2)}, u32[]{:S(2)}) %collective-permute-start.13) | collective-permute-done | bytes 393248 | tf_op jit(solution)/shard_map/ppermute | solution.py:30
  87.4 0.1 shard_map.119.refs_1_
  87.5 0.8 collective-permute-start.15
  88.4 3.4 %collective-permute-start.16 = (bf16[32,3584]{1,0:T(8,128)(2,1)S(1)}, bf16[32,3584]{1,0:T(8,128)(2,1)S(1)}, u32[]{:S(2)}, u32[]{:S(2)}) collective-permute-start(bf16[32,3584]{1,0:T(8,128)(2,1)S(1)} %shard_map.118.refs_1_.refs_3_), channel_id=1, source_target_pairs={{0,2},{1,3},{2,6},{3,7},{6,4},{7,5},{4,0},{5,1},{8,10},{9,11},{10,... | collective-permute-start | bytes 688136 | tf_op jit(solution)/shard_map/ppermute | solution.py:30
  91.7 11.4 %collective-permute-done.16.refs_2_.refs_0_ = bf16[32,3584]{1,0:T(8,128)(2,1)S(1)} collective-permute-done((bf16[32,3584]{1,0:T(8,128)(2,1)S(1)}, bf16[32,3584]{1,0:T(8,128)(2,1)S(1)}, u32[]{:S(2)}, u32[]{:S(2)}) %collective-permute-start.16) | collective-permute-done | bytes 229408 | tf_op jit(solution)/shard_map/ppermute | solution.py:30
  103.2 0.8 collective-permute-start.21
  104.0 0.1 shard_map.120.refs_4_
  104.1 3.4 %collective-permute-start.17 = (bf16[2,32,3072]{2,1,0:T(8,128)(2,1)S(1)}, bf16[2,32,3072]{2,1,0:T(8,128)(2,1)S(1)}, u32[]{:S(2)}, u32[]{:S(2)}) collective-permute-start(bf16[2,32,3072]{2,1,0:T(8,128)(2,1)S(1)} %shard_map.120.refs_4_), channel_id=1, source_target_pairs={{0,2},{1,3},{2,6},{3,7},{6,4},{7,5},{4,0},{5,1},{8,10},{9,11},{10,... | collective-permute-start | bytes 1179656 | tf_op jit(solution)/shard_map/ppermute | solution.py:30
  107.5 5.1 %collective-permute-done.21.refs_1_.refs_5_ = bf16[32,3584]{1,0:T(8,128)(2,1)S(1)} collective-permute-done((bf16[32,3584]{1,0:T(8,128)(2,1)S(1)}, bf16[32,3584]{1,0:T(8,128)(2,1)S(1)}, u32[]{:S(2)}, u32[]{:S(2)}) %collective-permute-start.21) | collective-permute-done | bytes 229408 | tf_op jit(solution)/shard_map/ppermute | solution.py:30
  112.6 0.8 collective-permute-start.22
  113.4 6.9 %collective-permute-done.17.flow_ref = bf16[2,32,3072]{2,1,0:T(8,128)(2,1)S(1)} collective-permute-done((bf16[2,32,3072]{2,1,0:T(8,128)(2,1)S(1)}, bf16[2,32,3072]{2,1,0:T(8,128)(2,1)S(1)}, u32[]{:S(2)}, u32[]{:S(2)}) %collective-permute-start.17) | collective-permute-done | bytes 393248 | tf_op jit(solution)/shard_map/ppermute | solution.py:30
  120.3 0.9 shard_map.121.refs_4_.refs_3_
  121.2 1.6 collective-permute-done.22.refs_2_
  122.9 0.8 collective-permute-start.18
  123.7 7.4 %collective-permute-done.18.refs_5_.refs_0_ = bf16[32,3072]{1,0:T(8,128)(2,1)S(1)} collective-permute-done((bf16[32,3072]{1,0:T(8,128)(2,1)S(1)}, bf16[32,3072]{1,0:T(8,128)(2,1)S(1)}, u32[]{:S(2)}, u32[]{:S(2)}) %collective-permute-start.18) | collective-permute-done | bytes 196640 | tf_op jit(solution)/shard_map/ppermute | solution.py:30
  131.1 0.8 collective-permute-start.19
  131.9 6.6 %collective-permute-done.19.refs_1_.refs_5_ = bf16[32,3072]{1,0:T(8,128)(2,1)S(1)} collective-permute-done((bf16[32,3072]{1,0:T(8,128)(2,1)S(1)}, bf16[32,3072]{1,0:T(8,128)(2,1)S(1)}, u32[]{:S(2)}, u32[]{:S(2)}) %collective-permute-start.19) | collective-permute-done | bytes 196640 | tf_op jit(solution)/shard_map/ppermute | solution.py:30
  138.5 0.8 collective-permute-start.20
  139.3 6.9 %shard_map.123 = (f32[256,2048]{1,0:T(8,128)S(1)}, bf16[1,512,2048]{2,1,0:T(8,128)(2,1)S(1)}) custom-call(s32[9]{0:T(128)S(1)} %pad_add_fusion.place_ref, bf16[128,3584]{1,0:T(8,128)(2,1)S(1)} %shard_map.122.refs_0_.refs_4_, bf16[128,3584]{1,0:T(8,128)(2,1)S(1)} %collective-permute-done.23.refs_1_, bf16[6656,2048]{1,0:T(8,128)(2,1)} %refs_2_.3, ...), custom_call_target="tpu_custom_call" | custom-call | flops 3758096384 | bytes 18874368 | tf_op jit(solution)/shard_map/pallas_call | solution.py:338
  146.3 2.3 %collective-permute-done.24.refs_1_ = bf16[128,3072]{1,0:T(8,128)(2,1)S(1)} collective-permute-done((bf16[128,3072]{1,0:T(8,128)(2,1)S(1)}, bf16[128,3072]{1,0:T(8,128)(2,1)S(1)}, u32[]{:S(2)}, u32[]{:S(2)}) %collective-permute-start.24) | collective-permute-done | bytes 786464 | tf_op jit(solution)/shard_map/ppermute | solution.py:23
  148.6 6.3 %shard_map.125 = (f32[64,2048]{1,0:T(8,128)S(1)}, bf16[64,2048]{1,0:T(8,128)(2,1)S(1)}, bf16[64,2048]{1,0:T(8,128)(2,1)S(1)}, bf16[64,2048]{1,0:T(8,128)(2,1)S(1)}) custom-call(s32[9]{0:T(128)S(1)} %pad_add_fusion.place_ref, bf16[128,3072]{1,0:T(8,128)(2,1)S(1)} %shard_map.124.refs_0_.refs_5_, bf16[128,3072]{1,0:T(8,128)(2,1)S(1)} %collective-permute-done.24.refs_1_, ...), custom_call_target="tpu_custom_call" | custom-call | flops 3221225472 | bytes 16777216 | tf_op jit(solution)/shard_map/pallas_call | solution.py:338
  154.9 1.6 collective-permute-start.25
  156.5 0.7 collective-permute-start.26
  157.2 1.3 collective-permute-start.27
  158.5 5.7 %collective-permute-done.25 = bf16[64,2048]{1,0:T(8,128)(2,1)S(1)} collective-permute-done((bf16[64,2048]{1,0:T(8,128)(2,1)S(1)}, bf16[64,2048]{1,0:T(8,128)(2,1)S(1)}, u32[]{:S(2)}, u32[]{:S(2)}) %collective-permute-start.25) | collective-permute-done | bytes 262176 | tf_op jit(solution)/shard_map/ppermute | solution.py:23
  164.1 6.0 %collective-permute-done.26 = bf16[64,2048]{1,0:T(8,128)(2,1)S(1)} collective-permute-done((bf16[64,2048]{1,0:T(8,128)(2,1)S(1)}, bf16[64,2048]{1,0:T(8,128)(2,1)S(1)}, u32[]{:S(2)}, u32[]{:S(2)}) %collective-permute-start.26) | collective-permute-done | bytes 262176 | tf_op jit(solution)/shard_map/ppermute | solution.py:23
  170.2 1.2 convert_add_fusion
  (39 shorter events, 0.9 us)
Async XLA Ops:
  0.0 3.1 %copy-start = (bf16[64,16384]{1,0:T(8,128)(2,1)S(1)}, bf16[64,16384]{1,0:T(8,128)(2,1)}, u32[]{:S(2)}) copy-start(bf16[64,16384]{1,0:T(8,128)(2,1)} %param.12) | copy-start | bytes 6291460
  0.0 3.4 %copy-start.2 = (bf16[64,1,64,128]{3,2,1,0:T(8,128)(2,1)S(1)}, bf16[64,1,64,128]{3,2,1,0:T(8,128)(2,1)}, u32[]{:S(2)}) copy-start(bf16[64,1,64,128]{3,2,1,0:T(8,128)(2,1)} %param.13) | copy-start | bytes 3145732
  3.1 1.5 copy-start.4
  4.2 1.1 copy-start.3
  5.6 15.2 %collective-permute-start.2 = (bf16[64,2048]{1,0:T(8,128)(2,1)S(1)}, bf16[64,2048]{1,0:T(8,128)(2,1)S(1)}, u32[]{:S(2)}, u32[]{:S(2)}) collective-permute-start(bf16[64,2048]{1,0:T(8,128)(2,1)S(1)} %get-tuple-element.32.refs_2_.refs_0_), channel_id=1, source_target_pairs={{0,24},{8,16},{16,8},{24,0},{1,25},{9,17},{17,9},{25,1},{2,26},{10... | collective-permute-start | bytes 786440 | tf_op jit(solution)/shard_map/ppermute | solution.py:23
  9.5 11.9 %collective-permute-start.1 = (bf16[64,2048]{1,0:T(8,128)(2,1)S(1)}, bf16[64,2048]{1,0:T(8,128)(2,1)S(1)}, u32[]{:S(2)}, u32[]{:S(2)}) collective-permute-start(bf16[64,2048]{1,0:T(8,128)(2,1)S(1)} %get-tuple-element.32.refs_2_.refs_0_), channel_id=1, source_target_pairs={{0,16},{8,24},{16,0},{24,8},{1,17},{9,25},{17,1},{25,9},{2,18},{10... | collective-permute-start | bytes 786440 | tf_op jit(solution)/shard_map/ppermute | solution.py:23
  10.1 11.7 %collective-permute-start = (bf16[64,2048]{1,0:T(8,128)(2,1)S(1)}, bf16[64,2048]{1,0:T(8,128)(2,1)S(1)}, u32[]{:S(2)}, u32[]{:S(2)}) collective-permute-start(bf16[64,2048]{1,0:T(8,128)(2,1)S(1)} %get-tuple-element.32.refs_2_.refs_0_), channel_id=1, source_target_pairs={{0,8},{8,0},{16,24},{24,16},{1,9},{9,1},{17,25},{25,17},{2,10},{10... | collective-permute-start | bytes 786440 | tf_op jit(solution)/shard_map/ppermute | solution.py:23
  10.3 1.2 collective-permute-start.3
  11.5 3.9 %collective-permute-start.4 = (f32[64,1]{1,0:T(8,128)S(1)}, f32[64,1]{1,0:T(8,128)S(1)}, u32[]{:S(2)}, u32[]{:S(2)}) collective-permute-start(f32[64,1]{1,0:T(8,128)S(1)} %add.85), channel_id=1, source_target_pairs={{0,2},{1,3},{2,0},{3,1},{4,6},{5,7},{6,4},{7,5},{8,10},{9,11},{10,... | collective-permute-start | bytes 776 | tf_op jit(solution)/shard_map/ppermute | solution.py:23
  15.4 5.3 %collective-permute-start.5 = (f32[64,1]{1,0:T(8,128)S(1)}, f32[64,1]{1,0:T(8,128)S(1)}, u32[]{:S(2)}, u32[]{:S(2)}) collective-permute-start(f32[64,1]{1,0:T(8,128)S(1)} %add.86), channel_id=1, source_target_pairs={{0,4},{1,5},{2,6},{3,7},{4,0},{5,1},{6,2},{7,3},{8,12},{9,13},{10,... | collective-permute-start | bytes 776 | tf_op jit(solution)/shard_map/ppermute | solution.py:23
  34.2 3.9 %collective-permute-start.6 = (bf16[2,128,3584]{2,1,0:T(8,128)(2,1)S(1)}, bf16[2,128,3584]{2,1,0:T(8,128)(2,1)S(1)}, u32[]{:S(2)}, u32[]{:S(2)}) collective-permute-start(bf16[2,128,3584]{2,1,0:T(8,128)(2,1)S(1)} %get-tuple-element.19), channel_id=1, source_target_pairs={{0,1},{1,0},{2,3},{3,2},{4,5},{5,4},{6,7},{7,6},{8,9},{9,8},{10,11... | collective-permute-start | bytes 5505032 | tf_op jit(solution)/shard_map/ppermute | solution.py:23
  34.3 16.3 %collective-permute-start.10 = (f32[64,1]{1,0:T(8,128)S(1)}, f32[64,1]{1,0:T(8,128)S(1)}, u32[]{:S(2)}, u32[]{:S(2)}) collective-permute-start(f32[64,1]{1,0:T(8,128)S(1)} %get-tuple-element.22.refs_2_.refs_0_), channel_id=1, source_target_pairs={{0,24},{8,16},{16,8},{24,0},{1,25},{9,17},{17,9},{25,1},{2,26},{10... | collective-permute-start | bytes 776 | tf_op jit(solution)/shard_map/ppermute | solution.py:23
  35.9 14.7 %collective-permute-start.9 = (f32[64,1]{1,0:T(8,128)S(1)}, f32[64,1]{1,0:T(8,128)S(1)}, u32[]{:S(2)}, u32[]{:S(2)}) collective-permute-start(f32[64,1]{1,0:T(8,128)S(1)} %get-tuple-element.22.refs_2_.refs_0_), channel_id=1, source_target_pairs={{0,16},{8,24},{16,0},{24,8},{1,17},{9,25},{17,1},{25,9},{2,18},{10... | collective-permute-start | bytes 776 | tf_op jit(solution)/shard_map/ppermute | solution.py:23
  37.3 13.3 %collective-permute-start.8 = (f32[64,1]{1,0:T(8,128)S(1)}, f32[64,1]{1,0:T(8,128)S(1)}, u32[]{:S(2)}, u32[]{:S(2)}) collective-permute-start(f32[64,1]{1,0:T(8,128)S(1)} %get-tuple-element.22.refs_2_.refs_0_), channel_id=1, source_target_pairs={{0,8},{8,0},{16,24},{24,16},{1,9},{9,1},{17,25},{25,17},{2,10},{10... | collective-permute-start | bytes 776 | tf_op jit(solution)/shard_map/ppermute | solution.py:23
  38.2 13.5 %collective-permute-start.7 = (bf16[2,32,3584]{2,1,0:T(8,128)(2,1)S(1)}, bf16[2,32,3584]{2,1,0:T(8,128)(2,1)S(1)}, u32[]{:S(2)}, u32[]{:S(2)}) collective-permute-start(bf16[2,32,3584]{2,1,0:T(8,128)(2,1)S(1)} %shard_map.111.refs_7_), channel_id=1, source_target_pairs={{0,2},{1,3},{2,6},{3,7},{6,4},{7,5},{4,0},{5,1},{8,10},{9,11},{10,... | collective-permute-start | bytes 1376264 | tf_op jit(solution)/shard_map/ppermute | solution.py:30
  51.8 14.9 %collective-permute-start.11 = (bf16[2,128,3072]{2,1,0:T(8,128)(2,1)S(1)}, bf16[2,128,3072]{2,1,0:T(8,128)(2,1)S(1)}, u32[]{:S(2)}, u32[]{:S(2)}) collective-permute-start(bf16[2,128,3072]{2,1,0:T(8,128)(2,1)S(1)} %shard_map.114.refs_1_), channel_id=1, source_target_pairs={{0,1},{1,0},{2,3},{3,2},{4,5},{5,4},{6,7},{7,6},{8,9},{9,8},{10,11... | collective-permute-start | bytes 4718600 | tf_op jit(solution)/shard_map/ppermute | solution.py:23
  51.9 13.8 %collective-permute-start.12 = (bf16[2,32,3584]{2,1,0:T(8,128)(2,1)S(1)}, bf16[2,32,3584]{2,1,0:T(8,128)(2,1)S(1)}, u32[]{:S(2)}, u32[]{:S(2)}) collective-permute-start(bf16[2,32,3584]{2,1,0:T(8,128)(2,1)S(1)} %shard_map.113.refs_1_), channel_id=1, source_target_pairs={{0,2},{1,3},{2,6},{3,7},{6,4},{7,5},{4,0},{5,1},{8,10},{9,11},{10,... | collective-permute-start | bytes 1376264 | tf_op jit(solution)/shard_map/ppermute | solution.py:30
  65.9 14.4 %collective-permute-start.14 = (bf16[2,32,3584]{2,1,0:T(8,128)(2,1)S(1)}, bf16[2,32,3584]{2,1,0:T(8,128)(2,1)S(1)}, u32[]{:S(2)}, u32[]{:S(2)}) collective-permute-start(bf16[2,32,3584]{2,1,0:T(8,128)(2,1)S(1)} %shard_map.116.refs_0_), channel_id=1, source_target_pairs={{0,2},{1,3},{2,6},{3,7},{6,4},{7,5},{4,0},{5,1},{8,10},{9,11},{10,... | collective-permute-start | bytes 1376264 | tf_op jit(solution)/shard_map/ppermute | solution.py:30
  66.8 20.5 %collective-permute-start.13 = (bf16[2,32,3072]{2,1,0:T(8,128)(2,1)S(1)}, bf16[2,32,3072]{2,1,0:T(8,128)(2,1)S(1)}, u32[]{:S(2)}, u32[]{:S(2)}) collective-permute-start(bf16[2,32,3072]{2,1,0:T(8,128)(2,1)S(1)} %shard_map.117.refs_4_), channel_id=1, source_target_pairs={{0,2},{1,3},{2,6},{3,7},{6,4},{7,5},{4,0},{5,1},{8,10},{9,11},{10,... | collective-permute-start | bytes 1179656 | tf_op jit(solution)/shard_map/ppermute | solution.py:30
  87.5 16.4 %collective-permute-start.15 = (bf16[2,32,3072]{2,1,0:T(8,128)(2,1)S(1)}, bf16[2,32,3072]{2,1,0:T(8,128)(2,1)S(1)}, u32[]{:S(2)}, u32[]{:S(2)}) collective-permute-start(bf16[2,32,3072]{2,1,0:T(8,128)(2,1)S(1)} %shard_map.119.refs_1_), channel_id=1, source_target_pairs={{0,2},{1,3},{2,6},{3,7},{6,4},{7,5},{4,0},{5,1},{8,10},{9,11},{10,... | collective-permute-start | bytes 1179656 | tf_op jit(solution)/shard_map/ppermute | solution.py:30
  88.4 14.8 %collective-permute-start.16 = (bf16[32,3584]{1,0:T(8,128)(2,1)S(1)}, bf16[32,3584]{1,0:T(8,128)(2,1)S(1)}, u32[]{:S(2)}, u32[]{:S(2)}) collective-permute-start(bf16[32,3584]{1,0:T(8,128)(2,1)S(1)} %shard_map.118.refs_1_.refs_3_), channel_id=1, source_target_pairs={{0,2},{1,3},{2,6},{3,7},{6,4},{7,5},{4,0},{5,1},{8,10},{9,11},{10,... | collective-permute-start | bytes 688136 | tf_op jit(solution)/shard_map/ppermute | solution.py:30
  103.2 9.4 %collective-permute-start.21 = (bf16[32,3584]{1,0:T(8,128)(2,1)S(1)}, bf16[32,3584]{1,0:T(8,128)(2,1)S(1)}, u32[]{:S(2)}, u32[]{:S(2)}) collective-permute-start(bf16[32,3584]{1,0:T(8,128)(2,1)S(1)} %collective-permute-done.16.refs_2_.refs_0_), channel_id=1, source_target_pairs={{0,2},{1,3},{2,6},{3,7},{6,4},{7,5},{4,0},{5,1},{8,10},{9,11},{10,... | collective-permute-start | bytes 688136 | tf_op jit(solution)/shard_map/ppermute | solution.py:30
  104.1 16.2 %collective-permute-start.17 = (bf16[2,32,3072]{2,1,0:T(8,128)(2,1)S(1)}, bf16[2,32,3072]{2,1,0:T(8,128)(2,1)S(1)}, u32[]{:S(2)}, u32[]{:S(2)}) collective-permute-start(bf16[2,32,3072]{2,1,0:T(8,128)(2,1)S(1)} %shard_map.120.refs_4_), channel_id=1, source_target_pairs={{0,2},{1,3},{2,6},{3,7},{6,4},{7,5},{4,0},{5,1},{8,10},{9,11},{10,... | collective-permute-start | bytes 1179656 | tf_op jit(solution)/shard_map/ppermute | solution.py:30
  112.6 10.2 %collective-permute-start.22 = (bf16[32,3584]{1,0:T(8,128)(2,1)S(1)}, bf16[32,3584]{1,0:T(8,128)(2,1)S(1)}, u32[]{:S(2)}, u32[]{:S(2)}) collective-permute-start(bf16[32,3584]{1,0:T(8,128)(2,1)S(1)} %collective-permute-done.21.refs_1_.refs_5_), channel_id=1, source_target_pairs={{0,2},{1,3},{2,6},{3,7},{6,4},{7,5},{4,0},{5,1},{8,10},{9,11},{10,... | collective-permute-start | bytes 688136 | tf_op jit(solution)/shard_map/ppermute | solution.py:30
  122.8 16.4 %collective-permute-start.23 = (bf16[128,3584]{1,0:T(8,128)(2,1)S(1)}, bf16[128,3584]{1,0:T(8,128)(2,1)S(1)}, u32[]{:S(2)}, u32[]{:S(2)}) collective-permute-start(bf16[128,3584]{1,0:T(8,128)(2,1)S(1)} %shard_map.122.refs_0_.refs_4_), channel_id=1, source_target_pairs={{0,1},{1,0},{2,3},{3,2},{4,5},{5,4},{6,7},{7,6},{8,9},{9,8},{10,11... | collective-permute-start | bytes 2752520 | tf_op jit(solution)/shard_map/ppermute | solution.py:23
  122.9 8.2 %collective-permute-start.18 = (bf16[32,3072]{1,0:T(8,128)(2,1)S(1)}, bf16[32,3072]{1,0:T(8,128)(2,1)S(1)}, u32[]{:S(2)}, u32[]{:S(2)}) collective-permute-start(bf16[32,3072]{1,0:T(8,128)(2,1)S(1)} %shard_map.121.refs_4_.refs_3_), channel_id=1, source_target_pairs={{0,2},{1,3},{2,6},{3,7},{6,4},{7,5},{4,0},{5,1},{8,10},{9,11},{10,... | collective-permute-start | bytes 589832 | tf_op jit(solution)/shard_map/ppermute | solution.py:30
  131.1 7.4 %collective-permute-start.19 = (bf16[32,3072]{1,0:T(8,128)(2,1)S(1)}, bf16[32,3072]{1,0:T(8,128)(2,1)S(1)}, u32[]{:S(2)}, u32[]{:S(2)}) collective-permute-start(bf16[32,3072]{1,0:T(8,128)(2,1)S(1)} %collective-permute-done.18.refs_5_.refs_0_), channel_id=1, source_target_pairs={{0,2},{1,3},{2,6},{3,7},{6,4},{7,5},{4,0},{5,1},{8,10},{9,11},{10,... | collective-permute-start | bytes 589832 | tf_op jit(solution)/shard_map/ppermute | solution.py:30
  138.5 7.7 %collective-permute-start.20 = (bf16[32,3072]{1,0:T(8,128)(2,1)S(1)}, bf16[32,3072]{1,0:T(8,128)(2,1)S(1)}, u32[]{:S(2)}, u32[]{:S(2)}) collective-permute-start(bf16[32,3072]{1,0:T(8,128)(2,1)S(1)} %collective-permute-done.19.refs_1_.refs_5_), channel_id=1, source_target_pairs={{0,2},{1,3},{2,6},{3,7},{6,4},{7,5},{4,0},{5,1},{8,10},{9,11},{10,... | collective-permute-start | bytes 589832 | tf_op jit(solution)/shard_map/ppermute | solution.py:30
  146.3 2.4 %collective-permute-start.24 = (bf16[128,3072]{1,0:T(8,128)(2,1)S(1)}, bf16[128,3072]{1,0:T(8,128)(2,1)S(1)}, u32[]{:S(2)}, u32[]{:S(2)}) collective-permute-start(bf16[128,3072]{1,0:T(8,128)(2,1)S(1)} %shard_map.124.refs_0_.refs_5_), channel_id=1, source_target_pairs={{0,1},{1,0},{2,3},{3,2},{4,5},{5,4},{6,7},{7,6},{8,9},{9,8},{10,11... | collective-permute-start | bytes 2359304 | tf_op jit(solution)/shard_map/ppermute | solution.py:23
  148.6 22.7 %copy-start.1 = (bf16[64,16384]{1,0:T(8,128)(2,1)S(1)}, bf16[64,16384]{1,0:T(8,128)(2,1)}, u32[]{:S(2)}) copy-start(bf16[64,16384]{1,0:T(8,128)(2,1)} %param.12) | copy-start | bytes 6291460
  154.9 9.2 %collective-permute-start.25 = (bf16[64,2048]{1,0:T(8,128)(2,1)S(1)}, bf16[64,2048]{1,0:T(8,128)(2,1)S(1)}, u32[]{:S(2)}, u32[]{:S(2)}) collective-permute-start(bf16[64,2048]{1,0:T(8,128)(2,1)S(1)} %get-tuple-element.26), channel_id=1, source_target_pairs={{0,8},{8,0},{16,24},{24,16},{1,9},{9,1},{17,25},{25,17},{2,10},{10... | collective-permute-start | bytes 786440 | tf_op jit(solution)/shard_map/ppermute | solution.py:23
  156.5 13.7 %collective-permute-start.26 = (bf16[64,2048]{1,0:T(8,128)(2,1)S(1)}, bf16[64,2048]{1,0:T(8,128)(2,1)S(1)}, u32[]{:S(2)}, u32[]{:S(2)}) collective-permute-start(bf16[64,2048]{1,0:T(8,128)(2,1)S(1)} %get-tuple-element.27), channel_id=1, source_target_pairs={{0,16},{8,24},{16,0},{24,8},{1,17},{9,25},{17,1},{25,9},{2,18},{10... | collective-permute-start | bytes 786440 | tf_op jit(solution)/shard_map/ppermute | solution.py:23
  157.2 13.0 %collective-permute-start.27 = (bf16[64,2048]{1,0:T(8,128)(2,1)S(1)}, bf16[64,2048]{1,0:T(8,128)(2,1)S(1)}, u32[]{:S(2)}, u32[]{:S(2)}) collective-permute-start(bf16[64,2048]{1,0:T(8,128)(2,1)S(1)} %get-tuple-element.28), channel_id=1, source_target_pairs={{0,24},{8,16},{16,8},{24,0},{1,25},{9,17},{17,9},{25,1},{2,26},{10... | collective-permute-start | bytes 786440 | tf_op jit(solution)/shard_map/ppermute | solution.py:23

commit v4 on v3

--- a/solution.py
+++ b/solution.py
@@ -464,10 +464,10 @@
     def turn_of(k, stage):
         return k + stage - (k == 0 and stage > 0)
 
-    flowing = [0, 2 * chips, chips, None, *range(chips - 1, 0, -1), 2 * chips - 1]
-    closing = [2 * chips, 2 * chips - 1, None]
+    flowing = [0, 2 * chips, *range(1, chips + 1), None, 2 * chips - 1]
+    closing = [None, 2 * chips, 2 * chips - 1]
     for turn in range(n_chunks + 2 * chips):
-        if turn == n_chunks:
+        if turn == n_chunks + 1:
             shape = (READY_DOWN, 2 * unit, down_weight.shape[1])
             ready = bring((down_weight,), shape, 0, True, last)
             last = [ready]
@@ -476,7 +476,10 @@
                 for k in range(n_chunks):
                     for j in range(1, chips - 1):
                         if turn_of(k, chips + j) == turn:
-                            last = last + [chunks[k]["hidden"][j]]
+                            hidden = hold(chunks[k]["hidden"][j], last)
+                            last = [hidden]
+                            chunks[k]["hidden"][j] = hidden
+                            chunks[k]["hidden"].append(along_ring(hidden))
                 if turn == 1:
                     last = last + squares
                 continue
@@ -508,9 +511,7 @@
                         place, chunk["flow"], chunk["own"], chunk["other"], squares, last
                     )
                     last = [hidden]
-                    chunk["hidden"] = [hidden]
-                    for _ in range(1, chips):
-                        chunk["hidden"].append(along_ring(chunk["hidden"][-1]))
+                    chunk["hidden"] = [hidden, along_ring(hidden)]
                 elif stage == 2 * chips - 1:
                     ours = join(chunk["hidden"][1:] + chunk["hidden"][:1], last)
                     last = [ours]

time: 172 us -> 165 us (0.959)
  starting transfers between devices: 36 us -> 31.6 us
  waiting for transfers between devices: 85 us -> 82.4 us
    ppermute x12, waiting for transfers between devices: 66.8 us -> 62.3 us  [along_ring(): lax.ppermute(x, 'blk', [(2 * a + c, 2 * b + c) for a, b in hops for c in...]
    ppermute x12, starting transfers between devices: 19.1 us -> 14.6 us  [along_ring(): lax.ppermute(x, 'blk', [(2 * a + c, 2 * b + c) for a, b in hops for c in...]
    ppermute x16, waiting for transfers between devices: 18.2 us -> 20 us  [partner(): lax.ppermute(x, axis, [(i, i ^ distance) for i in range(lax.axis_size(axi...]
  transfers between devices with their start and end apart: 28 -> 28, of which waited for: 18 -> 19; matrix products, arithmetic and copies ran while one was open for 0% -> 0% of each run, Pallas kernels for 14% -> 15%
where the time goes in v4:
time: 165 us; the launch traced here: 164 us
  waiting for transfers between devices  82.4 us (50%)
  Pallas kernels  43 us (26%)
  starting transfers between devices  31.6 us (19%)
  other arithmetic  4.32 us (3%)
  matrix products  1.67 us (1%)
    ppermute x12, waiting for transfers between devices, along_ring(): lax.ppermute(x, 'blk', [(2 * a + c, 2 * b + c) for a, b in hops for c in...  62.3 us
    pallas_call x2, Pallas kernels, gate_up(): pl.pallas_call(functools.partial(gate_up_kernel, len(blocks), len(rides),...  23.2 us
    ppermute x16, waiting for transfers between devices, partner(): lax.ppermute(x, axis, [(i, i ^ distance) for i in range(lax.axis_size(axi...  20 us
    ppermute x16, starting transfers between devices, partner(): lax.ppermute(x, axis, [(i, i ^ distance) for i in range(lax.axis_size(axi...  17 us
    ppermute x12, starting transfers between devices, along_ring(): lax.ppermute(x, 'blk', [(2 * a + c, 2 * b + c) for a, b in hops for c in...  14.6 us
    pallas_call x2, Pallas kernels, down(): pl.pallas_call(functools.partial(down_kernel, has_total, len(outs), start...  13.2 us
    pallas_call x2, Pallas kernels, bring(): pl.pallas_call(functools.partial(bring_kernel, len(weights), first_unit,...  3.85 us
  transfers between devices with their start and end apart: 28, of which 19 were waited for; matrix products, arithmetic and copies ran while one was open for 0% of the time, Pallas kernels for 15%

profile of v4, /device:TPU:0, one launch (start us, length us, event | category | flops | bytes accessed | tf_op | source)
XLA Modules:
  0.0 164.2 jit_solution(4111787843526478245)
XLA Ops:
  0.0 0.9 iota_compare_fusion
  0.9 0.8 convert_element_type.27
  1.7 0.7 dynamic-slice_bitcast_fusion.1
  2.4 0.7 dynamic-slice_convert_fusion
  3.2 0.2 fusion.7
  3.4 0.7 select_reduce_fusion
  4.2 0.4 fusion.3
  4.6 0.7 fusion
  5.3 0.3 multiply_reduce_fusion
  5.6 4.0 %collective-permute-start.2 = (bf16[64,2048]{1,0:T(8,128)(2,1)S(1)}, bf16[64,2048]{1,0:T(8,128)(2,1)S(1)}, u32[]{:S(2)}, u32[]{:S(2)}) collective-permute-start(bf16[64,2048]{1,0:T(8,128)(2,1)S(1)} %get-tuple-element.32.refs_2_.refs_0_), channel_id=1, source_target_pairs={{0,24},{8,16},{16,8},{24,0},{1,25},{9,17},{17,9},{25,1},{2,26},{10... | collective-permute-start | bytes 786440 | tf_op jit(solution)/shard_map/ppermute | solution.py:23
  9.5 0.5 collective-permute-start.1
  10.1 0.1 collective-permute-start
  10.4 1.1 collective-permute-done.3
  11.5 2.0 %collective-permute-start.4 = (f32[64,1]{1,0:T(8,128)S(1)}, f32[64,1]{1,0:T(8,128)S(1)}, u32[]{:S(2)}, u32[]{:S(2)}) collective-permute-start(f32[64,1]{1,0:T(8,128)S(1)} %add.85), channel_id=1, source_target_pairs={{0,2},{1,3},{2,0},{3,1},{4,6},{5,7},{6,4},{7,5},{8,10},{9,11},{10,... | collective-permute-start | bytes 776 | tf_op jit(solution)/shard_map/ppermute | solution.py:23
  13.5 1.9 %collective-permute-done.4 = f32[64,1]{1,0:T(8,128)S(1)} collective-permute-done((f32[64,1]{1,0:T(8,128)S(1)}, f32[64,1]{1,0:T(8,128)S(1)}, u32[]{:S(2)}, u32[]{:S(2)}) %collective-permute-start.4) | collective-permute-done | bytes 288 | tf_op jit(solution)/shard_map/ppermute | solution.py:23
  15.4 3.0 %collective-permute-start.5 = (f32[64,1]{1,0:T(8,128)S(1)}, f32[64,1]{1,0:T(8,128)S(1)}, u32[]{:S(2)}, u32[]{:S(2)}) collective-permute-start(f32[64,1]{1,0:T(8,128)S(1)} %add.86), channel_id=1, source_target_pairs={{0,4},{1,5},{2,6},{3,7},{4,0},{5,1},{6,2},{7,3},{8,12},{9,13},{10,... | collective-permute-start | bytes 776 | tf_op jit(solution)/shard_map/ppermute | solution.py:23
  18.5 2.3 %shard_map.109.refs_6_.refs_8_ = bf16[2,2048,512]{2,1,0:T(8,128)(2,1)S(1)} custom-call(bf16[2048,6656]{1,0:T(8,128)(2,1)} %refs_4_.3, bf16[2048,6656]{1,0:T(8,128)(2,1)} %refs_5_.3, bf16[64,2048]{1,0:T(8,128)(2,1)S(1)} %get-tuple-element.32.refs_2_.refs_0_), custom_call_target="tpu_custom_call" | custom-call | bytes 8388608 | tf_op jit(solution)/shard_map/pallas_call | solution.py:99
  20.8 0.7 collective-permute-done.1.refs_2_
  21.5 0.3 collective-permute-done.refs_1_
  21.8 12.4 %shard_map.110 = (bf16[2,128,3584]{2,1,0:T(8,128)(2,1)S(1)}, bf16[2,128,3584]{2,1,0:T(8,128)(2,1)S(1)}, f32[64,1]{1,0:T(8,128)S(1)}, bf16[2,2048,512]{2,1,0:T(8,128)(2,1)S(1)}) custom-call(s32[9]{0:T(128)S(1)} %pad_add_fusion.place_ref, bf16[64,2048]{1,0:T(8,128)(2,1)S(1)} %get-tuple-element.32.refs_2_.refs_0_, ...), custom_call_target="tpu_custom_call" | custom-call | flops 7516192768 | bytes 34078720 | tf_op jit(solution)/shard_map/pallas_call | solution.py:164
  34.3 1.6 collective-permute-start.10
  35.9 1.4 collective-permute-start.9
  37.3 0.5 collective-permute-start.8
  37.8 0.2 collective-permute-done.6.other_ref
  38.2 1.6 collective-permute-start.7
  39.8 10.8 %shard_map.112 = (bf16[2,128,3072]{2,1,0:T(8,128)(2,1)S(1)}, bf16[2,128,3072]{2,1,0:T(8,128)(2,1)S(1)}) custom-call(s32[9]{0:T(128)S(1)} %pad_add_fusion.place_ref, bf16[64,2048]{1,0:T(8,128)(2,1)S(1)} %get-tuple-element.32.refs_2_.refs_0_, bf16[64,2048]{1,0:T(8,128)(2,1)S(1)} %collective-permute-done.refs_1_, ...), custom_call_target="tpu_custom_call" | custom-call | flops 6442450944 | bytes 29360128 | tf_op jit(solution)/shard_map/pallas_call | solution.py:164
  50.5 1.1 collective-permute-done.7.refs_0_
  51.7 0.2 shard_map.113.refs_1_
  52.0 1.5 collective-permute-start.13
  53.5 1.9 %collective-permute-done.11.other_ref = bf16[2,128,3072]{2,1,0:T(8,128)(2,1)S(1)} collective-permute-done((bf16[2,128,3072]{2,1,0:T(8,128)(2,1)S(1)}, bf16[2,128,3072]{2,1,0:T(8,128)(2,1)S(1)}, u32[]{:S(2)}, u32[]{:S(2)}) %collective-permute-start.11) | collective-permute-done | bytes 1572896 | tf_op jit(solution)/shard_map/ppermute | solution.py:23
  55.4 1.5 collective-permute-start.12
  57.0 9.2 %collective-permute-done.13.refs_0_ = bf16[2,32,3584]{2,1,0:T(8,128)(2,1)S(1)} collective-permute-done((bf16[2,32,3584]{2,1,0:T(8,128)(2,1)S(1)}, bf16[2,32,3584]{2,1,0:T(8,128)(2,1)S(1)}, u32[]{:S(2)}, u32[]{:S(2)}) %collective-permute-start.13) | collective-permute-done | bytes 458784 | tf_op jit(solution)/shard_map/ppermute | solution.py:30
  66.2 0.2 shard_map.116.refs_1_
  66.4 0.8 collective-permute-start.15
  67.2 1.6 shard_map.117.refs_1_.refs_3_
  68.8 5.8 %collective-permute-done.12.refs_0_ = bf16[2,32,3072]{2,1,0:T(8,128)(2,1)S(1)} collective-permute-done((bf16[2,32,3072]{2,1,0:T(8,128)(2,1)S(1)}, bf16[2,32,3072]{2,1,0:T(8,128)(2,1)S(1)}, u32[]{:S(2)}, u32[]{:S(2)}) %collective-permute-start.12) | collective-permute-done | bytes 393248 | tf_op jit(solution)/shard_map/ppermute | solution.py:30
  74.7 0.1 shard_map.118.refs_4_
  74.8 0.8 collective-permute-start.14
  75.6 8.9 %collective-permute-done.15.flow_ref = bf16[2,32,3584]{2,1,0:T(8,128)(2,1)S(1)} collective-permute-done((bf16[2,32,3584]{2,1,0:T(8,128)(2,1)S(1)}, bf16[2,32,3584]{2,1,0:T(8,128)(2,1)S(1)}, u32[]{:S(2)}, u32[]{:S(2)}) %collective-permute-start.15) | collective-permute-done | bytes 458784 | tf_op jit(solution)/shard_map/ppermute | solution.py:30
  84.5 1.0 shard_map.119.refs_1_.refs_3_
  85.4 0.8 collective-permute-start.17
  86.3 6.6 %collective-permute-done.14.refs_0_ = bf16[2,32,3072]{2,1,0:T(8,128)(2,1)S(1)} collective-permute-done((bf16[2,32,3072]{2,1,0:T(8,128)(2,1)S(1)}, bf16[2,32,3072]{2,1,0:T(8,128)(2,1)S(1)}, u32[]{:S(2)}, u32[]{:S(2)}) %collective-permute-start.14) | collective-permute-done | bytes 393248 | tf_op jit(solution)/shard_map/ppermute | solution.py:30
  92.9 0.1 shard_map.120.refs_1_
  93.1 0.8 collective-permute-start.16
  93.9 3.9 %collective-permute-done.17.refs_0_ = bf16[32,3584]{1,0:T(8,128)(2,1)S(1)} collective-permute-done((bf16[32,3584]{1,0:T(8,128)(2,1)S(1)}, bf16[32,3584]{1,0:T(8,128)(2,1)S(1)}, u32[]{:S(2)}, u32[]{:S(2)}) %collective-permute-start.17) | collective-permute-done | bytes 229408 | tf_op jit(solution)/shard_map/ppermute | solution.py:30
  97.8 0.8 collective-permute-start.19
  98.6 7.6 %collective-permute-done.16.flow_ref = bf16[2,32,3072]{2,1,0:T(8,128)(2,1)S(1)} collective-permute-done((bf16[2,32,3072]{2,1,0:T(8,128)(2,1)S(1)}, bf16[2,32,3072]{2,1,0:T(8,128)(2,1)S(1)}, u32[]{:S(2)}, u32[]{:S(2)}) %collective-permute-start.16) | collective-permute-done | bytes 393248 | tf_op jit(solution)/shard_map/ppermute | solution.py:30
  106.3 0.9 shard_map.122.refs_1_.refs_3_
  107.1 3.6 %collective-permute-done.19.refs_0_ = bf16[32,3584]{1,0:T(8,128)(2,1)S(1)} collective-permute-done((bf16[32,3584]{1,0:T(8,128)(2,1)S(1)}, bf16[32,3584]{1,0:T(8,128)(2,1)S(1)}, u32[]{:S(2)}, u32[]{:S(2)}) %collective-permute-start.19) | collective-permute-done | bytes 229408 | tf_op jit(solution)/shard_map/ppermute | solution.py:30
  110.7 0.8 collective-permute-start.21
  111.5 3.4 %collective-permute-start.18 = (bf16[32,3072]{1,0:T(8,128)(2,1)S(1)}, bf16[32,3072]{1,0:T(8,128)(2,1)S(1)}, u32[]{:S(2)}, u32[]{:S(2)}) collective-permute-start(bf16[32,3072]{1,0:T(8,128)(2,1)S(1)} %shard_map.122.refs_1_.refs_3_), channel_id=1, source_target_pairs={{0,2},{1,3},{2,6},{3,7},{6,4},{7,5},{4,0},{5,1},{8,10},{9,11},{10,... | collective-permute-start | bytes 589832 | tf_op jit(solution)/shard_map/ppermute | solution.py:30
  114.9 8.1 %collective-permute-done.18.refs_0_ = bf16[32,3072]{1,0:T(8,128)(2,1)S(1)} collective-permute-done((bf16[32,3072]{1,0:T(8,128)(2,1)S(1)}, bf16[32,3072]{1,0:T(8,128)(2,1)S(1)}, u32[]{:S(2)}, u32[]{:S(2)}) %collective-permute-start.18) | collective-permute-done | bytes 196640 | tf_op jit(solution)/shard_map/ppermute | solution.py:30
  123.2 0.8 collective-permute-start.20
  124.0 7.4 %collective-permute-done.20.refs_0_ = bf16[32,3072]{1,0:T(8,128)(2,1)S(1)} collective-permute-done((bf16[32,3072]{1,0:T(8,128)(2,1)S(1)}, bf16[32,3072]{1,0:T(8,128)(2,1)S(1)}, u32[]{:S(2)}, u32[]{:S(2)}) %collective-permute-start.20) | collective-permute-done | bytes 196640 | tf_op jit(solution)/shard_map/ppermute | solution.py:30
  131.4 0.8 collective-permute-start.22
  132.1 6.9 %shard_map.127 = (f32[256,2048]{1,0:T(8,128)S(1)}, bf16[1,512,2048]{2,1,0:T(8,128)(2,1)S(1)}) custom-call(s32[9]{0:T(128)S(1)} %pad_add_fusion.place_ref, bf16[128,3584]{1,0:T(8,128)(2,1)S(1)} %shard_map.125.refs_1_.refs_0_, bf16[128,3584]{1,0:T(8,128)(2,1)S(1)} %collective-permute-done.23.refs_1_, bf16[6656,2048]{1,0:T(8,128)(2,1)} %refs_2_.3, ...), custom_call_target="tpu_custom_call" | custom-call | flops 3758096384 | bytes 18874368 | tf_op jit(solution)/shard_map/pallas_call | solution.py:338
  139.2 2.3 %collective-permute-done.24.refs_1_ = bf16[128,3072]{1,0:T(8,128)(2,1)S(1)} collective-permute-done((bf16[128,3072]{1,0:T(8,128)(2,1)S(1)}, bf16[128,3072]{1,0:T(8,128)(2,1)S(1)}, u32[]{:S(2)}, u32[]{:S(2)}) %collective-permute-start.24) | collective-permute-done | bytes 786464 | tf_op jit(solution)/shard_map/ppermute | solution.py:23
  141.5 6.3 %shard_map.129 = (f32[64,2048]{1,0:T(8,128)S(1)}, bf16[64,2048]{1,0:T(8,128)(2,1)S(1)}, bf16[64,2048]{1,0:T(8,128)(2,1)S(1)}, bf16[64,2048]{1,0:T(8,128)(2,1)S(1)}) custom-call(s32[9]{0:T(128)S(1)} %pad_add_fusion.place_ref, bf16[128,3072]{1,0:T(8,128)(2,1)S(1)} %shard_map.128.refs_0_.refs_5_, bf16[128,3072]{1,0:T(8,128)(2,1)S(1)} %collective-permute-done.24.refs_1_, ...), custom_call_target="tpu_custom_call" | custom-call | flops 3221225472 | bytes 16777216 | tf_op jit(solution)/shard_map/pallas_call | solution.py:338
  147.8 1.6 collective-permute-start.25
  149.4 0.7 collective-permute-start.26
  150.1 1.3 collective-permute-start.27
  151.4 5.7 %collective-permute-done.25 = bf16[64,2048]{1,0:T(8,128)(2,1)S(1)} collective-permute-done((bf16[64,2048]{1,0:T(8,128)(2,1)S(1)}, bf16[64,2048]{1,0:T(8,128)(2,1)S(1)}, u32[]{:S(2)}, u32[]{:S(2)}) %collective-permute-start.25) | collective-permute-done | bytes 262176 | tf_op jit(solution)/shard_map/ppermute | solution.py:23
  157.0 6.0 %collective-permute-done.26 = bf16[64,2048]{1,0:T(8,128)(2,1)S(1)} collective-permute-done((bf16[64,2048]{1,0:T(8,128)(2,1)S(1)}, bf16[64,2048]{1,0:T(8,128)(2,1)S(1)}, u32[]{:S(2)}, u32[]{:S(2)}) %collective-permute-start.26) | collective-permute-done | bytes 262176 | tf_op jit(solution)/shard_map/ppermute | solution.py:23
  163.0 1.2 convert_add_fusion
  (43 shorter events, 1.0 us)
Async XLA Ops:
  0.0 3.1 %copy-start = (bf16[64,16384]{1,0:T(8,128)(2,1)S(1)}, bf16[64,16384]{1,0:T(8,128)(2,1)}, u32[]{:S(2)}) copy-start(bf16[64,16384]{1,0:T(8,128)(2,1)} %param.12) | copy-start | bytes 6291460
  0.0 3.4 %copy-start.2 = (bf16[64,1,64,128]{3,2,1,0:T(8,128)(2,1)S(1)}, bf16[64,1,64,128]{3,2,1,0:T(8,128)(2,1)}, u32[]{:S(2)}) copy-start(bf16[64,1,64,128]{3,2,1,0:T(8,128)(2,1)} %param.13) | copy-start | bytes 3145732
  3.1 1.5 copy-start.4
  4.2 1.1 copy-start.3
  5.6 15.2 %collective-permute-start.2 = (bf16[64,2048]{1,0:T(8,128)(2,1)S(1)}, bf16[64,2048]{1,0:T(8,128)(2,1)S(1)}, u32[]{:S(2)}, u32[]{:S(2)}) collective-permute-start(bf16[64,2048]{1,0:T(8,128)(2,1)S(1)} %get-tuple-element.32.refs_2_.refs_0_), channel_id=1, source_target_pairs={{0,24},{8,16},{16,8},{24,0},{1,25},{9,17},{17,9},{25,1},{2,26},{10... | collective-permute-start | bytes 786440 | tf_op jit(solution)/shard_map/ppermute | solution.py:23
  9.5 11.9 %collective-permute-start.1 = (bf16[64,2048]{1,0:T(8,128)(2,1)S(1)}, bf16[64,2048]{1,0:T(8,128)(2,1)S(1)}, u32[]{:S(2)}, u32[]{:S(2)}) collective-permute-start(bf16[64,2048]{1,0:T(8,128)(2,1)S(1)} %get-tuple-element.32.refs_2_.refs_0_), channel_id=1, source_target_pairs={{0,16},{8,24},{16,0},{24,8},{1,17},{9,25},{17,1},{25,9},{2,18},{10... | collective-permute-start | bytes 786440 | tf_op jit(solution)/shard_map/ppermute | solution.py:23
  10.1 11.7 %collective-permute-start = (bf16[64,2048]{1,0:T(8,128)(2,1)S(1)}, bf16[64,2048]{1,0:T(8,128)(2,1)S(1)}, u32[]{:S(2)}, u32[]{:S(2)}) collective-permute-start(bf16[64,2048]{1,0:T(8,128)(2,1)S(1)} %get-tuple-element.32.refs_2_.refs_0_), channel_id=1, source_target_pairs={{0,8},{8,0},{16,24},{24,16},{1,9},{9,1},{17,25},{25,17},{2,10},{10... | collective-permute-start | bytes 786440 | tf_op jit(solution)/shard_map/ppermute | solution.py:23
  10.3 1.2 collective-permute-start.3
  11.5 3.9 %collective-permute-start.4 = (f32[64,1]{1,0:T(8,128)S(1)}, f32[64,1]{1,0:T(8,128)S(1)}, u32[]{:S(2)}, u32[]{:S(2)}) collective-permute-start(f32[64,1]{1,0:T(8,128)S(1)} %add.85), channel_id=1, source_target_pairs={{0,2},{1,3},{2,0},{3,1},{4,6},{5,7},{6,4},{7,5},{8,10},{9,11},{10,... | collective-permute-start | bytes 776 | tf_op jit(solution)/shard_map/ppermute | solution.py:23
  15.4 5.3 %collective-permute-start.5 = (f32[64,1]{1,0:T(8,128)S(1)}, f32[64,1]{1,0:T(8,128)S(1)}, u32[]{:S(2)}, u32[]{:S(2)}) collective-permute-start(f32[64,1]{1,0:T(8,128)S(1)} %add.86), channel_id=1, source_target_pairs={{0,4},{1,5},{2,6},{3,7},{4,0},{5,1},{6,2},{7,3},{8,12},{9,13},{10,... | collective-permute-start | bytes 776 | tf_op jit(solution)/shard_map/ppermute | solution.py:23
  34.2 3.9 %collective-permute-start.6 = (bf16[2,128,3584]{2,1,0:T(8,128)(2,1)S(1)}, bf16[2,128,3584]{2,1,0:T(8,128)(2,1)S(1)}, u32[]{:S(2)}, u32[]{:S(2)}) collective-permute-start(bf16[2,128,3584]{2,1,0:T(8,128)(2,1)S(1)} %get-tuple-element.19), channel_id=1, source_target_pairs={{0,1},{1,0},{2,3},{3,2},{4,5},{5,4},{6,7},{7,6},{8,9},{9,8},{10,11... | collective-permute-start | bytes 5505032 | tf_op jit(solution)/shard_map/ppermute | solution.py:23
  34.3 17.6 %collective-permute-start.10 = (f32[64,1]{1,0:T(8,128)S(1)}, f32[64,1]{1,0:T(8,128)S(1)}, u32[]{:S(2)}, u32[]{:S(2)}) collective-permute-start(f32[64,1]{1,0:T(8,128)S(1)} %get-tuple-element.22.refs_2_.refs_0_), channel_id=1, source_target_pairs={{0,24},{8,16},{16,8},{24,0},{1,25},{9,17},{17,9},{25,1},{2,26},{10... | collective-permute-start | bytes 776 | tf_op jit(solution)/shard_map/ppermute | solution.py:23
  35.9 16.0 %collective-permute-start.9 = (f32[64,1]{1,0:T(8,128)S(1)}, f32[64,1]{1,0:T(8,128)S(1)}, u32[]{:S(2)}, u32[]{:S(2)}) collective-permute-start(f32[64,1]{1,0:T(8,128)S(1)} %get-tuple-element.22.refs_2_.refs_0_), channel_id=1, source_target_pairs={{0,16},{8,24},{16,0},{24,8},{1,17},{9,25},{17,1},{25,9},{2,18},{10... | collective-permute-start | bytes 776 | tf_op jit(solution)/shard_map/ppermute | solution.py:23
  37.3 14.6 %collective-permute-start.8 = (f32[64,1]{1,0:T(8,128)S(1)}, f32[64,1]{1,0:T(8,128)S(1)}, u32[]{:S(2)}, u32[]{:S(2)}) collective-permute-start(f32[64,1]{1,0:T(8,128)S(1)} %get-tuple-element.22.refs_2_.refs_0_), channel_id=1, source_target_pairs={{0,8},{8,0},{16,24},{24,16},{1,9},{9,1},{17,25},{25,17},{2,10},{10... | collective-permute-start | bytes 776 | tf_op jit(solution)/shard_map/ppermute | solution.py:23
  38.2 13.5 %collective-permute-start.7 = (bf16[2,32,3584]{2,1,0:T(8,128)(2,1)S(1)}, bf16[2,32,3584]{2,1,0:T(8,128)(2,1)S(1)}, u32[]{:S(2)}, u32[]{:S(2)}) collective-permute-start(bf16[2,32,3584]{2,1,0:T(8,128)(2,1)S(1)} %shard_map.111.refs_7_), channel_id=1, source_target_pairs={{0,2},{1,3},{2,6},{3,7},{6,4},{7,5},{4,0},{5,1},{8,10},{9,11},{10,... | collective-permute-start | bytes 1376264 | tf_op jit(solution)/shard_map/ppermute | solution.py:30
  51.9 3.5 %collective-permute-start.11 = (bf16[2,128,3072]{2,1,0:T(8,128)(2,1)S(1)}, bf16[2,128,3072]{2,1,0:T(8,128)(2,1)S(1)}, u32[]{:S(2)}, u32[]{:S(2)}) collective-permute-start(bf16[2,128,3072]{2,1,0:T(8,128)(2,1)S(1)} %shard_map.114.refs_0_), channel_id=1, source_target_pairs={{0,1},{1,0},{2,3},{3,2},{4,5},{5,4},{6,7},{7,6},{8,9},{9,8},{10,11... | collective-permute-start | bytes 4718600 | tf_op jit(solution)/shard_map/ppermute | solution.py:23
  52.0 14.3 %collective-permute-start.13 = (bf16[2,32,3584]{2,1,0:T(8,128)(2,1)S(1)}, bf16[2,32,3584]{2,1,0:T(8,128)(2,1)S(1)}, u32[]{:S(2)}, u32[]{:S(2)}) collective-permute-start(bf16[2,32,3584]{2,1,0:T(8,128)(2,1)S(1)} %shard_map.113.refs_1_), channel_id=1, source_target_pairs={{0,2},{1,3},{2,6},{3,7},{6,4},{7,5},{4,0},{5,1},{8,10},{9,11},{10,... | collective-permute-start | bytes 1376264 | tf_op jit(solution)/shard_map/ppermute | solution.py:30
  55.4 19.2 %collective-permute-start.12 = (bf16[2,32,3072]{2,1,0:T(8,128)(2,1)S(1)}, bf16[2,32,3072]{2,1,0:T(8,128)(2,1)S(1)}, u32[]{:S(2)}, u32[]{:S(2)}) collective-permute-start(bf16[2,32,3072]{2,1,0:T(8,128)(2,1)S(1)} %shard_map.115.refs_1_), channel_id=1, source_target_pairs={{0,2},{1,3},{2,6},{3,7},{6,4},{7,5},{4,0},{5,1},{8,10},{9,11},{10,... | collective-permute-start | bytes 1179656 | tf_op jit(solution)/shard_map/ppermute | solution.py:30
  66.4 18.1 %collective-permute-start.15 = (bf16[2,32,3584]{2,1,0:T(8,128)(2,1)S(1)}, bf16[2,32,3584]{2,1,0:T(8,128)(2,1)S(1)}, u32[]{:S(2)}, u32[]{:S(2)}) collective-permute-start(bf16[2,32,3584]{2,1,0:T(8,128)(2,1)S(1)} %shard_map.116.refs_1_), channel_id=1, source_target_pairs={{0,2},{1,3},{2,6},{3,7},{6,4},{7,5},{4,0},{5,1},{8,10},{9,11},{10,... | collective-permute-start | bytes 1376264 | tf_op jit(solution)/shard_map/ppermute | solution.py:30
  74.8 18.1 %collective-permute-start.14 = (bf16[2,32,3072]{2,1,0:T(8,128)(2,1)S(1)}, bf16[2,32,3072]{2,1,0:T(8,128)(2,1)S(1)}, u32[]{:S(2)}, u32[]{:S(2)}) collective-permute-start(bf16[2,32,3072]{2,1,0:T(8,128)(2,1)S(1)} %shard_map.118.refs_4_), channel_id=1, source_target_pairs={{0,2},{1,3},{2,6},{3,7},{6,4},{7,5},{4,0},{5,1},{8,10},{9,11},{10,... | collective-permute-start | bytes 1179656 | tf_op jit(solution)/shard_map/ppermute | solution.py:30
  85.4 12.4 %collective-permute-start.17 = (bf16[32,3584]{1,0:T(8,128)(2,1)S(1)}, bf16[32,3584]{1,0:T(8,128)(2,1)S(1)}, u32[]{:S(2)}, u32[]{:S(2)}) collective-permute-start(bf16[32,3584]{1,0:T(8,128)(2,1)S(1)} %shard_map.119.refs_1_.refs_3_), channel_id=1, source_target_pairs={{0,2},{1,3},{2,6},{3,7},{6,4},{7,5},{4,0},{5,1},{8,10},{9,11},{10,... | collective-permute-start | bytes 688136 | tf_op jit(solution)/shard_map/ppermute | solution.py:30
  93.1 13.2 %collective-permute-start.16 = (bf16[2,32,3072]{2,1,0:T(8,128)(2,1)S(1)}, bf16[2,32,3072]{2,1,0:T(8,128)(2,1)S(1)}, u32[]{:S(2)}, u32[]{:S(2)}) collective-permute-start(bf16[2,32,3072]{2,1,0:T(8,128)(2,1)S(1)} %shard_map.120.refs_1_), channel_id=1, source_target_pairs={{0,2},{1,3},{2,6},{3,7},{6,4},{7,5},{4,0},{5,1},{8,10},{9,11},{10,... | collective-permute-start | bytes 1179656 | tf_op jit(solution)/shard_map/ppermute | solution.py:30
  97.8 12.9 %collective-permute-start.19 = (bf16[32,3584]{1,0:T(8,128)(2,1)S(1)}, bf16[32,3584]{1,0:T(8,128)(2,1)S(1)}, u32[]{:S(2)}, u32[]{:S(2)}) collective-permute-start(bf16[32,3584]{1,0:T(8,128)(2,1)S(1)} %shard_map.121.refs_4_.refs_0_), channel_id=1, source_target_pairs={{0,2},{1,3},{2,6},{3,7},{6,4},{7,5},{4,0},{5,1},{8,10},{9,11},{10,... | collective-permute-start | bytes 688136 | tf_op jit(solution)/shard_map/ppermute | solution.py:30
  110.7 12.3 %collective-permute-start.21 = (bf16[32,3584]{1,0:T(8,128)(2,1)S(1)}, bf16[32,3584]{1,0:T(8,128)(2,1)S(1)}, u32[]{:S(2)}, u32[]{:S(2)}) collective-permute-start(bf16[32,3584]{1,0:T(8,128)(2,1)S(1)} %shard_map.123.refs_1_), channel_id=1, source_target_pairs={{0,2},{1,3},{2,6},{3,7},{6,4},{7,5},{4,0},{5,1},{8,10},{9,11},{10,... | collective-permute-start | bytes 688136 | tf_op jit(solution)/shard_map/ppermute | solution.py:30
  111.5 11.5 %collective-permute-start.18 = (bf16[32,3072]{1,0:T(8,128)(2,1)S(1)}, bf16[32,3072]{1,0:T(8,128)(2,1)S(1)}, u32[]{:S(2)}, u32[]{:S(2)}) collective-permute-start(bf16[32,3072]{1,0:T(8,128)(2,1)S(1)} %shard_map.122.refs_1_.refs_3_), channel_id=1, source_target_pairs={{0,2},{1,3},{2,6},{3,7},{6,4},{7,5},{4,0},{5,1},{8,10},{9,11},{10,... | collective-permute-start | bytes 589832 | tf_op jit(solution)/shard_map/ppermute | solution.py:30
  123.1 9.1 %collective-permute-start.23 = (bf16[128,3584]{1,0:T(8,128)(2,1)S(1)}, bf16[128,3584]{1,0:T(8,128)(2,1)S(1)}, u32[]{:S(2)}, u32[]{:S(2)}) collective-permute-start(bf16[128,3584]{1,0:T(8,128)(2,1)S(1)} %shard_map.125.refs_1_.refs_0_), channel_id=1, source_target_pairs={{0,1},{1,0},{2,3},{3,2},{4,5},{5,4},{6,7},{7,6},{8,9},{9,8},{10,11... | collective-permute-start | bytes 2752520 | tf_op jit(solution)/shard_map/ppermute | solution.py:23
  123.2 8.2 %collective-permute-start.20 = (bf16[32,3072]{1,0:T(8,128)(2,1)S(1)}, bf16[32,3072]{1,0:T(8,128)(2,1)S(1)}, u32[]{:S(2)}, u32[]{:S(2)}) collective-permute-start(bf16[32,3072]{1,0:T(8,128)(2,1)S(1)} %shard_map.124.refs_4_.refs_0_), channel_id=1, source_target_pairs={{0,2},{1,3},{2,6},{3,7},{6,4},{7,5},{4,0},{5,1},{8,10},{9,11},{10,... | collective-permute-start | bytes 589832 | tf_op jit(solution)/shard_map/ppermute | solution.py:30
  131.4 7.7 %collective-permute-start.22 = (bf16[32,3072]{1,0:T(8,128)(2,1)S(1)}, bf16[32,3072]{1,0:T(8,128)(2,1)S(1)}, u32[]{:S(2)}, u32[]{:S(2)}) collective-permute-start(bf16[32,3072]{1,0:T(8,128)(2,1)S(1)} %shard_map.126.refs_4_.refs_1_), channel_id=1, source_target_pairs={{0,2},{1,3},{2,6},{3,7},{6,4},{7,5},{4,0},{5,1},{8,10},{9,11},{10,... | collective-permute-start | bytes 589832 | tf_op jit(solution)/shard_map/ppermute | solution.py:30
  139.1 2.4 %collective-permute-start.24 = (bf16[128,3072]{1,0:T(8,128)(2,1)S(1)}, bf16[128,3072]{1,0:T(8,128)(2,1)S(1)}, u32[]{:S(2)}, u32[]{:S(2)}) collective-permute-start(bf16[128,3072]{1,0:T(8,128)(2,1)S(1)} %shard_map.128.refs_0_.refs_5_), channel_id=1, source_target_pairs={{0,1},{1,0},{2,3},{3,2},{4,5},{5,4},{6,7},{7,6},{8,9},{9,8},{10,11... | collective-permute-start | bytes 2359304 | tf_op jit(solution)/shard_map/ppermute | solution.py:23
  141.5 22.7 %copy-start.1 = (bf16[64,16384]{1,0:T(8,128)(2,1)S(1)}, bf16[64,16384]{1,0:T(8,128)(2,1)}, u32[]{:S(2)}) copy-start(bf16[64,16384]{1,0:T(8,128)(2,1)} %param.12) | copy-start | bytes 6291460
  147.8 9.2 %collective-permute-start.25 = (bf16[64,2048]{1,0:T(8,128)(2,1)S(1)}, bf16[64,2048]{1,0:T(8,128)(2,1)S(1)}, u32[]{:S(2)}, u32[]{:S(2)}) collective-permute-start(bf16[64,2048]{1,0:T(8,128)(2,1)S(1)} %get-tuple-element.26), channel_id=1, source_target_pairs={{0,8},{8,0},{16,24},{24,16},{1,9},{9,1},{17,25},{25,17},{2,10},{10... | collective-permute-start | bytes 786440 | tf_op jit(solution)/shard_map/ppermute | solution.py:23
  149.4 13.7 %collective-permute-start.26 = (bf16[64,2048]{1,0:T(8,128)(2,1)S(1)}, bf16[64,2048]{1,0:T(8,128)(2,1)S(1)}, u32[]{:S(2)}, u32[]{:S(2)}) collective-permute-start(bf16[64,2048]{1,0:T(8,128)(2,1)S(1)} %get-tuple-element.27), channel_id=1, source_target_pairs={{0,16},{8,24},{16,0},{24,8},{1,17},{9,25},{17,1},{25,9},{2,18},{10... | collective-permute-start | bytes 786440 | tf_op jit(solution)/shard_map/ppermute | solution.py:23
  150.1 13.0 %collective-permute-start.27 = (bf16[64,2048]{1,0:T(8,128)(2,1)S(1)}, bf16[64,2048]{1,0:T(8,128)(2,1)S(1)}, u32[]{:S(2)}, u32[]{:S(2)}) collective-permute-start(bf16[64,2048]{1,0:T(8,128)(2,1)S(1)} %get-tuple-element.28), channel_id=1, source_target_pairs={{0,24},{8,16},{16,8},{24,0},{1,25},{9,17},{17,9},{25,1},{2,26},{10... | collective-permute-start | bytes 786440 | tf_op jit(solution)/shard_map/ppermute | solution.py:23
